TPU v7x, 32 devices: a whole 2x2x4 slice. The times are simulated.
32 devices in a mesh: dp: 16 (over z, y, x), seq: 2 (over core).
Axes of the slice: x: 2, y: 2, z: 4, core: 2. Of those that a mesh axis runs over, the one named last changes fastest.
Arguments:
- patches: bfloat16 [64, 544, 768], P('dp', 'seq'), may hold values from -6 to 6
- lengths: int32 [64], P('dp'), may hold values from 40 to 529, as said below
- gain_one: float32 [768], replicated, may hold values from 0.5 to 1.5
- shift_one: float32 [768], replicated, may hold values from -2 to 2
- w_query: bfloat16 [768, 768], replicated, may hold values from -0.21875 to 0.21875
- b_query: float32 [768], replicated, may hold values from -2 to 2
- w_key: bfloat16 [768, 768], replicated, may hold values from -0.21875 to 0.21875
- w_value: bfloat16 [768, 768], replicated, may hold values from -0.21875 to 0.21875
- b_value: float32 [768], replicated, may hold values from -2 to 2
- w_out: bfloat16 [768, 768], replicated, may hold values from -1.75 to 1.75
- b_out: float32 [768], replicated, may hold values from -2 to 2
- gain_two: float32 [768], replicated, may hold values from 0.5 to 1.5
- shift_two: float32 [768], replicated, may hold values from -2 to 2
- w_up: bfloat16 [768, 3072], replicated, may hold values from -0.21875 to 0.21875
- b_up: float32 [3072], replicated, may hold values from -2 to 2
- w_down: bfloat16 [3072, 768], replicated, may hold values from -0.109375 to 0.109375
- b_down: float32 [768], replicated, may hold values from -2 to 2
- cotangent: bfloat16 [64, 544, 768], P('dp', 'seq'), may hold values from -6 to 6
Outputs:
- output: bfloat16 [64, 544, 768], P('dp', 'seq')
- grad_patches: bfloat16 [64, 544, 768], P('dp', 'seq')
- grad_gain_one: float32 [768], replicated
- grad_shift_one: float32 [768], replicated
- grad_w_query: float32 [768, 768], replicated
- grad_b_query: float32 [768], replicated
- grad_w_key: float32 [768, 768], replicated
- grad_w_value: float32 [768, 768], replicated
- grad_b_value: float32 [768], replicated
- grad_w_out: float32 [768, 768], replicated
- grad_b_out: float32 [768], replicated
- grad_gain_two: float32 [768], replicated
- grad_shift_two: float32 [768], replicated
- grad_w_up: float32 [768, 3072], replicated
- grad_b_up: float32 [3072], replicated
- grad_w_down: float32 [3072, 768], replicated
- grad_b_down: float32 [768], replicated
Inputs may be any that keep to these rules, and one draw needn't show every extreme that they name: `lengths`: in each aligned block of 4 strips one strip has exactly 529 valid patches; valid patches come first in a strip.
All inputs are finite; a program needn't handle non-finite values.
Results may differ from a plain program's by a relative error of at most 0.012.
Values may be sent and summed in bfloat16 or wider, within the bound.
No kernel may reach another device: no remote copies, remote signals or barrier semaphores. Data moves between devices by JAX's collectives and lax.ppermute only.
A program may use at most 256 MiB of HBM per device.

v0:
```python
import jax
import jax.numpy as jnp
from jax import lax
from jax.sharding import PartitionSpec as P

HEAD_DIM = 64


epsilon = 1e-06


def exact_gelu(values):
    return jax.nn.gelu(values, approximate=False)


def project(left_rows, weight):
    return jnp.dot(left_rows, weight, preferred_element_type=jnp.float32)


def project_back(grad_rows, weight):
    return jnp.einsum("stf,df->std", grad_rows, weight, preferred_element_type=jnp.float32)


def weight_grad(left_rows, grad_rows):
    return jnp.einsum("std,stf->df", left_rows, grad_rows, preferred_element_type=jnp.float32)


def column_sums(grad_rows):
    return jnp.sum(grad_rows.astype(jnp.float32), axis=(0, 1))


def norm_forward(values, gain, shift):
    centre = jnp.mean(values, axis=-1, keepdims=True)
    centred = values - centre
    spread = jnp.mean(centred * centred, axis=-1, keepdims=True)
    rstd_rows = lax.rsqrt(spread + epsilon)
    scaled = centred * rstd_rows
    return ((scaled * gain + shift).astype(jnp.bfloat16), scaled, rstd_rows)


def norm_backward(grad_out, scaled, rstd_rows, gain):
    weighted = grad_out * gain
    mean_grad = jnp.mean(weighted, axis=-1, keepdims=True)
    mean_cross = jnp.mean(weighted * scaled, axis=-1, keepdims=True)
    grad_in = rstd_rows * (weighted - mean_grad - scaled * mean_cross)
    return (grad_in, jnp.sum(grad_out * scaled, axis=(0, 1)), jnp.sum(grad_out, axis=(0, 1)))


def split_heads(block_rows):
    return block_rows.reshape(block_rows.shape[0], block_rows.shape[1] // HEAD_DIM, HEAD_DIM)


def masked_scores(query_heads, key_heads, length):
    score_scale = HEAD_DIM ** (-0.5)
    scores = (
        jnp.einsum("qhd,khd->hqk", query_heads, key_heads, preferred_element_type=jnp.float32)
        * score_scale
    )
    key_valid = lax.iota(jnp.int32, key_heads.shape[0]) < length
    return jnp.where(key_valid[None, None, :], scores, -jnp.inf)


def attend(block_item):
    query_block, key_block, value_block, length = block_item
    value_heads = split_heads(value_block)
    scores = masked_scores(split_heads(query_block), split_heads(key_block), length)
    row_max = jnp.max(scores, axis=-1, keepdims=True)
    exponent = jnp.exp(scores - row_max)
    row_total = jnp.sum(exponent, axis=-1, keepdims=True)
    attn_probs = (exponent / row_total).astype(jnp.bfloat16)
    log_total = (row_max + jnp.log(row_total))[..., 0]
    context_rows = jnp.einsum(
        "hqk,khd->qhd", attn_probs, value_heads, preferred_element_type=jnp.float32
    )
    return (context_rows.reshape(context_rows.shape[0], -1).astype(jnp.bfloat16), log_total)


def attend_back(block_item):
    query_block, key_block, value_block, grad_block, log_total, length = block_item
    score_scale = HEAD_DIM ** (-0.5)
    query_heads = split_heads(query_block)
    key_heads = split_heads(key_block)
    value_heads = split_heads(value_block)
    grad_heads = split_heads(grad_block)
    scores = masked_scores(query_heads, key_heads, length)
    probs_exact = jnp.exp(scores - log_total[:, :, None])
    attn_probs = probs_exact.astype(jnp.bfloat16)
    grad_values = jnp.einsum(
        "hqk,qhd->khd", attn_probs, grad_heads, preferred_element_type=jnp.float32
    )
    grad_probs = jnp.einsum(
        "qhd,khd->hqk", grad_heads, value_heads, preferred_element_type=jnp.float32
    )
    inner = jnp.sum(grad_probs * probs_exact, axis=-1, keepdims=True)
    grad_scores = (probs_exact * (grad_probs - inner)).astype(jnp.bfloat16)
    grad_queries = (
        jnp.einsum("hqk,khd->qhd", grad_scores, key_heads, preferred_element_type=jnp.float32)
        * score_scale
    )
    grad_keys = (
        jnp.einsum("hqk,qhd->khd", grad_scores, query_heads, preferred_element_type=jnp.float32)
        * score_scale
    )
    slots = query_block.shape[0]
    return (
        grad_queries.reshape(slots, -1).astype(jnp.bfloat16),
        grad_keys.reshape(slots, -1).astype(jnp.bfloat16),
        grad_values.reshape(slots, -1).astype(jnp.bfloat16),
    )


def local(
    patches,
    lengths,
    gain_one,
    shift_one,
    w_query,
    b_query,
    w_key,
    w_value,
    b_value,
    w_out,
    b_out,
    gain_two,
    shift_two,
    w_up,
    b_up,
    w_down,
    b_down,
    cotangent,
):
    inputs = patches.astype(jnp.float32)
    normed_one, scaled_one, rstd_one = norm_forward(inputs, gain_one, shift_one)
    queries = (project(normed_one, w_query) + b_query).astype(jnp.bfloat16)
    key_rows = project(normed_one, w_key).astype(jnp.bfloat16)
    value_rows = (project(normed_one, w_value) + b_value).astype(jnp.bfloat16)
    query_whole, key_whole, value_whole = (
        lax.all_to_all(queries, "seq", split_axis=2, concat_axis=1, tiled=True),
        lax.all_to_all(key_rows, "seq", split_axis=2, concat_axis=1, tiled=True),
        lax.all_to_all(value_rows, "seq", split_axis=2, concat_axis=1, tiled=True),
    )
    context_whole, log_totals = lax.map(attend, (query_whole, key_whole, value_whole, lengths))
    context = lax.all_to_all(context_whole, "seq", split_axis=1, concat_axis=2, tiled=True)
    hidden = inputs + project(context, w_out) + b_out
    normed_two, scaled_two, rstd_two = norm_forward(hidden, gain_two, shift_two)
    upper_pre = project(normed_two, w_up) + b_up
    active = exact_gelu(upper_pre).astype(jnp.bfloat16)
    output = (hidden + project(active, w_down) + b_down).astype(jnp.bfloat16)
    grad_y = cotangent.astype(jnp.float32)
    g_down = weight_grad(active, cotangent)
    g_bdown = jnp.sum(grad_y, axis=(0, 1))
    grad_active = project_back(cotangent, w_down)
    unused_value, gelu_pull = jax.vjp(exact_gelu, upper_pre)
    grad_upper = gelu_pull(grad_active)[0].astype(jnp.bfloat16)
    g_up = weight_grad(normed_two, grad_upper)
    g_bup = column_sums(grad_upper)
    grad_normed_two = project_back(grad_upper, w_up)
    grad_from_two, g_gain_two, g_shift_two = norm_backward(
        grad_normed_two, scaled_two, rstd_two, gain_two
    )
    grad_hidden = grad_y + grad_from_two
    grad_attn = grad_hidden.astype(jnp.bfloat16)
    g_out = weight_grad(context, grad_attn)
    g_bout = column_sums(grad_attn)
    grad_context = project_back(grad_attn, w_out).astype(jnp.bfloat16)
    grad_context_whole = lax.all_to_all(
        grad_context, "seq", split_axis=2, concat_axis=1, tiled=True
    )
    grad_q_whole, grad_k_whole, grad_v_whole = lax.map(
        attend_back, (query_whole, key_whole, value_whole, grad_context_whole, log_totals, lengths)
    )
    grad_queries, grad_keys, grad_values = (
        lax.all_to_all(grad_q_whole, "seq", split_axis=1, concat_axis=2, tiled=True),
        lax.all_to_all(grad_k_whole, "seq", split_axis=1, concat_axis=2, tiled=True),
        lax.all_to_all(grad_v_whole, "seq", split_axis=1, concat_axis=2, tiled=True),
    )
    g_query = weight_grad(normed_one, grad_queries)
    g_bquery = column_sums(grad_queries)
    g_key = weight_grad(normed_one, grad_keys)
    g_value = weight_grad(normed_one, grad_values)
    g_bvalue = column_sums(grad_values)
    grad_normed_one = (
        project_back(grad_queries, w_query)
        + project_back(grad_keys, w_key)
        + project_back(grad_values, w_value)
    )
    grad_from_one, g_gain_one, g_shift_one = norm_backward(
        grad_normed_one, scaled_one, rstd_one, gain_one
    )
    grad_patches = (grad_hidden + grad_from_one).astype(jnp.bfloat16)
    (
        g_gain_one,
        g_shift_one,
        g_query,
        g_bquery,
        g_key,
        g_value,
        g_bvalue,
        g_out,
        g_bout,
        g_gain_two,
        g_shift_two,
        g_up,
        g_bup,
        g_down,
        g_bdown,
    ) = lax.psum(
        (
            g_gain_one,
            g_shift_one,
            g_query,
            g_bquery,
            g_key,
            g_value,
            g_bvalue,
            g_out,
            g_bout,
            g_gain_two,
            g_shift_two,
            g_up,
            g_bup,
            g_down,
            g_bdown,
        ),
        ("dp", "seq"),
    )
    return (
        output,
        grad_patches,
        g_gain_one,
        g_shift_one,
        g_query,
        g_bquery,
        g_key,
        g_value,
        g_bvalue,
        g_out,
        g_bout,
        g_gain_two,
        g_shift_two,
        g_up,
        g_bup,
        g_down,
        g_bdown,
    )


def solution(mesh):
    return jax.shard_map(
        local,
        mesh=mesh,
        in_specs=(
            P("dp", "seq", None),
            P("dp"),
            P(),
            P(),
            P(),
            P(),
            P(),
            P(),
            P(),
            P(),
            P(),
            P(),
            P(),
            P(),
            P(),
            P(),
            P(),
            P("dp", "seq", None),
        ),
        out_specs=(
            P("dp", "seq", None),
            P("dp", "seq", None),
            P(),
            P(),
            P(),
            P(),
            P(),
            P(),
            P(),
            P(),
            P(),
            P(),
            P(),
            P(),
            P(),
            P(),
            P(),
        ),
        check_vma=False,
    )
```

profile of v0, /device:TPU:0, one launch (start us, length us, event | category | flops | bytes accessed | tf_op | source)
XLA Modules:
  0.0 909.4 jit_solution(8345375993950918164)
XLA Ops:
  14.2 5.1 copy.101
  19.4 5.1 all-to-all-start
  24.5 4.2 add_convert_fusion.3
  28.7 5.1 copy.104
  33.8 4.9 all-to-all-start.1
  38.8 7.2 copy.136
  48.8 3.8 copy.110
  52.6 4.2 convolution_convert_fusion.1
  56.8 5.1 copy.107
  62.0 5.1 all-to-all-start.2
  67.1 7.2 copy.137
  77.1 3.8 copy.111
  80.9 7.2 copy.138
  90.9 3.8 copy.112
  96.2 45.2 %while.26 = (s32[]{:T(128)}, bf16[4,544,384]{1,2,0:T(8,128)(2,1)}, f32[4,6,544]{2,1,0:T(8,128)}, bf16[4,544,384]{1,2,0:T(8,128)(2,1)}, s32[4]{0:T(128)S(1)}, /*i...) while((s32[]{:T(128)}, bf16[4,544,384]{1,2,0:T(8,128)(2,1)}, ...), condition=%wide.region_5.6_spmd, body=%wide.region_2.5_spmd.sunk | while | flops 476071264 | bytes 26508796 | solution.py:142
  141.4 4.7 copy.113
  146.1 6.4 all_to_all.144
  156.4 11.9 %fusion.47 = (u8[272,3072]{1,0:T(8,128)(4,1)S(1)}, u8[272,3072]{1,0:T(8,128)(4,1)S(1)}, f32[4,272,3072]{2,1,0:T(8,128)S(1)}) fusion(f32[3072]{0:T(1024)S(1)} %copy-done.30, bf16[768,3072]{1,0:T(8,128)(2,1)} %param.35, f32[4,272,768]{2,1,0:T(8,128)S(1)} %get-tuple-element.238, f32[768]{0:T(1024)S(1)} %copy-done.44, f32[768]{0:T(1024)S(1)} %copy-done.32, ...), kind=kOutput, calls=%fused_computation.101 | convolution fusion | flops 5183127552 | bytes 23128576 | tf_op jit(solution)/shard_map/dot_general | solution.py:17
  168.2 32.6 %multiply_convert_fusion.1 = (bf16[4,272,3072]{2,1,0:T(8,128)(2,1)}, f32[4,272,3072]{2,1,0:T(8,128)}) fusion(f32[4,272,3072]{2,1,0:T(8,128)S(1)} %get-tuple-element.239, f32[3072]{0:T(1024)S(1)} %copy-done.30, u8[272,3072]{1,0:T(8,128)(4,1)S(1)} %get-tuple-element.166, u8[272,3072]{1,0:T(8,128)(4,1)S(1)} %get-tuple-element.165), kind=kLoop, calls=%fused_computation.46 | loop fusion | flops 237305856 | bytes 35106816 | tf_op jit(solution)/shard_map/convert_element_type | solution.py:147
  200.9 19.9 %convert_reduce_fusion = (f32[3072]{0:T(1024)}, bf16[4,272,3072]{2,1,0:T(8,128)(2,1)}) fusion(f32[4,272,3072]{2,1,0:T(8,128)} %get-tuple-element.227, bf16[4,272,768]{2,1,0:T(8,128)(2,1)} %param.39, bf16[3072,768]{1,0:T(8,128)(2,1)} %param.37, f32[4,272,3072]{2,1,0:T(8,128)} %copy-done.9, f32[3072]{0:T(1024)S(1)} %copy-done.30), kind=kOutput, calls=%fused_computation.44 | convolution fusion | flops 5190644736 | bytes 39837696 | tf_op jit(solution)/shard_map/stf,df->std/dot_general | solution.py:21
  220.8 10.6 %multiply_reduce_fusion.1 = (f32[768]{0:T(1024)}, f32[4,272]{1,0:T(4,128)S(1)}, f32[4,272]{1,0:T(4,128)S(1)}, f32[768]{0:T(1024)}, f32[4,272,768]{2,1,0:T(8,128)S(1)}) fusion(f32[4,272,768]{2,1,0:T(8,128)S(1)} %copy-done.6, f32[4,272]{1,0:T(4,128)S(1)} %add_rsqrt_fusion, f32[4,272]{1,0:T(4,128)S(1)} %broadcast_multiply_fusion.4, f32[768]{0:T(1024)S(1)} %copy-done.32, ...), kind=kOutput, calls=%fused_computation.89 | convolution fusion | flops 5141344256 | bytes 18114560 | tf_op jit(solution)/shard_map/stf,df->std/dot_general | solution.py:21
  238.2 3.9 copy.116
  242.1 6.7 all_to_all.145
  248.8 7.0 copy.139
  261.5 104.6 %while.27 = (s32[]{:T(128)}, bf16[4,544,384]{1,2,0:T(8,128)(2,1)}, bf16[4,544,384]{1,2,0:T(8,128)(2,1)}, bf16[4,544,384]{1,2,0:T(8,128)(2,1)}, bf16[4,544,384]{1...) while((s32[]{:T(128)}, bf16[4,544,384]{1,2,0:T(8,128)(2,1)}, ...), condition=%wide.region_12.13_spmd, body=%wide.region_10.12_spmd.sunk | while | flops 1164070272 | bytes 89513552 | solution.py:169
  263.7 4.7 fusion.133
  272.7 5.9 multiply_reduce_fusion.7
  289.8 4.7 fusion.133
  298.9 5.9 multiply_reduce_fusion.7
  316.0 4.7 fusion.133
  325.1 5.9 multiply_reduce_fusion.7
  342.2 4.7 fusion.133
  351.2 5.9 multiply_reduce_fusion.7
  366.1 4.8 copy.129
  370.9 4.7 all-to-all-start.7
  375.7 5.2 convolution_bitcast_fusion.2
  380.9 12.4 %convolution_bitcast_fusion.1 = f32[768,3072]{1,0:T(8,128)} fusion(bf16[4,272,3072]{2,1,0:T(8,128)(2,1)} %get-tuple-element.243, f32[4,272,768]{2,1,0:T(8,128)S(1)} %copy-done.7, f32[768]{0:T(1024)S(1)} %copy-done.45, f32[768]{0:T(1024)S(1)} %copy-done.33, f32[4,272]{1,0:T(4,128)S(1)} %add_rsqrt_fusion, f32[4,272]{1,0:T(4,128)S(1)} %broadcast_multiply_fusion.4), kind=kOutput, calls=%fused_computation.60 | convolution fusion | flops 5138006016 | bytes 19479040 | tf_op jit(solution)/shard_map/std,stf->df/dot_general | solution.py:25
  396.3 4.7 all-to-all-start.5
  404.0 4.7 copy.126
  408.7 4.6 all-to-all-start.6
  430.8 9.2 %convolution_bitcast_fusion = f32[3072,768]{1,0:T(8,128)} fusion(bf16[4,272,3072]{2,1,0:T(8,128)(2,1)S(1)} %bitcast.225, bf16[4,272,768]{2,1,0:T(8,128)(2,1)S(1)} %copy-done.23), kind=kOutput, calls=%fused_computation.59 | convolution fusion | flops 5133828096 | bytes 17793024 | tf_op jit(solution)/shard_map/std,stf->df/dot_general | solution.py:25
  447.5 3.9 fusion.43
  451.4 45.8 %all-reduce = (f32[768]{0:T(1024)}, f32[768]{0:T(1024)}, f32[768]{0:T(1024)}, f32[768]{0:T(1024)}, f32[768]{0:T(1024)}, /*index=5*/f32[768]{0:T(1024)}, f32[768]{0:T(1024)}, f32[3072]{0:T(1024)}, f32[768]{0:T(1024)}) all-reduce(f32[768]{0:T(1024)S(1)} %get-tuple-element.169, ...), channel_id=1, replica_groups=mesh['dp'=16,'seq'=2] {'dp','seq'}, use_global_device_ids=true, to_apply=%region_16.17 | all-reduce | flops 9216 | bytes 73728 | tf_op jit(solution)/shard_map/psum | solution.py:207
  497.2 5.2 fusion.42
  502.4 10.0 %add_convert_fusion.1 = bf16[4,272,768]{2,1,0:T(8,128)(2,1)} fusion(f32[4,272,768]{2,1,0:T(8,128)S(1)} %copy-done.8, bf16[4,272,3072]{2,1,0:T(8,128)(2,1)} %get-tuple-element.226, bf16[3072,768]{1,0:T(8,128)(2,1)} %param.37, f32[768]{0:T(1024)S(1)} %copy-done.48), kind=kOutput, calls=%fused_computation.95 | convolution fusion | flops 5136334848 | bytes 16419840 | tf_op jit(solution)/shard_map/dot_general | solution.py:17
  512.4 366.8 %all-reduce.4.cloned.1.call-done = (f32[768,768]{1,0:T(8,128)}, f32[768,768]{1,0:T(8,128)}, f32[768,768]{1,0:T(8,128)}, f32[768,768]{1,0:T(8,128)}, f32[768,3072]{1,0:T(8,128)}, /*index=5*/f32[3072,768]{1,0:T(8,128)}) async-done(((f32[768,768]{1,0:T(8,128)}, f32[768,768]{1,0:T(8,128)}, f32[768,768]{1,0:T(8,128)}, f32[768,768]{1,0:T(8,128)}, f32[768,3072]{1,0:T(8,128)}, /*index=5*/f32[3072,768]{1,0:T(8,128)}), ...) | async-done | bytes 28311568 | tf_op jit(solution)/shard_map/psum | solution.py:207
  889.0 9.3 %copy.185 = f32[768,3072]{1,0:T(8,128)} copy(f32[768,3072]{1,0:T(8,128)} %get-tuple-element.436) | data formatting | bytes 18874368
  898.3 3.7 copy.186
  (279 shorter events, 180.6 us)
Async XLA Ops:
  7.2 4.1 copy-start
  7.2 4.1 copy-start.2
  7.2 4.0 copy-start.41
  7.2 4.0 copy-start.46
  7.2 4.0 copy-start.34
  9.2 43.4 %copy-start.24 = (f32[4,272]{1,0:T(4,128)}, f32[4,272]{1,0:T(4,128)S(1)}, u32[]{:S(2)}) copy-start(f32[4,272]{1,0:T(4,128)S(1)} %broadcast_multiply_fusion.5) | copy-start | bytes 13060
  11.3 41.3 %copy-start.26 = (f32[4,272]{1,0:T(4,128)}, f32[4,272]{1,0:T(4,128)S(1)}, u32[]{:S(2)}) copy-start(f32[4,272]{1,0:T(4,128)S(1)} %add_rsqrt_fusion.1) | copy-start | bytes 13060
  19.4 5.1 copy-start.42
  19.4 14.5 %all-to-all-start = ((bf16[4,272,768]{1,0,2:T(4,128)(2,1)}), bf16[4,272,768]{1,0,2:T(4,128)(2,1)}, u32[]{:S(2)}, u32[]{:S(2)}) async-start(bf16[4,272,768]{1,0,2:T(4,128)(2,1)} %copy.101), calls=%async_computation | async-start | bytes 4718592 | tf_op jit(solution)/shard_map/all_to_all | solution.py:140
  33.8 28.1 %all-to-all-start.1 = ((bf16[4,272,768]{1,0,2:T(4,128)(2,1)}), bf16[4,272,768]{1,0,2:T(4,128)(2,1)}, u32[]{:S(2)}, u32[]{:S(2)}) async-start(bf16[4,272,768]{1,0,2:T(4,128)(2,1)} %copy.104), calls=%async_computation.1 | async-start | bytes 4718592 | tf_op jit(solution)/shard_map/all_to_all | solution.py:138
  62.0 19.0 %all-to-all-start.2 = ((bf16[4,272,768]{1,0,2:T(4,128)(2,1)}), bf16[4,272,768]{1,0,2:T(4,128)(2,1)}, u32[]{:S(2)}, u32[]{:S(2)}) async-start(bf16[4,272,768]{1,0,2:T(4,128)(2,1)} %copy.107), calls=%async_computation.2 | async-start | bytes 4718592 | tf_op jit(solution)/shard_map/all_to_all | solution.py:139
  90.9 5.3 copy-start.49
  155.5 12.7 %copy-start.5 = (f32[4,272,768]{2,1,0:T(8,128)}, f32[4,272,768]{2,1,0:T(8,128)S(1)}, u32[]{:S(2)}) copy-start(f32[4,272,768]{2,1,0:T(8,128)S(1)} %get-tuple-element.238) | copy-start | bytes 10027012
  168.2 32.6 %copy-start.9 = (f32[4,272,3072]{2,1,0:T(8,128)}, f32[4,272,3072]{2,1,0:T(8,128)S(1)}, u32[]{:S(2)}) copy-start(f32[4,272,3072]{2,1,0:T(8,128)S(1)} %get-tuple-element.239) | copy-start | bytes 40108036
  200.8 19.9 %copy-start.6 = (f32[4,272,768]{2,1,0:T(8,128)S(1)}, f32[4,272,768]{2,1,0:T(8,128)}, u32[]{:S(2)}) copy-start(f32[4,272,768]{2,1,0:T(8,128)} %copy-done.5) | copy-start | bytes 10027012
  220.8 10.6 %copy-start.22 = (bf16[4,272,768]{2,1,0:T(8,128)(2,1)S(1)}, bf16[4,272,768]{2,1,0:T(8,128)(2,1)}, u32[]{:S(2)}) copy-start(bf16[4,272,768]{2,1,0:T(8,128)(2,1)} %param.39) | copy-start | bytes 5013508
  231.4 4.1 copy-start.39
  257.2 4.3 copy-start.50
  272.7 6.0 slice-start
  272.7 6.0 slice-start.1
  298.9 6.0 slice-start
  298.9 6.0 slice-start.1
  325.1 6.0 slice-start
  325.1 6.0 slice-start.1
  351.2 6.0 slice-start
  351.2 6.0 slice-start.1
  366.1 9.5 %copy-start.16 = (bf16[4,2,34,8,384]{4,3,1,2,0:T(8,128)(2,1)S(1)}, bf16[4,2,34,8,384]{4,3,1,2,0:T(8,128)(2,1)}, u32[]{:S(2)}) copy-start(bf16[4,2,34,8,384]{4,3,1,2,0:T(8,128)(2,1)} %copy-done.15) | copy-start | bytes 5013508
  370.9 25.3 %all-to-all-start.7 = ((bf16[4,544,384]{2,0,1:T(4,128)(2,1)}), bf16[4,544,384]{2,0,1:T(4,128)(2,1)}, u32[]{:S(2)}, u32[]{:S(2)}) async-start(bf16[4,544,384]{2,0,1:T(4,128)(2,1)} %copy.129), calls=%async_computation.7 | async-start | bytes 3342336 | tf_op jit(solution)/shard_map/all_to_all | solution.py:175
  375.6 5.3 copy-start.7
  375.6 5.3 copy-start.33
  375.6 5.3 copy-start.45
  380.9 12.4 %copy-start.11 = (bf16[4,544,384]{1,2,0:T(8,128)(2,1)S(1)}, bf16[4,544,384]{1,2,0:T(8,128)(2,1)}, u32[]{:S(2)}) copy-start(bf16[4,544,384]{1,2,0:T(8,128)(2,1)} %get-tuple-element.111) | copy-start | bytes 5013508
  396.3 12.4 %all-to-all-start.5 = ((bf16[4,544,384]{2,0,1:T(4,128)(2,1)}), bf16[4,544,384]{2,0,1:T(4,128)(2,1)}, u32[]{:S(2)}, u32[]{:S(2)}) async-start(bf16[4,544,384]{2,0,1:T(4,128)(2,1)} %copy.123), calls=%async_computation.5 | async-start | bytes 3342336 | tf_op jit(solution)/shard_map/all_to_all | solution.py:173
  408.7 8.9 all-to-all-start.6
  413.3 465.8 %all-reduce.4.cloned.1.call-start = ((), (), s32[]{:S(2)}) async-start(), calls=%async_computation.8 | async-start | bytes 56623104 | tf_op jit(solution)/shard_map/psum | solution.py:207
  419.6 4.0 copy-start.20
  423.6 7.2 slice-start.5
  427.2 3.6 copy-start.23
  447.4 3.9 copy-start.28
  447.4 3.9 copy-start.29
  447.5 3.9 copy-start.31
  447.5 3.9 copy-start.36
  447.5 3.9 copy-start.37
  497.1 5.2 copy-start.8
  497.1 5.2 copy-start.48
  887.5 10.7 %slice-start.2 = ((s8[9437184]{0:T(1024)(128)(4,1)}), s8[4194304]{0:T(1024)(128)(4,1)S(1)}, s32[]{:S(2)}) async-start(s8[9437184]{0:T(1024)(128)(4,1)} %bitcast.211), calls=%async_computation.11 | async-start | bytes 8388608
  889.0 9.3 %slice-start.3 = ((s8[9437184]{0:T(1024)(128)(4,1)}), s8[4194304]{0:T(1024)(128)(4,1)S(1)}, s32[]{:S(2)}) async-start(s8[9437184]{0:T(1024)(128)(4,1)} %bitcast.211), calls=%async_computation.12 | async-start | bytes 8388608
  889.0 9.3 %slice-start.4 = ((s8[9437184]{0:T(1024)(128)(4,1)}), s8[1048576]{0:T(1024)(128)(4,1)S(1)}, s32[]{:S(2)}) async-start(s8[9437184]{0:T(1024)(128)(4,1)} %bitcast.211), calls=%async_computation.13 | async-start | bytes 2097152
  (23 other events, 49.1 us)
Sparse Core Ops, SparseCore 0:
  440.1 438.9 all-reduce.3
where the time goes:
time: 919 us; the launch traced here: 909 us
  waiting for transfers between devices  367 us (40%)
  matrix products  192 us (21%)
  local copies, waits for them, and re-layouts  175 us (19%)
  other arithmetic  72.7 us (8%)
  blocking collectives  58.9 us (6%)
  starting transfers between devices  29.1 us (3%)
  between operations  15.2 us (2%)
    psum x1, waiting for transfers between devices, local(): lax.psum((g_gain_one, g_shift_one, g_query, g_bquery, g_key, g_value, g_b...  367 us
    psum x1, blocking collectives, local(): lax.psum((g_gain_one, g_shift_one, g_query, g_bquery, g_key, g_value, g_b...  45.8 us
    dot_general x6, matrix products, project_back(): jnp.einsum('stf,df->std', grad_rows, weight, preferred_element_type=jnp.f...  42 us
    dot_general x6, matrix products, weight_grad(): jnp.einsum('std,stf->df', left_rows, grad_rows, preferred_element_type=jn...  37.5 us
    dot_general x6, matrix products, project(): return jnp.dot(left_rows, weight, preferred_element_type=jnp.float32)  34.9 us
    convert_element_type x1, other arithmetic, local(): active = exact_gelu(upper_pre).astype(jnp.bfloat16)  32.6 us
    dynamic_slice x36, local copies, waits for them, and re-layouts, local(): lax.map(attend, (query_whole, key_whole, value_whole, lengths))  32.2 us
    unnamed x118, local copies, waits for them, and re-layouts  28 us
  transfers between devices with their start and end apart: 7, of which 1 were waited for; matrix products, arithmetic and copies ran while one was open for 11% of the time, Pallas kernels for 0%

commit v1 on v0

v1 whole, which is shorter than its diff:
```python
import functools

import jax
import jax.numpy as jnp
from jax import lax
from jax.experimental import pallas as pl
from jax.experimental.pallas import tpu as pltpu
from jax.sharding import PartitionSpec as P

F32, BF16 = jnp.float32, jnp.bfloat16
D, HEADS, HEAD_DIM, FF, SLOTS = 768, 12, 64, 3072, 544
STRIPS = 2
ROWS = STRIPS * SLOTS
PAIRS = HEADS // 2
EPS = 1e-06
MASKED = -1e30
GROUPS = 3
GROUP_PAIRS = PAIRS // GROUPS
GCOLS = D // GROUPS
MLP_CALLS = 2
MLP_STEPS = 4
FSTEP = FF // (MLP_CALLS * MLP_STEPS)
FCALL = FF // MLP_CALLS
VMEM = 58 * 1024 * 1024


def params(vmem=VMEM, grid=1):
    return pltpu.CompilerParams(
        vmem_limit_bytes=vmem, dimension_semantics=("arbitrary",) * grid
    )


def dot(a, b):
    return lax.dot_general(a, b, (((1,), (0,)), ((), ())), preferred_element_type=F32)


def dot_bt(a, b):
    return lax.dot_general(a, b, (((1,), (1,)), ((), ())), preferred_element_type=F32)


def dot_at(a, b):
    return lax.dot_general(a, b, (((0,), (0,)), ((), ())), preferred_element_type=F32)


def norm_parts(values):
    centre = jnp.mean(values, axis=-1, keepdims=True)
    centred = values - centre
    spread = jnp.mean(centred * centred, axis=-1, keepdims=True)
    rstd = lax.rsqrt(spread + EPS)
    return centred * rstd, rstd


def gelu_parts(u):
    t = 1.0 / (1.0 + (0.3275911 * 0.7071067811865476) * jnp.abs(u))
    e = jnp.exp(-0.5 * u * u)
    poly = 0.5 * 1.061405429 * t + 0.5 * -1.453152027
    poly = poly * t + 0.5 * 1.421413741
    poly = poly * t + 0.5 * -0.284496736
    poly = poly * t + 0.5 * 0.254829592
    tail = poly * t * e
    cdf = jnp.where(u >= 0, 1.0 - tail, tail)
    return u * cdf, cdf + u * (e * 0.3989422804014327)


def split3(x):
    hi = x.astype(BF16).astype(F32)
    rest = x - hi
    mid = rest.astype(BF16).astype(F32)
    return hi, mid, rest - mid


def lane_iota():
    return lax.broadcasted_iota(jnp.int32, (SLOTS, 128), 1)


def half_mask(lane, h):
    return jnp.where((lane >= 64 * h) & (lane < 64 * h + 64), 1.0, 0.0).astype(BF16)


def key_extra(lane, length, h):
    first = 64 * (1 - h)
    row = lax.broadcasted_iota(jnp.int32, (SLOTS, 128), 0)
    bias = jnp.where(row < length, 0.0, MASKED)
    ones = (lane > first) & (lane < first + 4)
    return jnp.where(lane == first, bias, jnp.where(ones, 1.0, 0.0)).astype(BF16)


def pieces_extra(lane, column, h, lead):
    first = 64 * (1 - h)
    hi, mid, low = split3(column)
    out = jnp.where(lane == first + 3, low, jnp.where(lane == first, lead, 0.0))
    out = jnp.where(lane == first + 2, mid, out)
    return jnp.where(lane == first + 1, hi, out).astype(BF16)


def attend_kernel(
    len_ref, x_ref, g1_ref, s1_ref, wq_ref, bq_ref, wk_ref, wv_ref, bv_ref, wo_ref, bo_ref, g2_ref, s2_ref,
    n1_ref, qa_ref, k_ref, v_ref, ctx_ref, hid_ref, n2_ref, q_scr,
):
    x = x_ref[0].astype(F32)
    scaled, _ = norm_parts(x)
    n1 = (scaled * g1_ref[...] + s1_ref[...]).astype(BF16)
    n1_ref[0] = n1
    q_scr[...] = ((dot(n1, wq_ref[...]) + bq_ref[...]).astype(BF16).astype(F32) * (HEAD_DIM**-0.5)).astype(BF16)
    k_ref[0] = dot(n1, wk_ref[...]).astype(BF16)
    v_ref[0] = (dot(n1, wv_ref[...]) + bv_ref[...]).astype(BF16)
    length = len_ref[pl.program_id(0)]
    lane = lane_iota()
    own = [half_mask(lane, h) for h in (0, 1)]
    kx = [key_extra(lane, length, h) for h in (0, 1)]

    def pair(p, _):
        cols = pl.ds(pl.multiple_of(p * 128, 128), 128)
        qp, kp, vp = q_scr[:, cols], k_ref[0, :, cols], v_ref[0, :, cols]
        ctx = None
        inverses = []
        for h in (0, 1):
            first = 64 * (1 - h)
            query = qp * own[h] + jnp.where(lane == first, 1.0, 0.0).astype(BF16)
            scores = dot_bt(query, kp * own[h] + kx[h])
            top = jnp.max(scores, axis=-1, keepdims=True)
            weights = jnp.exp(scores - top)
            total = jnp.sum(weights, axis=-1, keepdims=True)
            part = dot(weights.astype(BF16), vp * own[h])
            ctx = part if ctx is None else ctx + part
            inverses.append(1.0 / total)
            extra = pieces_extra(lane, -(top + jnp.log(total)), h, 1.0)
            qa_ref[0, :, pl.ds(pl.multiple_of(p * 256 + 128 * h, 128), 128)] = qp * own[h] + extra
        scale = jnp.where(lane < 64, inverses[0], inverses[1])
        ctx_ref[0, :, cols] = (ctx * scale).astype(BF16)
        return 0

    lax.fori_loop(0, PAIRS, pair, 0)
    hidden = x + dot(ctx_ref[0], wo_ref[...]) + bo_ref[...]
    hid_ref[0] = hidden
    scaled, _ = norm_parts(hidden)
    n2_ref[0] = (scaled * g2_ref[...] + s2_ref[...]).astype(BF16)


def whole(shape):
    return pl.BlockSpec(shape, lambda *_: (0,) * len(shape))


def strip_block(cols):
    return pl.BlockSpec((1, SLOTS, cols), lambda s, *_: (s, 0, 0))


def strips_of(cols, dtype):
    return jax.ShapeDtypeStruct((STRIPS, SLOTS, cols), dtype)


def attend(lens, x, g1, s1, wq, bq, wk, wv, bv, wo, bo, g2, s2):
    vec, mat = whole((1, D)), whole((D, D))
    return pl.pallas_call(
        attend_kernel,
        grid_spec=pltpu.PrefetchScalarGridSpec(
            num_scalar_prefetch=1,
            grid=(STRIPS,),
            in_specs=[strip_block(D), vec, vec, mat, vec, mat, mat, vec, mat, vec, vec, vec],
            out_specs=[strip_block(D), strip_block(2 * D)] + [strip_block(D)] * 5,
            scratch_shapes=[pltpu.VMEM((SLOTS, D), BF16)],
        ),
        out_shape=[strips_of(D, BF16), strips_of(2 * D, BF16), strips_of(D, BF16), strips_of(D, BF16),
                   strips_of(D, BF16), strips_of(D, F32), strips_of(D, BF16)],
        compiler_params=params(),
        name="attend",
    )(lens, x, g1, s1, wq, bq, wk, wv, bv, wo, bo, g2, s2)


def mlp_kernel(
    first, last, at_ref, n2_ref, cot_ref, up_ref, bup_ref, dn_ref, bdn_ref, acc_in_ref, *rest
):
    if first:
        gn_in_ref = None
    else:
        gn_in_ref, rest = rest[0], rest[1:]
    keep_ref, send_ref, out_ref, gn_ref, gbup_ref, a_scr, g_scr = rest[:7]
    acc_ref = rest[7] if last else out_ref
    step = pl.program_id(0)

    @pl.when(step == 0)
    def _():
        acc_ref[...] = acc_in_ref[...] + bdn_ref[...] if first else acc_in_ref[...]
        gn_ref[...] = jnp.zeros_like(gn_ref) if first else gn_in_ref[...]

    up, down, bias = up_ref[...], dn_ref[...], bup_ref[...]
    sums = None
    for r in range(0, ROWS, SLOTS):
        rows = slice(r, r + SLOTS)
        u = dot(n2_ref[rows], up) + bias
        grad_active = dot_bt(cot_ref[rows], down)
        active, slope = gelu_parts(u)
        active = active.astype(BF16)
        grad_upper = (grad_active * slope).astype(BF16)
        a_scr[rows] = active
        g_scr[rows] = grad_upper
        acc_ref[rows] += dot(active, down)
        gn_ref[rows] += dot_bt(grad_upper, up)
        part = jnp.sum(grad_upper.astype(F32), axis=0, keepdims=True)
        sums = part if sums is None else sums + part
    gbup_ref[...] = sums
    grad_down = dot_at(a_scr[...], cot_ref[...]).astype(BF16)
    grad_up = dot_at(n2_ref[...], g_scr[...]).astype(BF16)
    core, place = at_ref[0], at_ref[1]
    chunk = FCALL // 16
    per_step = FSTEP // chunk
    rows_up = D // 16
    half, col = step // 2, lax.rem(step, 2)

    def put(down_ref, up_out_ref):
        for i in range(per_step):
            down_ref[(step * per_step + i) ^ place] = grad_down[i * chunk : (i + 1) * chunk]
        for i in range(16):
            up_out_ref[
                i ^ place,
                pl.ds(pl.multiple_of(half * rows_up, 16), rows_up),
                pl.ds(pl.multiple_of(col * FSTEP, 128), FSTEP),
            ] = grad_up[i * rows_up : (i + 1) * rows_up]

    @pl.when(core == 0)
    def _():
        put(keep_ref, send_ref)

    @pl.when(core == 1)
    def _():
        put(send_ref, keep_ref)

    if last:
        @pl.when(step == MLP_STEPS - 1)
        def _():
            out_ref[...] = acc_ref[...].astype(BF16)


def mlp(call, at, n2, cot, w_up, b_up, w_down, b_down, acc, gn):
    first, last = call == 0, call == MLP_CALLS - 1
    base = call * MLP_STEPS
    piece = jax.ShapeDtypeStruct((16, FCALL // 16, D), BF16)
    rows = whole((ROWS, D))
    in_specs = [
        rows, rows,
        pl.BlockSpec((D, FSTEP), lambda s, *_: (0, base + s)),
        pl.BlockSpec((1, FSTEP), lambda s, *_: (0, base + s)),
        pl.BlockSpec((FSTEP, D), lambda s, *_: (base + s, 0)),
        whole((1, D)), rows,
    ]
    operands = [n2, cot, w_up, b_up, w_down, b_down, acc]
    if not first:
        in_specs.append(rows)
        operands.append(gn)
    return pl.pallas_call(
        functools.partial(mlp_kernel, first, last),
        grid_spec=pltpu.PrefetchScalarGridSpec(
            num_scalar_prefetch=1,
            grid=(MLP_STEPS,),
            in_specs=in_specs,
            out_specs=[whole(piece.shape), whole(piece.shape), rows, rows,
                       pl.BlockSpec((1, FSTEP), lambda s, *_: (0, s))],
            scratch_shapes=[pltpu.VMEM((ROWS, FSTEP), BF16)] * 2
            + ([pltpu.VMEM((ROWS, D), F32)] if last else []),
        ),
        out_shape=[piece, piece, jax.ShapeDtypeStruct((ROWS, D), BF16 if last else F32),
                   jax.ShapeDtypeStruct((ROWS, D), F32), jax.ShapeDtypeStruct((1, FCALL), F32)],
        compiler_params=params(),
        name="mlp",
    )(at, *operands)


def mid_kernel(
    at_ref, gn_ref, hid_ref, cot_ref, ctx_ref, wo_ref, g2_ref,
    gh_ref, dctx_ref, gwo_ref, ggain_ref, gshift_ref, gbo_ref, gbdn_ref, acc_scr,
):
    strip = pl.program_id(0)
    grad = gn_ref[0]
    cot = cot_ref[0].astype(F32)
    scaled, rstd = norm_parts(hid_ref[0])
    t = grad * g2_ref[...]
    cross = jnp.mean(t * scaled, axis=-1, keepdims=True)
    grad_hidden = cot + rstd * (t - jnp.mean(t, axis=-1, keepdims=True) - scaled * cross)
    gh_ref[0] = grad_hidden
    grad_attn = grad_hidden.astype(BF16)
    dctx_ref[0] = dot_bt(grad_attn, wo_ref[...]).astype(BF16)
    grad_out = dot_at(ctx_ref[0], grad_attn)
    sums = [
        jnp.sum(grad * scaled, axis=0, keepdims=True),
        jnp.sum(grad, axis=0, keepdims=True),
        jnp.sum(grad_attn.astype(F32), axis=0, keepdims=True),
        jnp.sum(cot, axis=0, keepdims=True),
    ]
    refs = [ggain_ref, gshift_ref, gbo_ref, gbdn_ref]

    @pl.when(strip == 0)
    def _():
        acc_scr[...] = grad_out
        for ref, value in zip(refs, sums):
            ref[...] = value

    @pl.when(strip > 0)
    def _():
        total = (acc_scr[...] + grad_out).astype(BF16)
        for i in range(16):
            gwo_ref[i ^ at_ref[1]] = total[i * 48 : (i + 1) * 48]
        for ref, value in zip(refs, sums):
            ref[...] += value


def middle(at, gn, hid, cot, ctx, wo, g2):
    vec = jax.ShapeDtypeStruct((1, D), F32)
    return pl.pallas_call(
        mid_kernel,
        grid_spec=pltpu.PrefetchScalarGridSpec(
            num_scalar_prefetch=1,
            grid=(STRIPS,),
            in_specs=[strip_block(D)] * 4 + [whole((D, D)), whole((1, D))],
            out_specs=[strip_block(D), strip_block(D), whole((16, 48, D))] + [whole((1, D))] * 4,
            scratch_shapes=[pltpu.VMEM((D, D), F32)],
        ),
        out_shape=[strips_of(D, F32), strips_of(D, BF16), jax.ShapeDtypeStruct((16, 48, D), BF16)] + [vec] * 4,
        compiler_params=params(),
        name="middle",
    )(at, gn, hid, cot, ctx, wo, g2)


def back_kernel(
    first, at_ref, len_ref, qa_ref, k_ref, v_ref, dctx_ref, ctx_ref, n1_ref, wq_ref, wk_ref, wv_ref, *rest
):
    if first:
        gn_in_ref = None
    else:
        gn_in_ref, rest = rest[0], rest[1:]
    grads_ref, gn_ref, sums_ref, d_scr, acc_scr = rest
    strip = pl.program_id(0)
    lane = lane_iota()
    own = [half_mask(lane, h) for h in (0, 1)]
    length = len_ref[strip]
    kx = [key_extra(lane, length, h) for h in (0, 1)]
    vx = [
        jnp.where((lane > 64 * (1 - h)) & (lane < 64 * (1 - h) + 4), 1.0, 0.0).astype(BF16)
        for h in (0, 1)
    ]
    for p in range(GROUP_PAIRS):
        cols = slice(p * 128, p * 128 + 128)
        kp, vp, dp, cp = k_ref[0, :, cols], v_ref[0, :, cols], dctx_ref[0, :, cols], ctx_ref[0, :, cols]
        product = dp.astype(F32) * cp.astype(F32)
        dq, dk, dv = [], [], []
        for h in (0, 1):
            query = qa_ref[0, :, p * 256 + 128 * h : p * 256 + 128 * h + 128]
            inner = jnp.sum(product * own[h].astype(F32), axis=-1, keepdims=True)
            grad = dp * own[h] + pieces_extra(lane, -inner, h, 0.0)
            probs = jnp.exp(dot_bt(kp * own[h] + kx[h], query))
            grad_scores = (probs * dot_bt(vp * own[h] + vx[h], grad)).astype(BF16)
            dv.append(dot(probs.astype(BF16), dp))
            dk.append(dot(grad_scores, query))
            dq.append(dot_at(grad_scores, kp))
        low = lane < 64
        d_scr[:, cols] = (jnp.where(low, dq[0], dq[1]) * (HEAD_DIM**-0.5)).astype(BF16)
        d_scr[:, GCOLS + p * 128 : GCOLS + p * 128 + 128] = jnp.where(low, dk[0], dk[1]).astype(BF16)
        d_scr[:, 2 * GCOLS + p * 128 : 2 * GCOLS + p * 128 + 128] = jnp.where(low, dv[0], dv[1]).astype(BF16)
    d_all = d_scr[...]
    back = dot_bt(d_all[:, :GCOLS], wq_ref[...])
    back += dot_bt(d_all[:, GCOLS : 2 * GCOLS], wk_ref[...])
    back += dot_bt(d_all[:, 2 * GCOLS :], wv_ref[...])
    gn_ref[0] = back if first else back + gn_in_ref[0]
    grad = dot_at(n1_ref[0], d_all)
    sums = jnp.sum(d_all.astype(F32), axis=0, keepdims=True)

    @pl.when(strip == 0)
    def _():
        acc_scr[...] = grad
        sums_ref[...] = sums

    @pl.when(strip > 0)
    def _():
        total = (acc_scr[...] + grad).astype(BF16)
        for i in range(16):
            grads_ref[i ^ at_ref[1]] = total[i * 48 : (i + 1) * 48]
        sums_ref[...] += sums


def attend_back(group, at, lens, qa, k, v, dctx, ctx, n1, wq, wk, wv, gn):
    first = group == 0

    def cols(width):
        return pl.BlockSpec((1, SLOTS, width), lambda s, *_: (s, 0, group))

    weight = pl.BlockSpec((D, GCOLS), lambda s, *_: (0, group))
    in_specs = [cols(2 * GCOLS)] + [cols(GCOLS)] * 4 + [strip_block(D)] + [weight] * 3
    operands = [qa, k, v, dctx, ctx, n1, wq, wk, wv]
    if not first:
        in_specs.append(strip_block(D))
        operands.append(gn)
    return pl.pallas_call(
        functools.partial(back_kernel, first),
        grid_spec=pltpu.PrefetchScalarGridSpec(
            num_scalar_prefetch=2,
            grid=(STRIPS,),
            in_specs=in_specs,
            out_specs=[whole((16, 48, D)), strip_block(D), whole((1, 3 * GCOLS))],
            scratch_shapes=[pltpu.VMEM((SLOTS, 3 * GCOLS), BF16), pltpu.VMEM((D, 3 * GCOLS), F32)],
        ),
        out_shape=[jax.ShapeDtypeStruct((16, 48, D), BF16), strips_of(D, F32),
                   jax.ShapeDtypeStruct((1, 3 * GCOLS), F32)],
        compiler_params=params(),
        name="attend_back",
    )(at, lens, *operands)


def end_kernel(gn_ref, x_ref, gh_ref, g1_ref, gp_ref, ggain_ref, gshift_ref):
    strip = pl.program_id(0)
    grad = gn_ref[0]
    scaled, rstd = norm_parts(x_ref[0].astype(F32))
    t = grad * g1_ref[...]
    cross = jnp.mean(t * scaled, axis=-1, keepdims=True)
    grad_in = rstd * (t - jnp.mean(t, axis=-1, keepdims=True) - scaled * cross)
    gp_ref[0] = (gh_ref[0] + grad_in).astype(BF16)
    sums = [jnp.sum(grad * scaled, axis=0, keepdims=True), jnp.sum(grad, axis=0, keepdims=True)]

    @pl.when(strip == 0)
    def _():
        ggain_ref[...], gshift_ref[...] = sums

    @pl.when(strip > 0)
    def _():
        ggain_ref[...] += sums[0]
        gshift_ref[...] += sums[1]


def end(gn, x, gh, g1):
    vec = jax.ShapeDtypeStruct((1, D), F32)
    return pl.pallas_call(
        end_kernel,
        grid=(STRIPS,),
        in_specs=[strip_block(D)] * 3 + [whole((1, D))],
        out_specs=[strip_block(D)] + [whole((1, D))] * 2,
        out_shape=[strips_of(D, BF16), vec, vec],
        compiler_params=params(),
        name="end",
    )(gn, x, gh, g1)


def widen_mlp_kernel(at_ref, mine_ref, other_ref, *rest):
    down_ref, up_ref = rest[-2:]
    swap = at_ref[0] == 1
    mine, other = mine_ref[0], other_ref[0]
    down_ref[...] = jnp.where(swap, other, mine).astype(F32)
    up = jnp.where(swap, mine, other).astype(F32)
    up_ref[:, :D] = up[:48]
    up_ref[:, D:] = up[48:]


def widen_mlp(call, at, mine, other, given):
    block = pl.BlockSpec((1, FCALL // 16, D), lambda i, at_ref: (i ^ at_ref[1], 0, 0))
    operands = [mine, other] + list(given)
    return pl.pallas_call(
        widen_mlp_kernel,
        grid_spec=pltpu.PrefetchScalarGridSpec(
            num_scalar_prefetch=1,
            grid=(16,),
            in_specs=[block, block] + [pl.BlockSpec(memory_space=pl.ANY)] * len(given),
            out_specs=[
                pl.BlockSpec((FCALL // 16, D), lambda i, *_: (16 * call + i, 0)),
                pl.BlockSpec((D // 16, FCALL), lambda i, *_: (i, call)),
            ],
        ),
        out_shape=[jax.ShapeDtypeStruct((FF, D), F32), jax.ShapeDtypeStruct((D, FF), F32)],
        input_output_aliases={3: 0, 4: 1} if given else {},
        compiler_params=params(),
        name="widen_mlp",
    )(at, *operands)


def widen_attn_kernel(at_ref, mine_ref, other_ref, out_ref, q_ref, k_ref, v_ref):
    swap = at_ref[0] == 1
    mine, other = mine_ref[0], other_ref[0]
    low = jnp.where(swap, other, mine).astype(F32)
    high = jnp.where(swap, mine, other).astype(F32)
    out_ref[...] = low[:48]
    for g, block in enumerate((low[48:], high[:48], high[48:])):
        cols = slice(g * GCOLS, (g + 1) * GCOLS)
        q_ref[:, cols] = block[:, :GCOLS]
        k_ref[:, cols] = block[:, GCOLS : 2 * GCOLS]
        v_ref[:, cols] = block[:, 2 * GCOLS :]


def widen_attn(at, mine, other):
    block = pl.BlockSpec((1, 96, D), lambda i, at_ref: (i ^ at_ref[1], 0, 0))
    return pl.pallas_call(
        widen_attn_kernel,
        grid_spec=pltpu.PrefetchScalarGridSpec(
            num_scalar_prefetch=1,
            grid=(16,),
            in_specs=[block, block],
            out_specs=[pl.BlockSpec((48, D), lambda i, *_: (i, 0))] * 4,
        ),
        out_shape=[jax.ShapeDtypeStruct((D, D), F32)] * 4,
        compiler_params=params(),
        name="widen_attn",
    )(at, mine, other)


def swap(value, axis, bit, size):
    return lax.ppermute(value, axis, [(i, i ^ bit) for i in range(size)])


def sum_scatter(keep, send, bits, dp):
    total = keep + swap(send, "seq", 1, 2)
    for step, bit in enumerate(bits):
        if step < 4:
            half = total.shape[0] // 2
            total = total[:half] + swap(total[half:], "dp", bit, dp)
        else:
            total = total + swap(total, "dp", bit, dp)
    return total


def gather(total, bits, dp):
    for bit in reversed(bits[:4]):
        total = jnp.concatenate([total, swap(total, "dp", bit, dp)], axis=0)
    return total, swap(total, "seq", 1, 2)


def local(
    dp, patches, lengths, gain_one, shift_one, w_query, b_query, w_key, w_value, b_value, w_out, b_out,
    gain_two, shift_two, w_up, b_up, w_down, b_down, cotangent,
):
    core, block = lax.axis_index("seq"), lax.axis_index("dp")
    bits = [1 << i for i in range(dp.bit_length() - 1)]

    def order_of(bits):
        place = jnp.int32(0)
        for bit in bits[:4]:
            place = place * 2 + jnp.where((block & bit) != 0, 1, 0)
        return jnp.stack([core, place]).astype(jnp.int32)

    row = lambda v: v.reshape(1, -1)
    strips = lambda v: lax.all_to_all(v, "seq", split_axis=0, concat_axis=1, tiled=True)
    slots = lambda v: lax.all_to_all(v, "seq", split_axis=1, concat_axis=0, tiled=True)
    x, cot = strips(patches), strips(cotangent)
    lens = lax.dynamic_slice(lengths, (core * STRIPS,), (STRIPS,))
    n1, qa, k, v, ctx, hid, n2 = attend(
        lens, x, row(gain_one), row(shift_one), w_query, row(b_query), w_key, w_value, row(b_value),
        w_out, row(b_out), row(gain_two), row(shift_two),
    )
    flat = lambda v: v.reshape(ROWS, D)
    acc, gn = flat(hid), None
    at = order_of(bits)
    pieces, g_bup = [], []
    for call in range(MLP_CALLS):
        keep, send, acc, gn, sums = mlp(
            call, at, flat(n2), flat(cot), w_up, row(b_up), w_down, row(b_down), acc, gn
        )
        pieces.append((keep, send))
        g_bup.append(sums)
    output = slots(acc.reshape(STRIPS, SLOTS, D))
    gh, dctx, g_out, g_gain_two, g_shift_two, g_bout, g_bdown = middle(
        at, gn.reshape(STRIPS, SLOTS, D), hid, cot, ctx, w_out, row(gain_two)
    )
    gn, blocks, sums = None, [g_out], []
    for group in range(GROUPS):
        grads, gn, part = attend_back(
            group, at, lens, qa, k, v, dctx, ctx, n1, w_query, w_key, w_value, gn
        )
        blocks.append(grads)
        sums.append(part)
    gp, g_gain_one, g_shift_one = end(gn, x, gh, row(gain_one))
    grad_patches = slots(gp)
    low = jnp.concatenate(blocks[:2], axis=1)
    high = jnp.concatenate(blocks[2:], axis=1)
    pieces.append((jnp.where(core == 0, low, high), jnp.where(core == 0, high, low)))
    g_bquery = jnp.concatenate([s[:, :GCOLS] for s in sums], axis=1)
    g_bvalue = jnp.concatenate([s[:, 2 * GCOLS :] for s in sums], axis=1)
    small = [g_gain_one, g_shift_one, g_bquery, g_bvalue, g_bout, g_gain_two, g_shift_two, g_bdown] + g_bup
    small = lax.psum(jnp.concatenate(small, axis=1), ("dp", "seq"))[0]
    vecs = [small[i * D : (i + 1) * D] for i in range(8)]
    g_bup = small[8 * D :]
    given = ()
    for call in range(MLP_CALLS):
        mine, other = gather(sum_scatter(*pieces[call], bits, dp), bits, dp)
        given = widen_mlp(call, at, mine, other, given)
    g_down, g_up = given
    mine, other = gather(sum_scatter(*pieces[-1], bits, dp), bits, dp)
    g_out, g_query, g_key, g_value = widen_attn(at, mine, other)
    return (
        output, grad_patches, vecs[0], vecs[1], g_query, vecs[2], g_key, g_value, vecs[3], g_out, vecs[4],
        vecs[5], vecs[6], g_up, g_bup, g_down, vecs[7],
    )


def solution(mesh):
    dp = mesh.shape["dp"]
    rows, rep = P("dp", "seq", None), P()
    return jax.shard_map(
        functools.partial(local, dp),
        mesh=mesh,
        in_specs=(rows, P("dp")) + (rep,) * 15 + (rows,),
        out_specs=(rows, rows) + (rep,) * 15,
        check_vma=False,
    )
```

time: 919 us -> 536 us (0.58)
  Pallas kernels: 0 us -> 203 us
  matrix products: 192 us -> 0 us
  waiting for transfers between devices: 367 us -> 184 us
  local copies, waits for them, and re-layouts: 175 us -> 34.6 us
  other arithmetic: 72.7 us -> 16 us
  blocking collectives: 58.9 us -> 40.5 us
  starting transfers between devices: 29.1 us -> 45.8 us
  between operations: 15.2 us -> 1.58 us
    psum x1 -> x0, waiting for transfers between devices: 367 us -> none  [local(): lax.psum((g_gain_one, g_shift_one, g_query, g_bquery, g_key, g_value, g_b...]
    pallas_call x0 -> x11, Pallas kernels: none -> 203 us  [the longest x2 68.1 us: mlp(): pl.pallas_call(functools.partial(mlp_kernel, first, last), grid_spec=pltp...]
    dot_general x46 -> x0, matrix products: 192 us -> none  [the longest x6 42 us: project_back(): jnp.einsum('stf,df->std', grad_rows, weight, preferred_element_type=jnp.f...]
    ppermute x0 -> x30, waiting for transfers between devices: none -> 182 us  [swap(): return lax.ppermute(value, axis, [(i, i ^ bit) for i in range(size)])]
    convert_element_type x6 -> x0, other arithmetic: 48 us -> none  [the longest x1 32.6 us: local(): active = exact_gelu(upper_pre).astype(jnp.bfloat16)]
    all_to_all x16 -> x4, local copies, waits for them, and re-layouts: 46.8 us -> 5.38 us  [the longest x2 2.78 us: local(): lax.all_to_all(v, 'seq', split_axis=1, concat_axis=0, tiled=True)]
    dynamic_slice x36 -> x1, local copies, waits for them, and re-layouts: 32.2 us -> 0.66 us  [local(): lens = lax.dynamic_slice(lengths, (core * STRIPS,), (STRIPS,))]
    ppermute x0 -> x30, starting transfers between devices: none -> 30.7 us  [swap(): return lax.ppermute(value, axis, [(i, i ^ bit) for i in range(size)])]
  transfers between devices with their start and end apart: 7 -> 34, of which waited for: 1 -> 17; matrix products, arithmetic and copies ran while one was open for 11% -> 8% of each run, Pallas kernels for 0% -> 17%
where the time goes in v1:
time: 536 us; the launch traced here: 526 us
  Pallas kernels  203 us (38%)
  waiting for transfers between devices  184 us (34%)
  starting transfers between devices  45.8 us (9%)
  blocking collectives  40.5 us (8%)
  local copies, waits for them, and re-layouts  34.6 us (6%)
  other arithmetic  16 us (3%)
    ppermute x30, waiting for transfers between devices, swap(): return lax.ppermute(value, axis, [(i, i ^ bit) for i in range(size)])  182 us
    pallas_call x2, Pallas kernels, mlp(): pl.pallas_call(functools.partial(mlp_kernel, first, last), grid_spec=pltp...  68.1 us
    pallas_call x3, Pallas kernels, attend_back(): pl.pallas_call(functools.partial(back_kernel, first), grid_spec=pltpu.Pre...  50.3 us
    psum x1, blocking collectives, local(): small = lax.psum(jnp.concatenate(small, axis=1), ('dp', 'seq'))[0]  40.5 us
    pallas_call x1, Pallas kernels, attend(): pl.pallas_call(attend_kernel, grid_spec=pltpu.PrefetchScalarGridSpec(num_...  31.2 us
    ppermute x30, starting transfers between devices, swap(): return lax.ppermute(value, axis, [(i, i ^ bit) for i in range(size)])  30.7 us
    pallas_call x2, Pallas kernels, widen_mlp(): pl.pallas_call(widen_mlp_kernel, grid_spec=pltpu.PrefetchScalarGridSpec(n...  24.3 us
    unnamed x100, local copies, waits for them, and re-layouts  12.5 us
  transfers between devices with their start and end apart: 34, of which 17 were waited for; matrix products, arithmetic and copies ran while one was open for 8% of the time, Pallas kernels for 17%

profile of v1, /device:TPU:0, one launch (start us, length us, event | category | flops | bytes accessed | tf_op | source)
XLA Modules:
  0.0 526.2 jit_solution(14589449961848937045)
XLA Ops:
  0.7 3.8 all-to-all-start
  9.3 3.7 all-to-all-start.1
  18.2 31.2 %attend.1 = (bf16[2,544,768]{2,1,0:T(8,128)(2,1)}, bf16[2,544,1536]{2,1,0:T(8,128)(2,1)}, bf16[2,544,768]{2,1,0:T(8,128)(2,1)}, bf16[2,544,768]{2,1,0:T(8,128)(2...) custom-call(s32[2]{0:T(128)} %dynamic_slice.3.len_ref, ...), custom_call_target="tpu_custom_call" | custom-call | tf_op jit(solution)/shard_map/attend/pallas_call | solution.py:154
  49.4 33.7 %mlp.2 = (bf16[16,96,768]{2,1,0:T(8,128)(2,1)}, bf16[16,96,768]{2,1,0:T(8,128)(2,1)}, f32[1088,768]{1,0:T(8,128)}, f32[1088,768]{1,0:T(8,128)}, f32[1,1536]{1,0:T(1,128)}) custom-call(s32[2]{0:T(128)} %pad_add_fusion.at_ref, bf16[1088,768]{1,0:T(8,128)(2,1)} %bitcast.36, bf16[1088,768]{1,0:T(8,128)(2,1)} %bitcast.26, bf16[768,3072]{1,0:T(8,128)(2,1)} %up_ref.3, ...), custom_call_target="tpu_custom_call" | custom-call | tf_op jit(solution)/shard_map/mlp/pallas_call | solution.py:250
  83.1 34.4 %mlp.3 = (bf16[16,96,768]{2,1,0:T(8,128)(2,1)}, bf16[16,96,768]{2,1,0:T(8,128)(2,1)}, bf16[1088,768]{1,0:T(8,128)(2,1)}, f32[1088,768]{1,0:T(8,128)}, f32[1,1536]{1,0:T(1,128)}) custom-call(s32[2]{0:T(128)} %pad_add_fusion.at_ref, bf16[1088,768]{1,0:T(8,128)(2,1)} %bitcast.37, bf16[1088,768]{1,0:T(8,128)(2,1)} %bitcast.27, bf16[768,3072]{1,0:T(8,128)(2,1)} %up_ref.3, ...), custom_call_target="tpu_custom_call" | custom-call | tf_op jit(solution)/shard_map/mlp/pallas_call | solution.py:250
  118.0 11.7 %middle.1 = (f32[2,544,768]{2,1,0:T(8,128)}, bf16[2,544,768]{2,1,0:T(8,128)(2,1)}, bf16[16,48,768]{2,1,0:T(8,128)(2,1)}, f32[1,768]{1,0:T(1,128)}, f32[1,768]{1,...) custom-call(s32[2]{0:T(128)} %pad_add_fusion.at_ref, f32[2,544,768]{2,1,0:T(8,128)} %bitcast.38, ...), custom_call_target="tpu_custom_call" | custom-call | tf_op jit(solution)/shard_map/middle/pallas_call | solution.py:308
  131.1 16.4 %attend_back.3 = (bf16[16,48,768]{2,1,0:T(8,128)(2,1)}, f32[2,544,768]{2,1,0:T(8,128)}, f32[1,768]{1,0:T(1,128)}) custom-call(s32[2]{0:T(128)} %pad_add_fusion.at_ref, s32[2]{0:T(128)} %dynamic_slice.3.len_ref, bf16[2,544,1536]{2,1,0:T(8,128)(2,1)} %get-tuple-element.66.qa_ref, bf16[2,544,768]{2,1,0:T(8,128)(2,1)} %get-tuple-element.67.k_ref, ...), custom_call_target="tpu_custom_call" | custom-call | tf_op jit(solution)/shard_map/attend_back/pallas_call | solution.py:391
  147.5 16.8 %attend_back.4 = (bf16[16,48,768]{2,1,0:T(8,128)(2,1)}, f32[2,544,768]{2,1,0:T(8,128)}, f32[1,768]{1,0:T(1,128)}) custom-call(s32[2]{0:T(128)} %pad_add_fusion.at_ref, s32[2]{0:T(128)} %dynamic_slice.3.len_ref, bf16[2,544,1536]{2,1,0:T(8,128)(2,1)} %get-tuple-element.66.qa_ref, bf16[2,544,768]{2,1,0:T(8,128)(2,1)} %get-tuple-element.67.k_ref, ...), custom_call_target="tpu_custom_call" | custom-call | tf_op jit(solution)/shard_map/attend_back/pallas_call | solution.py:391
  164.3 17.0 %attend_back.5 = (bf16[16,48,768]{2,1,0:T(8,128)(2,1)}, f32[2,544,768]{2,1,0:T(8,128)}, f32[1,768]{1,0:T(1,128)}) custom-call(s32[2]{0:T(128)} %pad_add_fusion.at_ref, s32[2]{0:T(128)} %dynamic_slice.3.len_ref, bf16[2,544,1536]{2,1,0:T(8,128)(2,1)} %get-tuple-element.66.qa_ref, bf16[2,544,768]{2,1,0:T(8,128)(2,1)} %get-tuple-element.67.k_ref, ...), custom_call_target="tpu_custom_call" | custom-call | tf_op jit(solution)/shard_map/attend_back/pallas_call | solution.py:391
  184.8 2.4 add.68
  187.3 3.0 collective-permute-start.11
  191.1 1.6 collective-permute-start.21
  193.9 23.1 %collective-permute-done.11 = bf16[8,96,768]{2,1,0:T(8,128)(2,1)S(1)} collective-permute-done((bf16[8,96,768]{2,1,0:T(8,128)(2,1)S(1)}, bf16[8,96,768]{2,1,0:T(8,128)(2,1)S(1)}, u32[]{:S(2)}, u32[]{:S(2)}) %collective-permute-start.11) | collective-permute-done | bytes 1179680 | tf_op jit(solution)/shard_map/ppermute | solution.py:501
  217.2 2.1 collective-permute-start.12
  219.4 23.0 %collective-permute-done.21 = bf16[8,96,768]{2,1,0:T(8,128)(2,1)S(1)} collective-permute-done((bf16[8,96,768]{2,1,0:T(8,128)(2,1)S(1)}, bf16[8,96,768]{2,1,0:T(8,128)(2,1)S(1)}, u32[]{:S(2)}, u32[]{:S(2)}) %collective-permute-start.21) | collective-permute-done | bytes 1179680 | tf_op jit(solution)/shard_map/ppermute | solution.py:501
  242.5 2.1 collective-permute-start.22
  244.7 22.5 %collective-permute-done.1 = bf16[8,96,768]{2,1,0:T(8,128)(2,1)S(1)} collective-permute-done((bf16[8,96,768]{2,1,0:T(8,128)(2,1)S(1)}, bf16[8,96,768]{2,1,0:T(8,128)(2,1)S(1)}, u32[]{:S(2)}, u32[]{:S(2)}) %collective-permute-start.1) | collective-permute-done | bytes 1179680 | tf_op jit(solution)/shard_map/ppermute | solution.py:501
  267.3 1.8 collective-permute-start.2
  269.2 1.6 collective-permute-start.13
  271.5 10.7 %collective-permute-done.2 = bf16[4,96,768]{2,1,0:T(8,128)(2,1)S(1)} collective-permute-done((bf16[4,96,768]{2,1,0:T(8,128)(2,1)S(1)}, bf16[4,96,768]{2,1,0:T(8,128)(2,1)S(1)}, u32[]{:S(2)}, u32[]{:S(2)}) %collective-permute-start.2) | collective-permute-done | bytes 589856 | tf_op jit(solution)/shard_map/ppermute | solution.py:501
  282.3 1.6 collective-permute-start.3
  284.0 2.7 collective-permute-start.14
  287.1 8.3 %collective-permute-done.3 = bf16[2,96,768]{2,1,0:T(8,128)(2,1)S(1)} collective-permute-done((bf16[2,96,768]{2,1,0:T(8,128)(2,1)S(1)}, bf16[2,96,768]{2,1,0:T(8,128)(2,1)S(1)}, u32[]{:S(2)}, u32[]{:S(2)}) %collective-permute-start.3) | collective-permute-done | bytes 294944 | tf_op jit(solution)/shard_map/ppermute | solution.py:501
  295.5 1.4 collective-permute-start.4
  297.6 1.6 collective-permute-start.15
  299.2 8.9 %collective-permute-done.24 = bf16[1,96,768]{2,1,0:T(8,128)(2,1)S(1)} collective-permute-done((bf16[1,96,768]{2,1,0:T(8,128)(2,1)S(1)}, bf16[1,96,768]{2,1,0:T(8,128)(2,1)S(1)}, u32[]{:S(2)}, u32[]{:S(2)}) %collective-permute-start.24) | collective-permute-done | bytes 147488 | tf_op jit(solution)/shard_map/ppermute | solution.py:501
  308.8 2.5 collective-permute-done.4
  312.4 6.7 %collective-permute-done.15 = bf16[1,96,768]{2,1,0:T(8,128)(2,1)S(1)} collective-permute-done((bf16[1,96,768]{2,1,0:T(8,128)(2,1)S(1)}, bf16[1,96,768]{2,1,0:T(8,128)(2,1)S(1)}, u32[]{:S(2)}, u32[]{:S(2)}) %collective-permute-start.15) | collective-permute-done | bytes 147488 | tf_op jit(solution)/shard_map/ppermute | solution.py:501
  319.9 2.5 collective-permute-done.25
  323.1 1.6 collective-permute-done.5
  326.5 2.9 copy.43
  329.4 3.7 all-to-all-start.2
  333.1 5.7 %end.1 = (bf16[2,544,768]{2,1,0:T(8,128)(2,1)}, f32[1,768]{1,0:T(1,128)}, f32[1,768]{1,0:T(1,128)}) custom-call(f32[2,544,768]{2,1,0:T(8,128)} %get-tuple-element.75.gn_ref, bf16[2,544,768]{2,1,0:T(8,128)(2,1)} %bitcast.30, f32[2,544,768]{2,1,0:T(8,128)} %get-tuple-element.76.gh_ref, f32[1,768]{1,0:T(1,128)} %reshape.92.g1_ref), custom_call_target="tpu_custom_call" | custom-call | tf_op jit(solution)/shard_map/end/pallas_call | solution.py:429
  338.8 4.3 copy.45
  343.1 3.9 all-to-all-start.3
  352.2 1.6 collective-permute-start.17
  356.4 1.6 collective-permute-start.7
  358.0 10.4 %collective-permute-done.17 = bf16[4,96,768]{2,1,0:T(8,128)(2,1)S(1)} collective-permute-done((bf16[4,96,768]{2,1,0:T(8,128)(2,1)S(1)}, bf16[4,96,768]{2,1,0:T(8,128)(2,1)S(1)}, u32[]{:S(2)}, u32[]{:S(2)}) %collective-permute-start.17) | collective-permute-done | bytes 589856 | tf_op jit(solution)/shard_map/ppermute | solution.py:501
  370.9 10.2 %collective-permute-done.27 = bf16[4,96,768]{2,1,0:T(8,128)(2,1)S(1)} collective-permute-done((bf16[4,96,768]{2,1,0:T(8,128)(2,1)S(1)}, bf16[4,96,768]{2,1,0:T(8,128)(2,1)S(1)}, u32[]{:S(2)}, u32[]{:S(2)}) %collective-permute-start.27) | collective-permute-done | bytes 589856 | tf_op jit(solution)/shard_map/ppermute | solution.py:501
  383.5 9.4 %collective-permute-done.7 = bf16[4,96,768]{2,1,0:T(8,128)(2,1)S(1)} collective-permute-done((bf16[4,96,768]{2,1,0:T(8,128)(2,1)S(1)}, bf16[4,96,768]{2,1,0:T(8,128)(2,1)S(1)}, u32[]{:S(2)}, u32[]{:S(2)}) %collective-permute-start.7) | collective-permute-done | bytes 589856 | tf_op jit(solution)/shard_map/ppermute | solution.py:501
  397.7 1.7 constant_dynamic-update-slice_fusion.30
  399.4 1.7 constant_dynamic-update-slice_fusion.20
  403.1 20.7 %collective-permute-done.28 = bf16[8,96,768]{2,1,0:T(8,128)(2,1)S(1)} collective-permute-done((bf16[8,96,768]{2,1,0:T(8,128)(2,1)S(1)}, bf16[8,96,768]{2,1,0:T(8,128)(2,1)S(1)}, u32[]{:S(2)}, u32[]{:S(2)}) %collective-permute-start.28) | collective-permute-done | bytes 1179680 | tf_op jit(solution)/shard_map/ppermute | solution.py:501
  424.9 21.6 %collective-permute-done.8 = bf16[8,96,768]{2,1,0:T(8,128)(2,1)S(1)} collective-permute-done((bf16[8,96,768]{2,1,0:T(8,128)(2,1)S(1)}, bf16[8,96,768]{2,1,0:T(8,128)(2,1)S(1)}, u32[]{:S(2)}, u32[]{:S(2)}) %collective-permute-start.8) | collective-permute-done | bytes 1179680 | tf_op jit(solution)/shard_map/ppermute | solution.py:501
  447.8 40.5 %psum.7 = f32[1,9216]{1,0:T(1,128)S(1)} all-reduce(f32[1,9216]{1,0:T(1,128)S(1)} %constant_dynamic-update-slice_fusion), channel_id=1, replica_groups=mesh['dp'=16,'seq'=2] {'dp','seq'}, use_global_device_ids=true, to_apply=%region_0.1 | all-reduce | flops 9216 | bytes 73728 | tf_op jit(solution)/shard_map/psum | solution.py:572
  489.6 12.0 %widen_attn.1 = (f32[768,768]{1,0:T(8,128)}, f32[768,768]{1,0:T(8,128)}, f32[768,768]{1,0:T(8,128)}, f32[768,768]{1,0:T(8,128)}) custom-call(s32[2]{0:T(128)} %pad_add_fusion.at_ref, bf16[16,96,768]{2,1,0:T(8,128)(2,1)} %constant_dynamic-update-slice_fusion.18.mine_ref, bf16[16,96,768]{2,1,0:T(8,128)(2,1)} %collective-permute-done.9.other_ref), custom_call_target="tpu_custom_call" | custom-call | tf_op jit(solution)/shard_map/widen_attn/pallas_call | solution.py:486
  501.7 12.1 %widen_mlp.2 = (f32[3072,768]{1,0:T(8,128)}, f32[768,3072]{1,0:T(8,128)}) custom-call(s32[2]{0:T(128)} %pad_add_fusion.at_ref, bf16[16,96,768]{2,1,0:T(8,128)(2,1)} %constant_dynamic-update-slice_fusion.28.mine_ref, bf16[16,96,768]{2,1,0:T(8,128)(2,1)} %collective-permute-done.29.other_ref), custom_call_target="tpu_custom_call" | custom-call | tf_op jit(solution)/shard_map/widen_mlp/pallas_call | solution.py:453
  513.8 12.2 %widen_mlp.3 = (f32[3072,768]{1,0:T(8,128)}, f32[768,3072]{1,0:T(8,128)}) custom-call(s32[2]{0:T(128)} %pad_add_fusion.at_ref, bf16[16,96,768]{2,1,0:T(8,128)(2,1)} %copy-done.1, bf16[16,96,768]{2,1,0:T(8,128)(2,1)} %collective-permute-done.19.other_ref, f32[3072,768]{1,0:T(8,128)} %get-tuple-element.101.rest_0_, ...), custom_call_target="tpu_custom_call", output_to_operand_aliasing={{0}: (3, {}), {1}: (4, {})} | custom-call | tf_op jit(solution)/shard_map/widen_mlp/pallas_call | solution.py:453
  (192 shorter events, 48.1 us)
Async XLA Ops:
  0.7 8.5 %all-to-all-start = ((bf16[4,272,768]{2,1,0:T(8,128)(2,1)}), bf16[4,272,768]{2,1,0:T(8,128)(2,1)S(1)}, u32[]{:S(2)}, u32[]{:S(2)}) async-start(bf16[4,272,768]{2,1,0:T(8,128)(2,1)} %param.18), calls=%async_computation | async-start | bytes 3342336 | tf_op jit(solution)/shard_map/all_to_all | solution.py:535
  9.3 6.2 %all-to-all-start.1 = ((bf16[4,272,768]{2,1,0:T(8,128)(2,1)}), bf16[4,272,768]{2,1,0:T(8,128)(2,1)S(1)}, u32[]{:S(2)}, u32[]{:S(2)}) async-start(bf16[4,272,768]{2,1,0:T(8,128)(2,1)} %param.35), calls=%async_computation.1 | async-start | bytes 3342336 | tf_op jit(solution)/shard_map/all_to_all | solution.py:535
  117.5 66.2 %collective-permute-start.10 = (bf16[16,96,768]{2,1,0:T(8,128)(2,1)}, bf16[16,96,768]{2,1,0:T(8,128)(2,1)}, u32[]{:S(2)}, u32[]{:S(2)}) collective-permute-start(bf16[16,96,768]{2,1,0:T(8,128)(2,1)} %get-tuple-element.98), channel_id=1, source_target_pairs={{0,1},{1,0},{2,3},{3,2},{4,5},{5,4},{6,7},{7,6},{8,9},{9,8},{10,11... | collective-permute-start | bytes 7077896 | tf_op jit(solution)/shard_map/ppermute | solution.py:501
  117.7 72.7 %collective-permute-start.20 = (bf16[16,96,768]{2,1,0:T(8,128)(2,1)}, bf16[16,96,768]{2,1,0:T(8,128)(2,1)S(1)}, u32[]{:S(2)}, u32[]{:S(2)}) collective-permute-start(bf16[16,96,768]{2,1,0:T(8,128)(2,1)} %get-tuple-element.100), channel_id=1, source_target_pairs={{0,1},{1,0},{2,3},{3,2},{4,5},{5,4},{6,7},{7,6},{8,9},{9,8},{10,11... | collective-permute-start | bytes 7077896 | tf_op jit(solution)/shard_map/ppermute | solution.py:501
  164.3 17.1 %copy-start.15 = (bf16[16,48,768]{2,1,0:T(8,128)(2,1)S(1)}, bf16[16,48,768]{2,1,0:T(8,128)(2,1)}, u32[]{:S(2)}) copy-start(bf16[16,48,768]{2,1,0:T(8,128)(2,1)} %get-tuple-element.91) | copy-start | bytes 3538948
  183.5 9.2 %collective-permute-start = (bf16[16,96,768]{2,1,0:T(8,128)(2,1)S(1)}, bf16[16,96,768]{2,1,0:T(8,128)(2,1)S(1)}, u32[]{:S(2)}, u32[]{:S(2)}) collective-permute-start(bf16[16,96,768]{2,1,0:T(8,128)(2,1)S(1)} %broadcast_select_fusion), channel_id=1, source_target_pairs={{0,1},{1,0},{2,3},{3,2},{4,5},{5,4},{6,7},{7,6},{8,9},{9,8},{10,11... | collective-permute-start | bytes 7077896 | tf_op jit(solution)/shard_map/ppermute | solution.py:501
  187.3 29.8 %collective-permute-start.11 = (bf16[8,96,768]{2,1,0:T(8,128)(2,1)S(1)}, bf16[8,96,768]{2,1,0:T(8,128)(2,1)S(1)}, u32[]{:S(2)}, u32[]{:S(2)}) collective-permute-start(bf16[8,96,768]{2,1,0:T(8,128)(2,1)S(1)} %slice.208), channel_id=1, source_target_pairs={{0,2},{2,0},{4,6},{6,4},{8,10},{10,8},{12,14},{14,12},{16,18},{18,... | collective-permute-start | bytes 3538952 | tf_op jit(solution)/shard_map/ppermute | solution.py:501
  191.1 51.2 %collective-permute-start.21 = (bf16[8,96,768]{2,1,0:T(8,128)(2,1)S(1)}, bf16[8,96,768]{2,1,0:T(8,128)(2,1)S(1)}, u32[]{:S(2)}, u32[]{:S(2)}) collective-permute-start(bf16[8,96,768]{2,1,0:T(8,128)(2,1)S(1)} %slice.216), channel_id=1, source_target_pairs={{0,2},{2,0},{4,6},{6,4},{8,10},{10,8},{12,14},{14,12},{16,18},{18,... | collective-permute-start | bytes 3538952 | tf_op jit(solution)/shard_map/ppermute | solution.py:501
  193.4 73.8 %collective-permute-start.1 = (bf16[8,96,768]{2,1,0:T(8,128)(2,1)S(1)}, bf16[8,96,768]{2,1,0:T(8,128)(2,1)S(1)}, u32[]{:S(2)}, u32[]{:S(2)}) collective-permute-start(bf16[8,96,768]{2,1,0:T(8,128)(2,1)S(1)} %slice.195), channel_id=1, source_target_pairs={{0,2},{2,0},{4,6},{6,4},{8,10},{10,8},{12,14},{14,12},{16,18},{18,... | collective-permute-start | bytes 3538952 | tf_op jit(solution)/shard_map/ppermute | solution.py:501
  217.2 51.9 %collective-permute-start.12 = (bf16[4,96,768]{2,1,0:T(8,128)(2,1)S(1)}, bf16[4,96,768]{2,1,0:T(8,128)(2,1)S(1)}, u32[]{:S(2)}, u32[]{:S(2)}) collective-permute-start(bf16[4,96,768]{2,1,0:T(8,128)(2,1)S(1)} %slice.210), channel_id=1, source_target_pairs={{0,4},{2,6},{4,0},{6,2},{8,12},{10,14},{12,8},{14,10},{16,20},{18,... | collective-permute-start | bytes 1769480 | tf_op jit(solution)/shard_map/ppermute | solution.py:501
  242.5 28.4 %collective-permute-start.22 = (bf16[4,96,768]{2,1,0:T(8,128)(2,1)S(1)}, bf16[4,96,768]{2,1,0:T(8,128)(2,1)S(1)}, u32[]{:S(2)}, u32[]{:S(2)}) collective-permute-start(bf16[4,96,768]{2,1,0:T(8,128)(2,1)S(1)} %slice.218), channel_id=1, source_target_pairs={{0,4},{2,6},{4,0},{6,2},{8,12},{10,14},{12,8},{14,10},{16,20},{18,... | collective-permute-start | bytes 1769480 | tf_op jit(solution)/shard_map/ppermute | solution.py:501
  267.3 14.9 %collective-permute-start.2 = (bf16[4,96,768]{2,1,0:T(8,128)(2,1)S(1)}, bf16[4,96,768]{2,1,0:T(8,128)(2,1)S(1)}, u32[]{:S(2)}, u32[]{:S(2)}) collective-permute-start(bf16[4,96,768]{2,1,0:T(8,128)(2,1)S(1)} %slice.197), channel_id=1, source_target_pairs={{0,4},{2,6},{4,0},{6,2},{8,12},{10,14},{12,8},{14,10},{16,20},{18,... | collective-permute-start | bytes 1769480 | tf_op jit(solution)/shard_map/ppermute | solution.py:501
  269.2 14.7 %collective-permute-start.13 = (bf16[2,96,768]{2,1,0:T(8,128)(2,1)S(1)}, bf16[2,96,768]{2,1,0:T(8,128)(2,1)S(1)}, u32[]{:S(2)}, u32[]{:S(2)}) collective-permute-start(bf16[2,96,768]{2,1,0:T(8,128)(2,1)S(1)} %slice.212), channel_id=1, source_target_pairs={{0,8},{2,10},{4,12},{6,14},{8,0},{10,2},{12,4},{14,6},{16,24},{18,... | collective-permute-start | bytes 884744 | tf_op jit(solution)/shard_map/ppermute | solution.py:501
  271.0 15.7 %collective-permute-start.23 = (bf16[2,96,768]{2,1,0:T(8,128)(2,1)S(1)}, bf16[2,96,768]{2,1,0:T(8,128)(2,1)S(1)}, u32[]{:S(2)}, u32[]{:S(2)}) collective-permute-start(bf16[2,96,768]{2,1,0:T(8,128)(2,1)S(1)} %slice.220), channel_id=1, source_target_pairs={{0,8},{2,10},{4,12},{6,14},{8,0},{10,2},{12,4},{14,6},{16,24},{18,... | collective-permute-start | bytes 884744 | tf_op jit(solution)/shard_map/ppermute | solution.py:501
  282.3 13.1 %collective-permute-start.3 = (bf16[2,96,768]{2,1,0:T(8,128)(2,1)S(1)}, bf16[2,96,768]{2,1,0:T(8,128)(2,1)S(1)}, u32[]{:S(2)}, u32[]{:S(2)}) collective-permute-start(bf16[2,96,768]{2,1,0:T(8,128)(2,1)S(1)} %slice.199), channel_id=1, source_target_pairs={{0,8},{2,10},{4,12},{6,14},{8,0},{10,2},{12,4},{14,6},{16,24},{18,... | collective-permute-start | bytes 884744 | tf_op jit(solution)/shard_map/ppermute | solution.py:501
  284.0 12.9 %collective-permute-start.14 = (bf16[1,96,768]{2,1,0:T(8,128)(2,1)S(1)}, bf16[1,96,768]{2,1,0:T(8,128)(2,1)S(1)}, u32[]{:S(2)}, u32[]{:S(2)}) collective-permute-start(bf16[1,96,768]{2,1,0:T(8,128)(2,1)S(1)} %slice.214), channel_id=1, source_target_pairs={{0,16},{2,18},{4,20},{6,22},{8,24},{10,26},{12,28},{14,30},{16,0},... | collective-permute-start | bytes 442376 | tf_op jit(solution)/shard_map/ppermute | solution.py:501
  286.7 39.8 %copy-start.14 = (bf16[1088,768]{1,0:T(8,128)(2,1)S(1)}, bf16[1088,768]{1,0:T(8,128)(2,1)}, u32[]{:S(2)}) copy-start(bf16[1088,768]{1,0:T(8,128)(2,1)} %get-tuple-element.65) | copy-start | bytes 5013508
  286.7 21.3 %collective-permute-start.24 = (bf16[1,96,768]{2,1,0:T(8,128)(2,1)S(1)}, bf16[1,96,768]{2,1,0:T(8,128)(2,1)S(1)}, u32[]{:S(2)}, u32[]{:S(2)}) collective-permute-start(bf16[1,96,768]{2,1,0:T(8,128)(2,1)S(1)} %slice.222), channel_id=1, source_target_pairs={{0,16},{2,18},{4,20},{6,22},{8,24},{10,26},{12,28},{14,30},{16,0},... | collective-permute-start | bytes 442376 | tf_op jit(solution)/shard_map/ppermute | solution.py:501
  295.5 15.7 %collective-permute-start.4 = (bf16[1,96,768]{2,1,0:T(8,128)(2,1)S(1)}, bf16[1,96,768]{2,1,0:T(8,128)(2,1)S(1)}, u32[]{:S(2)}, u32[]{:S(2)}) collective-permute-start(bf16[1,96,768]{2,1,0:T(8,128)(2,1)S(1)} %slice.201), channel_id=1, source_target_pairs={{0,16},{2,18},{4,20},{6,22},{8,24},{10,26},{12,28},{14,30},{16,0},... | collective-permute-start | bytes 442376 | tf_op jit(solution)/shard_map/ppermute | solution.py:501
  297.6 29.0 %copy-start.8 = (bf16[1,96,768]{2,1,0:T(8,128)(2,1)}, bf16[1,96,768]{2,1,0:T(8,128)(2,1)S(1)}, u32[]{:S(2)}) copy-start(bf16[1,96,768]{2,1,0:T(8,128)(2,1)S(1)} %get-tuple-element.116) | copy-start | bytes 442372
  297.6 21.5 %collective-permute-start.15 = (bf16[1,96,768]{2,1,0:T(8,128)(2,1)S(1)}, bf16[1,96,768]{2,1,0:T(8,128)(2,1)S(1)}, u32[]{:S(2)}, u32[]{:S(2)}) collective-permute-start(bf16[1,96,768]{2,1,0:T(8,128)(2,1)S(1)} %get-tuple-element.116), channel_id=1, source_target_pairs={{0,16},{2,18},{4,20},{6,22},{8,24},{10,26},{12,28},{14,30},{16,0},... | collective-permute-start | bytes 442376 | tf_op jit(solution)/shard_map/ppermute | solution.py:501
  308.7 17.8 %copy-start.10 = (bf16[1,96,768]{2,1,0:T(8,128)(2,1)}, bf16[1,96,768]{2,1,0:T(8,128)(2,1)S(1)}, u32[]{:S(2)}) copy-start(bf16[1,96,768]{2,1,0:T(8,128)(2,1)S(1)} %get-tuple-element.114) | copy-start | bytes 442372
  308.8 13.6 %collective-permute-start.25 = (bf16[1,96,768]{2,1,0:T(8,128)(2,1)S(1)}, bf16[1,96,768]{2,1,0:T(8,128)(2,1)S(1)}, u32[]{:S(2)}, u32[]{:S(2)}) collective-permute-start(bf16[1,96,768]{2,1,0:T(8,128)(2,1)S(1)} %get-tuple-element.114), channel_id=1, source_target_pairs={{0,16},{2,18},{4,20},{6,22},{8,24},{10,26},{12,28},{14,30},{16,0},... | collective-permute-start | bytes 442376 | tf_op jit(solution)/shard_map/ppermute | solution.py:501
  311.9 12.7 %collective-permute-start.5 = (bf16[1,96,768]{2,1,0:T(8,128)(2,1)S(1)}, bf16[1,96,768]{2,1,0:T(8,128)(2,1)S(1)}, u32[]{:S(2)}, u32[]{:S(2)}) collective-permute-start(bf16[1,96,768]{2,1,0:T(8,128)(2,1)S(1)} %get-tuple-element.118), channel_id=1, source_target_pairs={{0,16},{2,18},{4,20},{6,22},{8,24},{10,26},{12,28},{14,30},{16,0},... | collective-permute-start | bytes 442376 | tf_op jit(solution)/shard_map/ppermute | solution.py:501
  319.9 31.1 %collective-permute-start.16 = (bf16[2,96,768]{2,1,0:T(8,128)(2,1)}, bf16[2,96,768]{2,1,0:T(8,128)(2,1)}, u32[]{:S(2)}, u32[]{:S(2)}) collective-permute-start(bf16[2,96,768]{2,1,0:T(8,128)(2,1)} %pad_maximum_fusion.7), channel_id=1, source_target_pairs={{0,8},{2,10},{4,12},{6,14},{8,0},{10,2},{12,4},{14,6},{16,24},{18,... | collective-permute-start | bytes 884744 | tf_op jit(solution)/shard_map/ppermute | solution.py:501
  323.1 30.7 %collective-permute-start.26 = (bf16[2,96,768]{2,1,0:T(8,128)(2,1)}, bf16[2,96,768]{2,1,0:T(8,128)(2,1)}, u32[]{:S(2)}, u32[]{:S(2)}) collective-permute-start(bf16[2,96,768]{2,1,0:T(8,128)(2,1)} %pad_maximum_fusion.8), channel_id=1, source_target_pairs={{0,8},{2,10},{4,12},{6,14},{8,0},{10,2},{12,4},{14,6},{16,24},{18,... | collective-permute-start | bytes 884744 | tf_op jit(solution)/shard_map/ppermute | solution.py:501
  326.1 29.3 %collective-permute-start.6 = (bf16[2,96,768]{2,1,0:T(8,128)(2,1)}, bf16[2,96,768]{2,1,0:T(8,128)(2,1)}, u32[]{:S(2)}, u32[]{:S(2)}) collective-permute-start(bf16[2,96,768]{2,1,0:T(8,128)(2,1)} %pad_maximum_fusion.6), channel_id=1, source_target_pairs={{0,8},{2,10},{4,12},{6,14},{8,0},{10,2},{12,4},{14,6},{16,24},{18,... | collective-permute-start | bytes 884744 | tf_op jit(solution)/shard_map/ppermute | solution.py:501
  329.4 13.7 %all-to-all-start.2 = ((bf16[2,544,768]{2,0,1:T(2,128)(2,1)}), bf16[2,544,768]{2,0,1:T(2,128)(2,1)S(1)}, u32[]{:S(2)}, u32[]{:S(2)}) async-start(bf16[2,544,768]{2,0,1:T(2,128)(2,1)} %copy.43), calls=%async_computation.2 | async-start | bytes 3342336 | tf_op jit(solution)/shard_map/all_to_all | solution.py:536
  343.1 6.4 %all-to-all-start.3 = ((bf16[2,544,768]{2,0,1:T(2,128)(2,1)}), bf16[2,544,768]{2,0,1:T(2,128)(2,1)S(1)}, u32[]{:S(2)}, u32[]{:S(2)}) async-start(bf16[2,544,768]{2,0,1:T(2,128)(2,1)} %copy.45), calls=%async_computation.3 | async-start | bytes 3342336 | tf_op jit(solution)/shard_map/all_to_all | solution.py:536
  352.2 16.2 %collective-permute-start.17 = (bf16[4,96,768]{2,1,0:T(8,128)(2,1)S(1)}, bf16[4,96,768]{2,1,0:T(8,128)(2,1)S(1)}, u32[]{:S(2)}, u32[]{:S(2)}) collective-permute-start(bf16[4,96,768]{2,1,0:T(8,128)(2,1)S(1)} %pad_maximum_fusion.4), channel_id=1, source_target_pairs={{0,4},{2,6},{4,0},{6,2},{8,12},{10,14},{12,8},{14,10},{16,20},{18,... | collective-permute-start | bytes 1769480 | tf_op jit(solution)/shard_map/ppermute | solution.py:501
  354.8 26.3 %collective-permute-start.27 = (bf16[4,96,768]{2,1,0:T(8,128)(2,1)S(1)}, bf16[4,96,768]{2,1,0:T(8,128)(2,1)S(1)}, u32[]{:S(2)}, u32[]{:S(2)}) collective-permute-start(bf16[4,96,768]{2,1,0:T(8,128)(2,1)S(1)} %pad_maximum_fusion.5), channel_id=1, source_target_pairs={{0,4},{2,6},{4,0},{6,2},{8,12},{10,14},{12,8},{14,10},{16,20},{18,... | collective-permute-start | bytes 1769480 | tf_op jit(solution)/shard_map/ppermute | solution.py:501
  356.4 36.5 %collective-permute-start.7 = (bf16[4,96,768]{2,1,0:T(8,128)(2,1)S(1)}, bf16[4,96,768]{2,1,0:T(8,128)(2,1)S(1)}, u32[]{:S(2)}, u32[]{:S(2)}) collective-permute-start(bf16[4,96,768]{2,1,0:T(8,128)(2,1)S(1)} %pad_maximum_fusion.3), channel_id=1, source_target_pairs={{0,4},{2,6},{4,0},{6,2},{8,12},{10,14},{12,8},{14,10},{16,20},{18,... | collective-permute-start | bytes 1769480 | tf_op jit(solution)/shard_map/ppermute | solution.py:501
  369.5 33.3 %collective-permute-start.18 = (bf16[8,96,768]{2,1,0:T(8,128)(2,1)S(1)}, bf16[8,96,768]{2,1,0:T(8,128)(2,1)S(1)}, u32[]{:S(2)}, u32[]{:S(2)}) collective-permute-start(bf16[8,96,768]{2,1,0:T(8,128)(2,1)S(1)} %pad_maximum_fusion.1), channel_id=1, source_target_pairs={{0,2},{2,0},{4,6},{6,4},{8,10},{10,8},{12,14},{14,12},{16,18},{18,... | collective-permute-start | bytes 3538952 | tf_op jit(solution)/shard_map/ppermute | solution.py:501
  382.2 41.6 %collective-permute-start.28 = (bf16[8,96,768]{2,1,0:T(8,128)(2,1)S(1)}, bf16[8,96,768]{2,1,0:T(8,128)(2,1)S(1)}, u32[]{:S(2)}, u32[]{:S(2)}) collective-permute-start(bf16[8,96,768]{2,1,0:T(8,128)(2,1)S(1)} %pad_maximum_fusion.2), channel_id=1, source_target_pairs={{0,2},{2,0},{4,6},{6,4},{8,10},{10,8},{12,14},{14,12},{16,18},{18,... | collective-permute-start | bytes 3538952 | tf_op jit(solution)/shard_map/ppermute | solution.py:501
  394.0 52.5 %collective-permute-start.8 = (bf16[8,96,768]{2,1,0:T(8,128)(2,1)S(1)}, bf16[8,96,768]{2,1,0:T(8,128)(2,1)S(1)}, u32[]{:S(2)}, u32[]{:S(2)}) collective-permute-start(bf16[8,96,768]{2,1,0:T(8,128)(2,1)S(1)} %pad_maximum_fusion), channel_id=1, source_target_pairs={{0,2},{2,0},{4,6},{6,4},{8,10},{10,8},{12,14},{14,12},{16,18},{18,... | collective-permute-start | bytes 3538952 | tf_op jit(solution)/shard_map/ppermute | solution.py:501
  402.9 44.7 %copy-start.1 = (bf16[16,96,768]{2,1,0:T(8,128)(2,1)}, bf16[16,96,768]{2,1,0:T(8,128)(2,1)S(1)}, u32[]{:S(2)}) copy-start(bf16[16,96,768]{2,1,0:T(8,128)(2,1)S(1)} %constant_dynamic-update-slice_fusion.23.mine_ref) | copy-start | bytes 7077892
  402.9 44.7 %copy-start.34 = (f32[1,768]{1,0:T(1,128)S(1)}, f32[1,768]{1,0:T(1,128)}, u32[]{:S(2)}) copy-start(f32[1,768]{1,0:T(1,128)} %get-tuple-element.80) | copy-start | bytes 9220
  402.9 44.7 %copy-start.35 = (f32[1,768]{1,0:T(1,128)S(1)}, f32[1,768]{1,0:T(1,128)}, u32[]{:S(2)}) copy-start(f32[1,768]{1,0:T(1,128)} %get-tuple-element.81) | copy-start | bytes 9220
  402.9 44.7 %copy-start.36 = (f32[1,768]{1,0:T(1,128)S(1)}, f32[1,768]{1,0:T(1,128)}, u32[]{:S(2)}) copy-start(f32[1,768]{1,0:T(1,128)} %get-tuple-element.82) | copy-start | bytes 9220
  403.0 44.7 %copy-start.31 = (f32[1,768]{1,0:T(1,128)S(1)}, f32[1,768]{1,0:T(1,128)}, u32[]{:S(2)}) copy-start(f32[1,768]{1,0:T(1,128)} %get-tuple-element.83) | copy-start | bytes 9220
  403.0 44.7 %copy-start.30 = (f32[1,768]{1,0:T(1,128)S(1)}, f32[1,768]{1,0:T(1,128)}, u32[]{:S(2)}) copy-start(f32[1,768]{1,0:T(1,128)} %get-tuple-element.84) | copy-start | bytes 9220
  403.0 44.7 %copy-start.29 = (f32[1,768]{1,0:T(1,128)S(1)}, f32[1,768]{1,0:T(1,128)}, u32[]{:S(2)}) copy-start(f32[1,768]{1,0:T(1,128)} %get-tuple-element.85) | copy-start | bytes 9220
  403.0 44.8 %copy-start.28 = (f32[1,768]{1,0:T(1,128)S(1)}, f32[1,768]{1,0:T(1,128)}, u32[]{:S(2)}) copy-start(f32[1,768]{1,0:T(1,128)} %get-tuple-element.86) | copy-start | bytes 9220
  403.0 44.8 %copy-start.18 = (f32[1,1536]{1,0:T(1,128)S(1)}, f32[1,1536]{1,0:T(1,128)}, u32[]{:S(2)}) copy-start(f32[1,1536]{1,0:T(1,128)} %get-tuple-element.87) | copy-start | bytes 18436
  403.0 44.8 %copy-start.19 = (f32[1,1536]{1,0:T(1,128)S(1)}, f32[1,1536]{1,0:T(1,128)}, u32[]{:S(2)}) copy-start(f32[1,1536]{1,0:T(1,128)} %get-tuple-element.88) | copy-start | bytes 18436
  403.0 110.8 %collective-permute-start.19 = (bf16[16,96,768]{2,1,0:T(8,128)(2,1)S(1)}, bf16[16,96,768]{2,1,0:T(8,128)(2,1)}, u32[]{:S(2)}, u32[]{:S(2)}) collective-permute-start(bf16[16,96,768]{2,1,0:T(8,128)(2,1)S(1)} %constant_dynamic-update-slice_fusion.23.mine_ref), channel_id=1, source_target_pairs={{0,1},{1,0},{2,3},{3,2},{4,5},{5,4},{6,7},{7,6},{8,9},{9,8},{10,11... | collective-permute-start | bytes 7077896 | tf_op jit(solution)/shard_map/ppermute | solution.py:501
  424.9 76.8 %collective-permute-start.29 = (bf16[16,96,768]{2,1,0:T(8,128)(2,1)}, bf16[16,96,768]{2,1,0:T(8,128)(2,1)}, u32[]{:S(2)}, u32[]{:S(2)}) collective-permute-start(bf16[16,96,768]{2,1,0:T(8,128)(2,1)} %constant_dynamic-update-slice_fusion.28.mine_ref), channel_id=1, source_target_pairs={{0,1},{1,0},{2,3},{3,2},{4,5},{5,4},{6,7},{7,6},{8,9},{9,8},{10,11... | collective-permute-start | bytes 7077896 | tf_op jit(solution)/shard_map/ppermute | solution.py:501
  447.6 42.1 %collective-permute-start.9 = (bf16[16,96,768]{2,1,0:T(8,128)(2,1)}, bf16[16,96,768]{2,1,0:T(8,128)(2,1)}, u32[]{:S(2)}, u32[]{:S(2)}) collective-permute-start(bf16[16,96,768]{2,1,0:T(8,128)(2,1)} %constant_dynamic-update-slice_fusion.18.mine_ref), channel_id=1, source_target_pairs={{0,1},{1,0},{2,3},{3,2},{4,5},{5,4},{6,7},{7,6},{8,9},{9,8},{10,11... | collective-permute-start | bytes 7077896 | tf_op jit(solution)/shard_map/ppermute | solution.py:501
  (24 other events, 120.6 us)

commit v2 on v1

v2 whole, which is shorter than its diff:
```python
import functools

import jax
import jax.numpy as jnp
from jax import lax
from jax.experimental import pallas as pl
from jax.experimental.pallas import tpu as pltpu
from jax.sharding import PartitionSpec as P

F32, BF16 = jnp.float32, jnp.bfloat16
D, HEADS, HEAD_DIM, FF, SLOTS = 768, 12, 64, 3072, 544
X_LAST, Y_LAST = (8, 4, 2, 1), (8, 4, 1, 2)
STRIPS = 2
ROWS = STRIPS * SLOTS
PAIRS = HEADS // 2
EPS = 1e-06
MASKED = -1e30
GROUPS = 3
GROUP_PAIRS = PAIRS // GROUPS
GCOLS = D // GROUPS
HALF = SLOTS // 2
FSTEP = 768
PIECE_STEPS = 2
FCALL = FSTEP * PIECE_STEPS
GAIN_1, SHIFT_1, B_QUERY, B_VALUE, B_OUT, GAIN_2, SHIFT_2, B_DOWN, B_UP = range(9)
VECTORS = B_UP + FF // D
SMALL = 16


def params(mib):
    return pltpu.CompilerParams(vmem_limit_bytes=mib << 20, dimension_semantics=("arbitrary",))


def far(value):
    return pltpu.with_memory_space_constraint(value, pltpu.HBM)


def cost(micros):
    return pl.CostEstimate(flops=int(micros * 1.15e10), bytes_accessed=0, transcendentals=0)


def call(kernel, operands, in_specs, after, prefetch=0, micros=10, mib=16, **kw):
    after = [v for v in after if v is not None]
    count = len(after)
    scalars = operands[:prefetch]

    def body(*refs):
        n = prefetch + len(in_specs)
        kernel(*refs[:n], *refs[n + count :])

    spec = pltpu.PrefetchScalarGridSpec(
        num_scalar_prefetch=prefetch,
        grid=kw.pop("grid"),
        in_specs=list(in_specs) + [pl.BlockSpec(memory_space=pl.ANY)] * count,
        out_specs=kw.pop("out_specs"),
        scratch_shapes=kw.pop("scratch_shapes", []),
    )
    return pl.pallas_call(body, grid_spec=spec, compiler_params=params(mib), cost_estimate=cost(micros), **kw)(
        *operands, *after
    )


def dot(a, b):
    return lax.dot_general(a, b, (((1,), (0,)), ((), ())), preferred_element_type=F32)


def dot_bt(a, b):
    return lax.dot_general(a, b, (((1,), (1,)), ((), ())), preferred_element_type=F32)


def dot_at(a, b):
    return lax.dot_general(a, b, (((0,), (0,)), ((), ())), preferred_element_type=F32)


def norm_parts(values):
    centre = jnp.mean(values, axis=-1, keepdims=True)
    centred = values - centre
    spread = jnp.mean(centred * centred, axis=-1, keepdims=True)
    rstd = lax.rsqrt(spread + EPS)
    return centred * rstd, rstd


def gelu_parts(u):
    t = 1.0 / (1.0 + (0.3275911 * 0.7071067811865476) * jnp.abs(u))
    e = jnp.exp(-0.5 * u * u)
    poly = 0.5 * 1.061405429 * t + 0.5 * -1.453152027
    poly = poly * t + 0.5 * 1.421413741
    poly = poly * t + 0.5 * -0.284496736
    poly = poly * t + 0.5 * 0.254829592
    tail = poly * t * e
    cdf = jnp.where(u >= 0, 1.0 - tail, tail)
    return u * cdf, cdf + u * (e * 0.3989422804014327)


def split3(x):
    hi = x.astype(BF16).astype(F32)
    rest = x - hi
    mid = rest.astype(BF16).astype(F32)
    return hi, mid, rest - mid


def lane_iota():
    return lax.broadcasted_iota(jnp.int32, (SLOTS, 128), 1)


def half_mask(lane, h):
    return jnp.where((lane >= 64 * h) & (lane < 64 * h + 64), 1.0, 0.0).astype(BF16)


def key_extra(lane, length, h):
    first = 64 * (1 - h)
    row = lax.broadcasted_iota(jnp.int32, (SLOTS, 128), 0)
    bias = jnp.where(row < length, 0.0, MASKED)
    ones = (lane > first) & (lane < first + 4)
    return jnp.where(lane == first, bias, jnp.where(ones, 1.0, 0.0)).astype(BF16)


def pieces_extra(lane, column, h, lead):
    first = 64 * (1 - h)
    hi, mid, low = split3(column)
    out = jnp.where(lane == first + 3, low, jnp.where(lane == first, lead, 0.0))
    out = jnp.where(lane == first + 2, mid, out)
    return jnp.where(lane == first + 1, hi, out).astype(BF16)


def row_of(ref, i):
    return ref[i : i + 1]


def attend_kernel(
    at_ref, len_ref, own_ref, got_ref, own_cot_ref, got_cot_ref, vec_ref, wq_ref, wk_ref, wv_ref, wo_ref,
    n1_ref, qa_ref, k_ref, v_ref, ctx_ref, hid_ref, n2_ref, x_ref, cot_ref, q_scr,
):
    core = at_ref[0]
    own_rows = pl.ds(pl.multiple_of(core * HALF, 16), HALF)
    got_rows = pl.ds(pl.multiple_of((1 - core) * HALF, 16), HALF)
    x_ref[0, own_rows], x_ref[0, got_rows] = own_ref[0], got_ref[0]
    cot_ref[0, own_rows], cot_ref[0, got_rows] = own_cot_ref[0], got_cot_ref[0]
    x = x_ref[0].astype(F32)
    scaled, _ = norm_parts(x)
    n1 = (scaled * row_of(vec_ref, GAIN_1) + row_of(vec_ref, SHIFT_1)).astype(BF16)
    n1_ref[0] = n1
    queries = (dot(n1, wq_ref[...]) + row_of(vec_ref, B_QUERY)).astype(BF16)
    q_scr[...] = (queries.astype(F32) * (HEAD_DIM**-0.5)).astype(BF16)
    k_ref[0] = dot(n1, wk_ref[...]).astype(BF16)
    v_ref[0] = (dot(n1, wv_ref[...]) + row_of(vec_ref, B_VALUE)).astype(BF16)
    length = len_ref[STRIPS * core + pl.program_id(0)]
    lane = lane_iota()
    own = [half_mask(lane, h) for h in (0, 1)]
    kx = [key_extra(lane, length, h) for h in (0, 1)]

    def pair(p, _):
        cols = pl.ds(pl.multiple_of(p * 128, 128), 128)
        qp, kp, vp = q_scr[:, cols], k_ref[0, :, cols], v_ref[0, :, cols]
        ctx = None
        inverses = []
        for h in (0, 1):
            first = 64 * (1 - h)
            query = qp * own[h] + jnp.where(lane == first, 1.0, 0.0).astype(BF16)
            scores = dot_bt(query, kp * own[h] + kx[h])
            top = jnp.max(scores, axis=-1, keepdims=True)
            weights = jnp.exp(scores - top)
            total = jnp.sum(weights, axis=-1, keepdims=True)
            part = dot(weights.astype(BF16), vp * own[h])
            ctx = part if ctx is None else ctx + part
            inverses.append(1.0 / total)
            extra = pieces_extra(lane, -(top + jnp.log(total)), h, 1.0)
            qa_ref[0, :, pl.ds(pl.multiple_of(p * 256 + 128 * h, 128), 128)] = qp * own[h] + extra
        scale = jnp.where(lane < 64, inverses[0], inverses[1])
        ctx_ref[0, :, cols] = (ctx * scale).astype(BF16)
        return 0

    lax.fori_loop(0, PAIRS, pair, 0)
    hidden = x + dot(ctx_ref[0], wo_ref[...]) + row_of(vec_ref, B_OUT)
    hid_ref[0] = hidden
    scaled, _ = norm_parts(hidden)
    n2_ref[0] = (scaled * row_of(vec_ref, GAIN_2) + row_of(vec_ref, SHIFT_2)).astype(BF16)


def whole(shape):
    return pl.BlockSpec(shape, lambda *_: (0,) * len(shape), pipeline_mode=pl.Buffered(1))


def strip_block(cols):
    return pl.BlockSpec((1, SLOTS, cols), lambda s, *_: (s, 0, 0))


def strips_of(cols, dtype):
    return jax.ShapeDtypeStruct((STRIPS, SLOTS, cols), dtype)


def attend(at, lengths, patches, got, cotangent, got_cot, vec, wq, wk, wv, wo):
    mat = whole((D, D))
    mine = pl.BlockSpec((1, HALF, D), lambda s, at_ref, *_: (STRIPS * at_ref[0] + s, 0, 0))
    half = pl.BlockSpec((1, HALF, D), lambda s, *_: (s, 0, 0))
    return call(
        attend_kernel,
        [at, lengths, far(patches), got, far(cotangent), got_cot, vec, far(wq), far(wk), far(wv), far(wo)],
        [mine, half, mine, half, whole((VECTORS, D)), mat, mat, mat, mat],
        [],
        prefetch=2,
        grid=(STRIPS,),
        out_specs=[strip_block(D), strip_block(2 * D)] + [strip_block(D)] * 7,
        scratch_shapes=[pltpu.VMEM((SLOTS, D), BF16)],
        out_shape=[pltpu.HBM((STRIPS, SLOTS, D), BF16), pltpu.HBM((STRIPS, SLOTS, 2 * D), BF16)]
        + [pltpu.HBM((STRIPS, SLOTS, D), BF16)] * 3
        + [pltpu.HBM((STRIPS, SLOTS, D), F32), pltpu.VMEM((STRIPS, SLOTS, D), BF16)]
        + [pltpu.HBM((STRIPS, SLOTS, D), BF16), pltpu.VMEM((STRIPS, SLOTS, D), BF16)],
        micros=28,
        mib=30,
        name="attend",
    )


def mlp_kernel(
    base, steps, which, at_ref, n2_ref, cot_ref, up_ref, dn_ref, vec_ref, acc_in_ref, *rest
):
    first, last = base == 0, (base + steps) * FSTEP == FF
    into = base % PIECE_STEPS
    gn_in_ref, rest = (None, rest) if first else (rest[0], rest[1:])
    rest = rest[2:] if into else rest
    keep_ref, send_ref, gn_ref, gbup_ref = rest[:4]
    acc_ref, outs, (a_scr, g_scr) = rest[4], rest[5:-2], rest[-2:]
    step = pl.program_id(0)

    @pl.when(step == 0)
    def _():
        if first:
            acc_ref[...] = acc_in_ref[...] + row_of(vec_ref, B_DOWN)
            gn_ref[...] = jnp.zeros_like(gn_ref)

    up, down = up_ref[...], dn_ref[...]
    bias = vec_ref[pl.ds(B_UP + base + step, 1)]
    sums = None
    for r in range(0, ROWS, SLOTS):
        rows = slice(r, r + SLOTS)
        u = dot(n2_ref[rows], up) + bias
        grad_active = dot_bt(cot_ref[rows], down)
        active, slope = gelu_parts(u)
        active = active.astype(BF16)
        grad_upper = (grad_active * slope).astype(BF16)
        a_scr[rows] = active
        g_scr[rows] = grad_upper
        acc_ref[rows] += dot(active, down)
        gn_ref[rows] += dot_bt(grad_upper, up)
        part = jnp.sum(grad_upper.astype(F32), axis=0, keepdims=True)
        sums = part if sums is None else sums + part
    gbup_ref[0] = sums
    grad_down = dot_at(a_scr[...], cot_ref[...]).astype(BF16)
    grad_up = dot_at(n2_ref[...], g_scr[...]).astype(BF16)
    core, place = at_ref[0], at_ref[which]
    chunk, rows_up = FCALL // 16, D // 16
    per_step = FSTEP // chunk
    part = into + step

    def put(down_ref, up_out_ref):
        for i in range(per_step):
            down_ref[(part * per_step + i) ^ place] = grad_down[i * chunk : (i + 1) * chunk]
        for i in range(16):
            rows = pl.ds(pl.multiple_of(part * rows_up, 16), rows_up)
            up_out_ref[i ^ place, rows] = grad_up[i * rows_up : (i + 1) * rows_up]

    @pl.when(core == 0)
    def _():
        put(keep_ref, send_ref)

    @pl.when(core == 1)
    def _():
        put(send_ref, keep_ref)

    if last:
        @pl.when(step == steps - 1)
        def _():
            for s in range(STRIPS):
                for ref, c in zip(outs, (core, 1 - core)):
                    rows = pl.ds(pl.multiple_of(SLOTS * s + HALF * c, 16), HALF)
                    ref[s] = acc_ref[rows].astype(BF16)


def mlp(base, steps, which, at, n2, cot, w_up, w_down, vec, acc, gn, piece, after):
    first, last = base == 0, (base + steps) * FSTEP == FF
    shape = (16, FCALL // 16, D)
    rows, near = whole((ROWS, D)), pl.BlockSpec(memory_space=pltpu.VMEM)
    in_specs = [
        near, near,
        pl.BlockSpec((D, FSTEP), lambda s, *_: (0, base + s)),
        pl.BlockSpec((FSTEP, D), lambda s, *_: (base + s, 0)),
        whole((VECTORS, D)), rows if first else near,
    ]
    operands = [at, n2, cot, far(w_up), far(w_down), vec, far(acc) if first else acc]
    aliases = {}
    if not first:
        in_specs.append(near)
        operands.append(gn)
        aliases = {6: 4, 7: 2}
    if piece:
        in_specs += [near, near]
        aliases |= {len(operands): 0, len(operands) + 1: 1}
        operands += piece
    kept = pltpu.VMEM(shape, BF16)
    halves = [jax.ShapeDtypeStruct((STRIPS, HALF, D), BF16)] * 2
    return call(
        functools.partial(mlp_kernel, base, steps, which), operands, in_specs, after,
        prefetch=1,
        grid=(steps,),
        out_specs=[near, near, near, pl.BlockSpec((1, 1, FSTEP), lambda s, *_: (s, 0, 0)), near]
        + ([whole((STRIPS, HALF, D))] * 2 if last else []),
        scratch_shapes=[pltpu.VMEM((ROWS, FSTEP), BF16)] * 2,
        out_shape=[kept, kept, pltpu.VMEM((ROWS, D), F32), jax.ShapeDtypeStruct((steps, 1, FSTEP), F32),
                   pltpu.VMEM((ROWS, D), F32)] + (halves if last else []),
        input_output_aliases=aliases,
        micros=12 * steps,
        mib=26,
        name="mlp",
    )


def mid_kernel(
    which, at_ref, gn_ref, hid_ref, cot_ref, ctx_ref, wo_ref, vec_ref,
    gh_ref, dctx_ref, gwo_ref, sums_ref, acc_scr,
):
    strip = pl.program_id(0)
    grad = gn_ref[0]
    cot = cot_ref[0].astype(F32)
    scaled, rstd = norm_parts(hid_ref[0])
    t = grad * row_of(vec_ref, GAIN_2)
    cross = jnp.mean(t * scaled, axis=-1, keepdims=True)
    grad_hidden = cot + rstd * (t - jnp.mean(t, axis=-1, keepdims=True) - scaled * cross)
    grad_attn = grad_hidden.astype(BF16)
    gh_ref[0] = grad_attn
    dctx_ref[0] = dot_bt(grad_attn, wo_ref[...]).astype(BF16)
    grad_out = dot_at(ctx_ref[0], grad_attn)
    sums = [
        jnp.sum(grad * scaled, axis=0, keepdims=True),
        jnp.sum(grad, axis=0, keepdims=True),
        jnp.sum(grad_attn.astype(F32), axis=0, keepdims=True),
        jnp.sum(cot, axis=0, keepdims=True),
    ]

    @pl.when(strip == 0)
    def _():
        acc_scr[...] = grad_out
        for i, value in enumerate(sums):
            sums_ref[i : i + 1] = value

    @pl.when(strip > 0)
    def _():
        total = (acc_scr[...] + grad_out).astype(BF16)
        for i in range(16):
            gwo_ref[i ^ at_ref[which]] = total[i * 48 : (i + 1) * 48]
        for i, value in enumerate(sums):
            sums_ref[i : i + 1] += value


def middle(which, at, gn, hid, cot, ctx, wo, vec, after):
    return call(
        functools.partial(mid_kernel, which), [at, gn, far(hid), cot, far(ctx), far(wo), vec],
        [strip_block(D)] * 4 + [whole((D, D)), whole((VECTORS, D))], after,
        prefetch=1,
        grid=(STRIPS,),
        out_specs=[strip_block(D), strip_block(D), whole((16, 48, D)), whole((8, D))],
        scratch_shapes=[pltpu.VMEM((D, D), F32)],
        out_shape=[pltpu.HBM((STRIPS, SLOTS, D), BF16)] * 2
        + [jax.ShapeDtypeStruct((16, 48, D), BF16), jax.ShapeDtypeStruct((8, D), F32)],
        micros=10,
        mib=22,
        name="middle",
    )


def back_kernel(
    which, at_ref, len_ref, qa_ref, k_ref, v_ref, dctx_ref, ctx_ref, n1_ref,
    grads_ref, d_ref, sums_ref, acc_scr,
):
    d_scr = d_ref.at[0]
    strip = pl.program_id(0)
    lane = lane_iota()
    own = [half_mask(lane, h) for h in (0, 1)]
    length = len_ref[STRIPS * at_ref[0] + strip]
    kx = [key_extra(lane, length, h) for h in (0, 1)]
    vx = [
        jnp.where((lane > 64 * (1 - h)) & (lane < 64 * (1 - h) + 4), 1.0, 0.0).astype(BF16)
        for h in (0, 1)
    ]
    for p in range(GROUP_PAIRS):
        cols = slice(p * 128, p * 128 + 128)
        kp, vp, dp, cp = k_ref[0, :, cols], v_ref[0, :, cols], dctx_ref[0, :, cols], ctx_ref[0, :, cols]
        product = dp.astype(F32) * cp.astype(F32)
        dq, dk, dv = [], [], []
        for h in (0, 1):
            query = qa_ref[0, :, p * 256 + 128 * h : p * 256 + 128 * h + 128]
            inner = jnp.sum(product * own[h].astype(F32), axis=-1, keepdims=True)
            grad = dp * own[h] + pieces_extra(lane, -inner, h, 0.0)
            probs = jnp.exp(dot_bt(kp * own[h] + kx[h], query))
            grad_scores = (probs * dot_bt(vp * own[h] + vx[h], grad)).astype(BF16)
            dv.append(dot(probs.astype(BF16), dp))
            dk.append(dot(grad_scores, query))
            dq.append(dot_at(grad_scores, kp))
        low = lane < 64
        d_scr[:, cols] = (jnp.where(low, dq[0], dq[1]) * (HEAD_DIM**-0.5)).astype(BF16)
        d_scr[:, GCOLS + p * 128 : GCOLS + p * 128 + 128] = jnp.where(low, dk[0], dk[1]).astype(BF16)
        d_scr[:, 2 * GCOLS + p * 128 : 2 * GCOLS + p * 128 + 128] = jnp.where(low, dv[0], dv[1]).astype(BF16)
    d_all = d_scr[...]
    grad = dot_at(n1_ref[0], d_all)
    sums = jnp.sum(d_all.astype(F32), axis=0, keepdims=True)

    @pl.when(strip == 0)
    def _():
        acc_scr[...] = grad
        sums_ref[...] = sums

    @pl.when(strip > 0)
    def _():
        total = (acc_scr[...] + grad).astype(BF16)
        for i in range(16):
            grads_ref[i ^ at_ref[which]] = total[i * 48 : (i + 1) * 48]
        sums_ref[...] += sums


def attend_back(group, which, at, lengths, qa, k, v, dctx, ctx, n1, after):
    def cols(width):
        return pl.BlockSpec((1, SLOTS, width), lambda s, *_: (s, 0, group))

    return call(
        functools.partial(back_kernel, which),
        [at, lengths] + [far(o) for o in (qa, k, v, dctx, ctx, n1)],
        [cols(2 * GCOLS)] + [cols(GCOLS)] * 4 + [strip_block(D)], after,
        prefetch=2,
        grid=(STRIPS,),
        out_specs=[whole((16, 48, D)), strip_block(3 * GCOLS), whole((1, 3 * GCOLS))],
        scratch_shapes=[pltpu.VMEM((D, 3 * GCOLS), F32)],
        out_shape=[jax.ShapeDtypeStruct((16, 48, D), BF16), pltpu.HBM((STRIPS, SLOTS, 3 * GCOLS), BF16),
                   jax.ShapeDtypeStruct((1, 3 * GCOLS), F32)],
        micros=12,
        mib=18,
        name="attend_back",
    )


def end_kernel(
    at_ref, d0_ref, d1_ref, d2_ref, wq_ref, wk_ref, wv_ref, x_ref, gh_ref, vec_ref, mid_ref, s0_ref, s1_ref, s2_ref,
    up0_ref, up1_ref, up2_ref, own_ref, other_ref, small_ref, acc_scr, gp_scr,
):
    strip = pl.program_id(0)
    grad = None
    for g, d_ref in enumerate((d0_ref, d1_ref, d2_ref)):
        for i, w_ref in enumerate((wq_ref, wk_ref, wv_ref)):
            part = dot_bt(d_ref[0, :, i * GCOLS : (i + 1) * GCOLS], w_ref[:, g * GCOLS : (g + 1) * GCOLS])
            grad = part if grad is None else grad + part
    scaled, rstd = norm_parts(x_ref[0].astype(F32))
    t = grad * row_of(vec_ref, GAIN_1)
    cross = jnp.mean(t * scaled, axis=-1, keepdims=True)
    grad_in = rstd * (t - jnp.mean(t, axis=-1, keepdims=True) - scaled * cross)
    gp_scr[...] = (gh_ref[0].astype(F32) + grad_in).astype(BF16)
    core = at_ref[0]
    own_ref[0] = gp_scr[pl.ds(pl.multiple_of(core * HALF, 16), HALF)]
    other_ref[0] = gp_scr[pl.ds(pl.multiple_of((1 - core) * HALF, 16), HALF)]
    sums = [jnp.sum(grad * scaled, axis=0, keepdims=True), jnp.sum(grad, axis=0, keepdims=True)]

    @pl.when(strip == 0)
    def _():
        acc_scr[0:1], acc_scr[1:2] = sums

    @pl.when(strip > 0)
    def _():
        acc_scr[0:1] += sums[0]
        acc_scr[1:2] += sums[1]
        for g, s_ref in enumerate((s0_ref, s1_ref, s2_ref)):
            cols = slice(g * GCOLS, (g + 1) * GCOLS)
            acc_scr[2:3, cols] = s_ref[:, :GCOLS]
            acc_scr[3:4, cols] = s_ref[:, 2 * GCOLS :]
        acc_scr[4:8] = mid_ref[0:4]
        ups = [up0_ref[0], up0_ref[1], up1_ref[0], up2_ref[0]]
        for i, value in enumerate(ups):
            acc_scr[8 + i : 9 + i] = value
        acc_scr[12:16] = jnp.zeros((4, D), F32)
        small_ref[...] = acc_scr[...].astype(BF16)


def end(at, ds, wq, wk, wv, x, gh, vec, mid, sums, ups, after):
    half = pl.BlockSpec((1, HALF, D), lambda s, *_: (s, 0, 0))
    small = [mid, *sums, *ups]
    return call(
        end_kernel, [at, *(far(d) for d in ds), far(wq), far(wk), far(wv), far(x), far(gh), vec, *small],
        [strip_block(D)] * 3 + [whole((D, D))] * 3 + [strip_block(D)] * 2 + [whole((VECTORS, D))]
        + [whole(v.shape) for v in small], after,
        prefetch=1,
        grid=(STRIPS,),
        out_specs=[half, half, whole((SMALL, D))],
        scratch_shapes=[pltpu.VMEM((SMALL, D), F32), pltpu.VMEM((SLOTS, D), BF16)],
        out_shape=[jax.ShapeDtypeStruct((STRIPS, HALF, D), BF16)] * 2 + [jax.ShapeDtypeStruct((SMALL, D), BF16)],
        micros=9,
        mib=24,
        name="end",
    )


def back_in_place_kernel(at_ref, own_ref, got_ref, out_ref):
    mine = (pl.program_id(0) // STRIPS) == at_ref[0]

    @pl.when(mine)
    def _():
        out_ref[...] = own_ref[...]

    @pl.when(jnp.logical_not(mine))
    def _():
        out_ref[...] = got_ref[...]


def back_in_place(at, own, other, after):
    got = swap(other, "seq", 1, 2)
    block = (1, HALF, D)
    spec = pl.BlockSpec(block, lambda i, *_: (lax.rem(i, STRIPS), 0, 0))
    return call(
        back_in_place_kernel, [at, own, got], [spec, spec], after,
        prefetch=1,
        grid=(2 * STRIPS,),
        out_specs=pl.BlockSpec(block, lambda i, *_: (i, 0, 0)),
        out_shape=pltpu.HBM((2 * STRIPS, HALF, D), BF16),
        micros=2,
        mib=8,
        name="in_place",
    )


WIDE = 4


def crossed(i, cross):
    return i // 2 + 2 * lax.rem(i, 2) if cross else i


def widen_mlp_kernel(which, at_ref, mine_ref, other_ref, *rest):
    down_ref, up_ref = rest[-2:]
    swapped = at_ref[0] == 1
    place = lax.rem(at_ref[which], WIDE)
    for i in range(WIDE):
        mine, other = mine_ref[i ^ place], other_ref[i ^ place]
        down_ref[i * 96 : i * 96 + 96] = jnp.where(swapped, other, mine).astype(F32)
        up = jnp.where(swapped, mine, other).astype(F32)
        up_ref[i * 48 : i * 48 + 48, :D] = up[:48]
        up_ref[i * 48 : i * 48 + 48, D:] = up[48:]


def widen_mlp(part, at, p, given, after):
    which = p.which
    block = pl.BlockSpec(
        (WIDE, FCALL // 16, D), lambda i, at_ref: (crossed(i, p.cross) ^ (at_ref[which] // WIDE), 0, 0)
    )
    given = list(given)
    return call(
        functools.partial(widen_mlp_kernel, which), [at, p.total, p.got] + given,
        [block, block] + [pl.BlockSpec(memory_space=pl.ANY)] * len(given), after,
        prefetch=1,
        grid=(16 // WIDE,),
        out_specs=[
            pl.BlockSpec((WIDE * FCALL // 16, D), lambda i, *_: (16 // WIDE * part + i, 0)),
            pl.BlockSpec((WIDE * D // 16, FCALL), lambda i, *_: (i, part)),
        ],
        out_shape=[jax.ShapeDtypeStruct((FF, D), F32), jax.ShapeDtypeStruct((D, FF), F32)],
        input_output_aliases={3: 0, 4: 1} if given else {},
        micros=4,
        mib=12,
        name="widen_mlp",
    )


def widen_attn_kernel(w0, w1, cross1, at_ref, m0_ref, o0_ref, m1_ref, o1_ref, out_ref, q_ref, k_ref, v_ref, small_ref):
    swapped = at_ref[0] == 1
    first, second = lax.rem(at_ref[w0], WIDE), lax.rem(at_ref[w1], WIDE)
    block1 = crossed(pl.program_id(0), cross1) ^ (at_ref[w1] // WIDE)
    for i in range(WIDE):
        rows = slice(i * 48, i * 48 + 48)
        m0, o0 = m0_ref[i ^ first].astype(F32), o0_ref[i ^ first].astype(F32)
        at1 = pl.ds(pl.multiple_of((block1 * WIDE + (i ^ second)) * 48, 16), 48)
        m1, o1 = m1_ref[at1].astype(F32), o1_ref[at1].astype(F32)
        out_ref[rows] = jnp.where(swapped, o0, m0)
        blocks = (jnp.where(swapped, m0, o0), jnp.where(swapped, o1, m1), jnp.where(swapped, m1, o1))
        for g, block in enumerate(blocks):
            cols = slice(g * GCOLS, (g + 1) * GCOLS)
            q_ref[rows, cols] = block[:, :GCOLS]
            k_ref[rows, cols] = block[:, GCOLS : 2 * GCOLS]
            v_ref[rows, cols] = block[:, 2 * GCOLS :]
    small_ref[...] = m1_ref[16 * 48 :].astype(F32) + o1_ref[16 * 48 :].astype(F32)


def widen_attn(at, p0, p1, after):
    w0, w1 = p0.which, p1.which
    block = pl.BlockSpec((WIDE, 48, D), lambda i, at_ref: (crossed(i, p0.cross) ^ (at_ref[w0] // WIDE), 0, 0))
    rows = whole((16 * 48 + SMALL, D))
    return call(
        functools.partial(widen_attn_kernel, w0, w1, p1.cross), [at, p0.total, p0.got, p1.total, p1.got], [block, block, rows, rows], after,
        prefetch=1,
        grid=(16 // WIDE,),
        out_specs=[pl.BlockSpec((WIDE * 48, D), lambda i, *_: (i, 0))] * 4 + [whole((SMALL, D))],
        out_shape=[jax.ShapeDtypeStruct((D, D), F32)] * 4 + [jax.ShapeDtypeStruct((SMALL, D), F32)],
        micros=4,
        mib=16,
        name="widen_attn",
    )


def swap(value, axis, bit, size):
    return lax.ppermute(value, axis, [(i, i ^ bit) for i in range(size)])


TAIL = (
    "b", "end", "1", "0", "a", "b", "place", "b", "a", "1", "0", "b", "a", "0", "1", "a",
    "b", "a", "1", "b", "b", "0", "1", "a", "wide", "b", "a", "b", "1",
)


class Sum:
    def __init__(self, order, back, dp, keep=None, send=None, pick=None):
        self.keep, self.send, self.pick, self.small = keep, send, pick, None
        rest = [1 << i for i in range(4, dp.bit_length() - 1)]
        hops = [("seq", 1, 2, "half")] + [("dp", b, dp, "half") for b in order]
        hops += [("dp", b, dp, "whole") for b in rest]
        hops += [("dp", b, dp, "join") for b in back] + [("seq", 1, 2, "pair")]
        self.hops, self.total, self.got = hops, None, None
        self.which = 1 if back[-1] == 1 else 2
        self.cross = back[-1] != order[0]

    def start(self):
        axis, bit, size, kind = self.hops[0]
        self.got = swap(self.send if kind == "half" else self.total, axis, bit, size)


def merge_kernel(kinds, *refs):
    at_ref, refs = refs[0], refs[1:]
    outs = refs[sum(3 if kind == "load" else 2 for kind in kinds) :]
    for kind in kinds:
        (a, b), refs = refs[:2], refs[2:]
        if kind == "pick":
            keep, send = outs[:2]

            @pl.when(at_ref[0] == 0)
            def _():
                keep[...], send[...] = a[...], b[...]

            @pl.when(at_ref[0] != 0)
            def _():
                keep[...], send[...] = b[...], a[...]

        elif kind == "split":
            half = a.shape[0] // 2
            outs[0][...] = a[:half] + b[:half]
            outs[1][...] = a[half:] + b[half:]
        elif kind == "add":
            outs[0][...] = a[...] + b[...]
        elif kind == "load":
            rows = a.shape[1]
            outs[0][:rows] = a[0] + b[0]
            outs[0][rows:] = refs[0][...]
            refs = refs[1:]
        elif kind == "join":
            half = a.shape[0]
            outs[0][:half] = a[...]
            outs[0][half:] = b[...]
        else:
            rows = a.shape[0] - SMALL
            outs[0][:rows], outs[0][rows : 2 * rows] = a[:rows], b[:rows]
            outs[0][2 * rows :] = a[rows:] + b[rows:]
        outs = outs[2 if kind in ("pick", "split") else 1 :]


def merge(at, pieces, after):
    kinds, operands, shapes = [], [], []
    for p in pieces:
        if p.pick:
            kind, args = "pick", list(p.pick)
        else:
            kind = p.hops.pop(0)[3]
            args = [p.keep if kind == "half" else p.total, p.got]
            if kind == "half":
                kind = "split" if p.hops[0][3] == "half" else "add"
            elif kind == "whole":
                kind = "add"
            if p.small is not None and kind == "add" and p.hops[0][3] == "join":
                kind, args = "load", args + [p.small]
            elif p.small is not None and kind == "join":
                kind = "carry"
        n, tail = args[0].shape[0], args[0].shape[1:]
        n = {"pick": [n, n], "split": [n // 2, n // 2], "add": [n], "join": [2 * n], "carry": [2 * n - SMALL],
             "load": [1]}[kind]
        kinds.append(kind)
        operands += args
        shapes.append([(tail[0] + SMALL, D)] if kind == "load" else [(m,) + tail for m in n])
    flat = [shape for group in shapes for shape in group]
    size = sum(2 * v.size for v in operands) + sum(2 * D * (s[0] * s[1] // D if len(s) == 2 else s[0] * s[1]) for s in flat)
    outs = list(call(
        functools.partial(merge_kernel, kinds), [at] + operands, [whole(v.shape) for v in operands], after,
        prefetch=1,
        grid=(1,),
        out_specs=[whole(shape) for shape in flat],
        out_shape=[jax.ShapeDtypeStruct(shape, BF16) for shape in flat],
        micros=2,
        mib=4 + (size >> 20),
        name="merge",
    ))
    made = list(outs)
    for p, kind in zip(pieces, kinds):
        p.pick = None
        if kind in ("pick", "split"):
            p.keep, p.send = outs[:2]
            outs = outs[2:]
        else:
            p.total, outs = outs[0], outs[1:]
        p.start()
    return made


def local(
    dp, patches, lengths, gain_one, shift_one, w_query, b_query, w_key, w_value, b_value, w_out, b_out,
    gain_two, shift_two, w_up, b_up, w_down, b_down, cotangent,
):
    core, block = lax.axis_index("seq"), lax.axis_index("dp")
    x_first, y_first = (1, 2, 4, 8), (2, 1, 4, 8)

    def place_of(order):
        return sum(jnp.where((block & bit) != 0, 8 >> i, 0) for i, bit in enumerate(order))

    at = jnp.stack([core, place_of(x_first), place_of(y_first)]).astype(jnp.int32)
    foreign = lambda v: lax.dynamic_slice(v, (STRIPS * (1 - core), 0, 0), (STRIPS, HALF, D))
    got = swap(foreign(patches), "seq", 1, 2)
    got_cot = swap(foreign(cotangent), "seq", 1, 2)
    vectors = (gain_one, shift_one, b_query, b_value, b_out, gain_two, shift_two, b_down, b_up)
    vec = jnp.concatenate(vectors).reshape(VECTORS, D)
    n1, qa, k, v, ctx, hid, n2, x, cot = attend(
        at, lengths, patches, got, cotangent, got_cot, vec, w_query, w_key, w_value, w_out
    )
    flat = lambda v: v.reshape(ROWS, D)
    shared = (at, flat(n2), flat(cot), w_up, w_down, vec)
    keep, send, gn, up_0, acc = mlp(0, 2, 1, *shared, flat(hid), None, None, [])
    m0 = Sum(x_first, Y_LAST, dp, keep, send)
    m0.start()
    keep, send, gn, up_1, acc = mlp(2, 1, 1, *shared, acc, gn, None, [])
    made = merge(at, [m0], [gn])
    keep, send, gn, up_2, _, out_own, out_other = mlp(3, 1, 1, *shared, acc, gn, (keep, send), made)
    m1 = Sum(x_first, Y_LAST, dp, keep, send)
    m1.start()
    gh, dctx, g_out, sums_mid = middle(1, at, gn.reshape(STRIPS, SLOTS, D), hid, cot, ctx, w_out, vec, [send])
    made = merge(at, [m0, m1], [g_out])
    back = (at, lengths, qa, k, v, dctx, ctx, n1)
    grads_0, d_0, sums_0 = attend_back(0, 1, *back, made)
    a0 = Sum(x_first, X_LAST, dp, pick=(g_out, grads_0))
    made = merge(at, [m0, a0], [grads_0])
    output = back_in_place(at, out_own, out_other, made)
    grads_1, d_1, sums_1 = attend_back(1, 1, *back, made)
    made = merge(at, [m0, m1, a0], [grads_1])
    grads_2, d_2, sums_2 = attend_back(2, 1, *back, made + [output])
    a1 = Sum(x_first, X_LAST, dp, pick=(grads_1, grads_2))
    made = merge(at, [m0, m1, a0, a1], [grads_2])
    pieces = {"0": m0, "1": m1, "a": a0, "b": a1}
    for turn in TAIL:
        if turn == "end":
            gp_own, gp_other, a1.small = end(
                at, (d_0, d_1, d_2), w_query, w_key, w_value, x, gh, vec, sums_mid, (sums_0, sums_1, sums_2),
                (up_0, up_1, up_2), made,
            )
            for bit in range(4, dp.bit_length() - 1):
                a1.small = a1.small + swap(a1.small, "dp", 1 << bit, dp)
            made = [a1.small]
        elif turn == "place":
            grad_patches = back_in_place(at, gp_own, gp_other, made)
            made = [grad_patches]
        elif turn == "wide":
            given = widen_mlp(0, at, m0, (), made)
            made = [given[0]]
        else:
            made = merge(at, [pieces[c] for c in turn], made)
    for p in pieces.values():
        while len(p.hops) > 1:
            made = merge(at, [p], made)
    g_out, g_query, g_key, g_value, small = widen_attn(at, a0, a1, [])
    g_down, g_up = widen_mlp(1, at, m1, given, [])
    small = small.reshape(-1)
    vecs = [small[i * D : (i + 1) * D] for i in range(8)]
    g_bup = small[8 * D : 8 * D + FF]
    return (
        output, grad_patches, vecs[0], vecs[1], g_query, vecs[2], g_key, g_value, vecs[3], g_out, vecs[6],
        vecs[4], vecs[5], g_up, g_bup, g_down, vecs[7],
    )


def solution(mesh):
    dp = mesh.shape["dp"]
    rows, rep = P("dp", "seq", None), P()
    return jax.shard_map(
        functools.partial(local, dp),
        mesh=mesh,
        in_specs=(rows, P("dp")) + (rep,) * 15 + (rows,),
        out_specs=(rows, rows) + (rep,) * 15,
        check_vma=False,
    )
```

time: 536 us -> 323 us (0.60); the launches traced: 526 us -> 319 us
  waiting for transfers between devices: 184 us -> 73.8 us
  blocking collectives: 40.5 us -> 0 us
  local copies, waits for them, and re-layouts: 34.6 us -> 7.89 us
  other arithmetic: 16 us -> 0.08 us
  starting transfers between devices: 45.8 us -> 36.4 us
    ppermute x30 -> x44, waiting for transfers between devices: 182 us -> 73.8 us  [swap(): return lax.ppermute(value, axis, [(i, i ^ bit) for i in range(size)])]
    psum x1 -> x0, blocking collectives: 40.5 us -> none  [local(): small = lax.psum(jnp.concatenate(small, axis=1), ('dp', 'seq'))[0]]
    all_to_all x4 -> x0, starting transfers between devices: 15.1 us -> none  [the longest x2 7.59 us: local(): lax.all_to_all(v, 'seq', split_axis=1, concat_axis=0, tiled=True)]
    concatenate x9 -> x0, other arithmetic: 8.68 us -> none  [gather(): total = jnp.concatenate([total, swap(total, 'dp', bit, dp)], axis=0)]
    reshape x9 -> x1, local copies, waits for them, and re-layouts: 7.54 us -> 0.01 us  [local(): vec = jnp.concatenate(vectors).reshape(VECTORS, D)]
    unnamed x100 -> x44, local copies, waits for them, and re-layouts: 12.5 us -> 5.23 us
    ppermute x30 -> x44, starting transfers between devices: 30.7 us -> 36.4 us  [swap(): return lax.ppermute(value, axis, [(i, i ^ bit) for i in range(size)])]
    all_to_all x4 -> x0, local copies, waits for them, and re-layouts: 5.38 us -> none  [the longest x2 2.78 us: local(): lax.all_to_all(v, 'seq', split_axis=1, concat_axis=0, tiled=True)]
  transfers between devices with their start and end apart: 34 -> 44, of which waited for: 17 -> 16; matrix products, arithmetic and copies ran while one was open for 8% -> 0% of each run, Pallas kernels for 17% -> 40%
where the time goes in v2:
time: 323 us; the launch traced here: 319 us
  Pallas kernels  199 us (62%)
  waiting for transfers between devices  73.8 us (23%)
  starting transfers between devices  36.4 us (11%)
  local copies, waits for them, and re-layouts  7.89 us (2%)
    pallas_call x45, Pallas kernels, call(): pl.pallas_call(body, grid_spec=spec, compiler_params=params(mib), cost_es...  199 us
    ppermute x44, waiting for transfers between devices, swap(): return lax.ppermute(value, axis, [(i, i ^ bit) for i in range(size)])  73.8 us
    ppermute x44, starting transfers between devices, swap(): return lax.ppermute(value, axis, [(i, i ^ bit) for i in range(size)])  36.4 us
  transfers between devices with their start and end apart: 44, of which 16 were waited for; matrix products, arithmetic and copies ran while one was open for 0% of the time, Pallas kernels for 40%

profile of v2, /device:TPU:0, one launch (start us, length us, event | category | flops | bytes accessed | tf_op | source)
XLA Modules:
  0.0 318.6 jit_solution(15972122026238507096)
XLA Ops:
  5.8 32.0 %attend.1 = (bf16[2,544,768]{2,1,0:T(8,128)(2,1)}, bf16[2,544,1536]{2,1,0:T(8,128)(2,1)}, bf16[2,544,768]{2,1,0:T(8,128)(2,1)}, bf16[2,544,768]{2,1,0:T(8,128)(2...) custom-call(s32[3]{0:T(128)S(1)} %pad_add_fusion.refs_0_, ...), custom_call_target="tpu_custom_call" | custom-call | flops 321999994880 | tf_op jit(solution)/shard_map/attend/pallas_call | solution.py:58
  37.7 25.2 %mlp.3 = (bf16[16,96,768]{2,1,0:T(8,128)(2,1)S(1)}, bf16[16,96,768]{2,1,0:T(8,128)(2,1)S(1)}, f32[1088,768]{1,0:T(8,128)S(1)}, f32[2,1,768]{2,1,0:T(1,128)S(1)}, f32[1088,768]{1,0:T(8,128)S(1)}) custom-call(s32[3]{0:T(128)S(1)} %pad_add_fusion.refs_0_, bf16[1088,768]{1,0:T(8,128)(2,1)S(1)} %bitcast.11, bf16[1088,768]{1,0:T(8,128)(2,1)S(1)} %bitcast.8, ...), custom_call_target="tpu_custom_call" | custom-call | flops 276000014336 | tf_op jit(solution)/shard_map/mlp/pallas_call | solution.py:58
  63.4 12.7 %mlp.4 = (bf16[16,96,768]{2,1,0:T(8,128)(2,1)S(1)}, bf16[16,96,768]{2,1,0:T(8,128)(2,1)S(1)}, f32[1088,768]{1,0:T(8,128)S(1)}, f32[1,1,768]{2,1,0:T(1,128)S(1)}, f32[1088,768]{1,0:T(8,128)S(1)}) custom-call(s32[3]{0:T(128)S(1)} %pad_add_fusion.refs_0_, bf16[1088,768]{1,0:T(8,128)(2,1)S(1)} %bitcast.12, ...), custom_call_target="tpu_custom_call", output_to_operand_aliasing={{4}: (6, {}), {2}: (7, {})} | custom-call | flops 138000007168 | tf_op jit(solution)/shard_map/mlp/pallas_call | solution.py:58
  76.1 1.9 merge.31
  78.0 2.6 collective-permute-start.4
  80.6 14.0 %mlp.5 = (bf16[16,96,768]{2,1,0:T(8,128)(2,1)S(1)}, bf16[16,96,768]{2,1,0:T(8,128)(2,1)S(1)}, f32[1088,768]{1,0:T(8,128)S(1)}, f32[1,1,768]{2,1,0:T(1,128)S(1)},...) custom-call(s32[3]{0:T(128)S(1)} %pad_add_fusion.refs_0_, ...), custom_call_target="tpu_custom_call", output_to_operand_aliasing={{4}: (6, {}), {2}: (7, {}), {0}: (8, {}), {1}: (9, {})} | custom-call | flops 138000007168 | tf_op jit(solution)/shard_map/mlp/pallas_call | solution.py:58
  95.1 10.4 %middle.1 = (bf16[2,544,768]{2,1,0:T(8,128)(2,1)}, bf16[2,544,768]{2,1,0:T(8,128)(2,1)}, bf16[16,48,768]{2,1,0:T(8,128)(2,1)S(1)}, f32[8,768]{1,0:T(8,128)S(1)}) custom-call(s32[3]{0:T(128)S(1)} %pad_add_fusion.refs_0_, f32[2,544,768]{2,1,0:T(8,128)S(1)} %bitcast.7, f32[2,544,768]{2,1,0:T(8,128)} %get-tuple-element.106.refs_2_, ...), custom_call_target="tpu_custom_call" | custom-call | flops 115000000512 | tf_op jit(solution)/shard_map/middle/pallas_call | solution.py:58
  105.5 1.9 collective-permute-done.4.refs_2_
  107.4 3.3 %merge.32 = (bf16[4,96,768]{2,1,0:T(8,128)(2,1)S(1)}, bf16[4,96,768]{2,1,0:T(8,128)(2,1)S(1)}, bf16[8,96,768]{2,1,0:T(8,128)(2,1)S(1)}, bf16[8,96,768]{2,1,0:T(8,128)(2,1)}) custom-call(s32[3]{0:T(128)S(1)} %pad_add_fusion.refs_0_, bf16[8,96,768]{2,1,0:T(8,128)(2,1)S(1)} %get-tuple-element.115.refs_10_.refs_1_, ...), custom_call_target="tpu_custom_call" | custom-call | flops 23000000512 | tf_op jit(solution)/shard_map/merge/pallas_call | solution.py:58
  110.7 1.8 collective-permute-start.6
  112.5 1.5 collective-permute-start.8
  114.0 14.0 %attend_back.3 = (bf16[16,48,768]{2,1,0:T(8,128)(2,1)S(1)}, bf16[2,544,768]{2,1,0:T(8,128)(2,1)}, f32[1,768]{1,0:T(1,128)S(1)}) custom-call(s32[3]{0:T(128)S(1)} %pad_add_fusion.refs_0_, s32[4]{0:T(128)S(1)} %copy-done, bf16[2,544,1536]{2,1,0:T(8,128)(2,1)} %get-tuple-element.126.refs_2_, bf16[2,544,768]{2,1,0:T(8,128)(2,1)} %get-tuple-element.127.refs_3_, ...), custom_call_target="tpu_custom_call" | custom-call | flops 138000007168 | tf_op jit(solution)/shard_map/attend_back/pallas_call | solution.py:58
  128.0 2.1 merge.33
  130.0 1.6 collective-permute-start.7
  131.6 14.0 %attend_back.4 = (bf16[16,48,768]{2,1,0:T(8,128)(2,1)S(1)}, bf16[2,544,768]{2,1,0:T(8,128)(2,1)}, f32[1,768]{1,0:T(1,128)S(1)}) custom-call(s32[3]{0:T(128)S(1)} %pad_add_fusion.refs_0_, s32[4]{0:T(128)S(1)} %copy-done, bf16[2,544,1536]{2,1,0:T(8,128)(2,1)} %get-tuple-element.126.refs_2_, bf16[2,544,768]{2,1,0:T(8,128)(2,1)} %get-tuple-element.127.refs_3_, ...), custom_call_target="tpu_custom_call" | custom-call | flops 138000007168 | tf_op jit(solution)/shard_map/attend_back/pallas_call | solution.py:58
  145.6 4.2 %in_place.2.refs_14_ = bf16[4,272,768]{2,1,0:T(8,128)(2,1)} custom-call(s32[3]{0:T(128)S(1)} %pad_add_fusion.refs_0_, bf16[2,272,768]{2,1,0:T(8,128)(2,1)S(1)} %get-tuple-element.117.refs_1_, bf16[2,272,768]{2,1,0:T(8,128)(2,1)} %collective-permute-done.3.refs_2_, bf16[2,96,768]{2,1,0:T(8,128)(2,1)S(1)} %get-tuple-element.134.refs_3_.refs_8_.refs_1_, ...), custom_call_target="tpu_custom_call" | custom-call | flops 23000000512 | tf_op jit(solution)/shard_map/in_place/pallas_call | solution.py:58
  149.8 2.6 merge.34
  153.5 2.6 collective-permute-start.10
  156.1 14.0 %attend_back.5 = (bf16[16,48,768]{2,1,0:T(8,128)(2,1)S(1)}, bf16[2,544,768]{2,1,0:T(8,128)(2,1)}, f32[1,768]{1,0:T(1,128)S(1)}) custom-call(s32[3]{0:T(128)S(1)} %pad_add_fusion.refs_0_, s32[4]{0:T(128)S(1)} %copy-done, bf16[2,544,1536]{2,1,0:T(8,128)(2,1)} %get-tuple-element.126.refs_2_, bf16[2,544,768]{2,1,0:T(8,128)(2,1)} %get-tuple-element.127.refs_3_, ...), custom_call_target="tpu_custom_call" | custom-call | flops 138000007168 | tf_op jit(solution)/shard_map/attend_back/pallas_call | solution.py:58
  170.1 1.8 merge.35
  173.0 1.5 collective-permute-start.16
  174.8 1.5 merge.36
  176.3 1.5 collective-permute-start.15
  177.8 10.4 %end.1 = (bf16[2,272,768]{2,1,0:T(8,128)(2,1)S(1)}, bf16[2,272,768]{2,1,0:T(8,128)(2,1)S(1)}, bf16[16,768]{1,0:T(8,128)(2,1)S(1)}) custom-call(s32[3]{0:T(128)S(1)} %pad_add_fusion.refs_0_, bf16[2,544,768]{2,1,0:T(8,128)(2,1)} %get-tuple-element.138.refs_1_, bf16[2,544,768]{2,1,0:T(8,128)(2,1)} %get-tuple-element.139.refs_2_, ...), custom_call_target="tpu_custom_call" | custom-call | flops 103499997184 | tf_op jit(solution)/shard_map/end/pallas_call | solution.py:58
  188.8 2.1 collective-permute-start.24
  190.9 1.5 merge.38.refs_3_.refs_1_
  192.5 1.6 collective-permute-start.23
  194.1 1.5 merge.39
  196.2 1.7 merge.40
  198.4 2.3 in_place.3.refs_3_
  200.7 5.8 %collective-permute-done.20.refs_2_ = bf16[4,48,768]{2,1,0:T(8,128)(2,1)S(1)} collective-permute-done((bf16[4,48,768]{2,1,0:T(8,128)(2,1)S(1)}, bf16[4,48,768]{2,1,0:T(8,128)(2,1)S(1)}, u32[]{:S(2)}, u32[]{:S(2)}) %collective-permute-start.20) | collective-permute-done | bytes 294944 | tf_op jit(solution)/shard_map/ppermute | solution.py:604
  208.5 1.6 collective-permute-start.22
  211.7 2.6 collective-permute-start.26
  216.8 5.9 %collective-permute-done.21.refs_2_ = bf16[1,48,768]{2,1,0:T(8,128)(2,1)S(1)} collective-permute-done((bf16[1,48,768]{2,1,0:T(8,128)(2,1)S(1)}, bf16[1,48,768]{2,1,0:T(8,128)(2,1)S(1)}, u32[]{:S(2)}, u32[]{:S(2)}) %collective-permute-start.21) | collective-permute-done | bytes 73760 | tf_op jit(solution)/shard_map/ppermute | solution.py:604
  223.3 4.8 %collective-permute-done.27.refs_2_ = bf16[4,96,768]{2,1,0:T(8,128)(2,1)S(1)} collective-permute-done((bf16[4,96,768]{2,1,0:T(8,128)(2,1)S(1)}, bf16[4,96,768]{2,1,0:T(8,128)(2,1)S(1)}, u32[]{:S(2)}, u32[]{:S(2)}) %collective-permute-start.27) | collective-permute-done | bytes 589856 | tf_op jit(solution)/shard_map/ppermute | solution.py:604
  230.4 1.6 collective-permute-start.28
  233.0 7.8 %collective-permute-done.28.refs_2_ = bf16[2,48,768]{2,1,0:T(8,128)(2,1)S(1)} collective-permute-done((bf16[2,48,768]{2,1,0:T(8,128)(2,1)S(1)}, bf16[2,48,768]{2,1,0:T(8,128)(2,1)S(1)}, u32[]{:S(2)}, u32[]{:S(2)}) %collective-permute-start.28) | collective-permute-done | bytes 147488 | tf_op jit(solution)/shard_map/ppermute | solution.py:604
  243.2 1.5 collective-permute-start.30
  245.3 2.8 collective-permute-done.35.refs_2_
  249.2 22.4 %collective-permute-done.33.refs_2_ = bf16[8,96,768]{2,1,0:T(8,128)(2,1)S(1)} collective-permute-done((bf16[8,96,768]{2,1,0:T(8,128)(2,1)S(1)}, bf16[8,96,768]{2,1,0:T(8,128)(2,1)S(1)}, u32[]{:S(2)}, u32[]{:S(2)}) %collective-permute-start.33) | collective-permute-done | bytes 1179680 | tf_op jit(solution)/shard_map/ppermute | solution.py:604
  273.6 1.7 collective-permute-done.30.refs_2_
  276.9 4.5 %widen_mlp.2 = (f32[3072,768]{1,0:T(8,128)}, f32[768,3072]{1,0:T(8,128)}) custom-call(s32[3]{0:T(128)S(1)} %pad_add_fusion.refs_0_, bf16[16,96,768]{2,1,0:T(8,128)(2,1)S(1)} %merge.55.refs_3_.refs_1_, bf16[16,96,768]{2,1,0:T(8,128)(2,1)S(1)} %collective-permute-done.38.refs_2_, bf16[8,48,768]{2,1,0:T(8,128)(2,1)S(1)} %merge.57.refs_3_.refs_1_), custom_call_target="tpu_custom_call" | custom-call | flops 46000001024 | tf_op jit(solution)/shard_map/widen_mlp/pallas_call | solution.py:58
  281.4 3.7 %copy-done.1 = f32[3072,768]{1,0:T(8,128)S(1)} copy-done((f32[3072,768]{1,0:T(8,128)S(1)}, f32[3072,768]{1,0:T(8,128)}, u32[]{:S(2)}) %copy-start.1) | copy-done | bytes 9437208
  286.8 4.1 %collective-permute-done.36.refs_2_ = bf16[8,48,768]{2,1,0:T(8,128)(2,1)S(1)} collective-permute-done((bf16[8,48,768]{2,1,0:T(8,128)(2,1)S(1)}, bf16[8,48,768]{2,1,0:T(8,128)(2,1)S(1)}, u32[]{:S(2)}, u32[]{:S(2)}) %collective-permute-start.36) | collective-permute-done | bytes 589856 | tf_op jit(solution)/shard_map/ppermute | solution.py:604
  291.6 11.3 %collective-permute-done.40.refs_2_ = bf16[400,768]{1,0:T(8,128)(2,1)S(1)} collective-permute-done((bf16[400,768]{1,0:T(8,128)(2,1)S(1)}, bf16[400,768]{1,0:T(8,128)(2,1)S(1)}, u32[]{:S(2)}, u32[]{:S(2)}) %collective-permute-start.40) | collective-permute-done | bytes 614432 | tf_op jit(solution)/shard_map/ppermute | solution.py:604
  304.8 1.6 collective-permute-done.41.refs_4_
  306.4 4.3 %widen_attn.1 = (f32[768,768]{1,0:T(8,128)}, f32[768,768]{1,0:T(8,128)}, f32[768,768]{1,0:T(8,128)}, f32[768,768]{1,0:T(8,128)}, f32[16,768]{1,0:T(8,128)S(1)}) custom-call(s32[3]{0:T(128)S(1)} %pad_add_fusion.refs_0_, bf16[16,48,768]{2,1,0:T(8,128)(2,1)S(1)} %merge.59.refs_3_.refs_1_, bf16[16,48,768]{2,1,0:T(8,128)(2,1)S(1)} %collective-permute-done.39.refs_2_, ...), custom_call_target="tpu_custom_call" | custom-call | flops 46000001024 | tf_op jit(solution)/shard_map/widen_attn/pallas_call | solution.py:58
  312.0 6.3 %widen_mlp.3 = (f32[3072,768]{1,0:T(8,128)}, f32[768,3072]{1,0:T(8,128)}) custom-call(s32[3]{0:T(128)S(1)} %pad_add_fusion.refs_0_, bf16[16,96,768]{2,1,0:T(8,128)(2,1)S(1)} %merge.61.refs_1_, bf16[16,96,768]{2,1,0:T(8,128)(2,1)} %collective-permute-done.43.refs_2_, ...), custom_call_target="tpu_custom_call", output_to_operand_aliasing={{0}: (3, {}), {1}: (4, {})} | custom-call | flops 46000001024 | tf_op jit(solution)/shard_map/widen_mlp/pallas_call | solution.py:58
  (138 shorter events, 33.0 us)
Async XLA Ops:
  0.8 5.0 %copy-start = (s32[4]{0:T(128)S(1)}, s32[4]{0:T(128)}, u32[]{:S(2)}) copy-start(s32[4]{0:T(128)} %refs_1_.7) | copy-start | bytes 52
  2.1 2.5 collective-permute-start
  2.7 3.1 collective-permute-start.1
  62.9 13.2 %collective-permute-start.2 = (bf16[16,96,768]{2,1,0:T(8,128)(2,1)S(1)}, bf16[16,96,768]{2,1,0:T(8,128)(2,1)S(1)}, u32[]{:S(2)}, u32[]{:S(2)}) collective-permute-start(bf16[16,96,768]{2,1,0:T(8,128)(2,1)S(1)} %get-tuple-element.114), channel_id=1, source_target_pairs={{0,1},{1,0},{2,3},{3,2},{4,5},{5,4},{6,7},{7,6},{8,9},{9,8},{10,11... | collective-permute-start | bytes 7077896 | tf_op jit(solution)/shard_map/ppermute | solution.py:604
  78.0 29.4 %collective-permute-start.4 = (bf16[8,96,768]{2,1,0:T(8,128)(2,1)}, bf16[8,96,768]{2,1,0:T(8,128)(2,1)}, u32[]{:S(2)}, u32[]{:S(2)}) collective-permute-start(bf16[8,96,768]{2,1,0:T(8,128)(2,1)} %get-tuple-element.116.refs_11_), channel_id=1, source_target_pairs={{0,2},{2,0},{4,6},{6,4},{8,10},{10,8},{12,14},{14,12},{16,18},{18,... | collective-permute-start | bytes 3538952 | tf_op jit(solution)/shard_map/ppermute | solution.py:604
  94.6 12.8 %collective-permute-start.5 = (bf16[16,96,768]{2,1,0:T(8,128)(2,1)S(1)}, bf16[16,96,768]{2,1,0:T(8,128)(2,1)S(1)}, u32[]{:S(2)}, u32[]{:S(2)}) collective-permute-start(bf16[16,96,768]{2,1,0:T(8,128)(2,1)S(1)} %get-tuple-element.120.refs_7_), channel_id=1, source_target_pairs={{0,1},{1,0},{2,3},{3,2},{4,5},{5,4},{6,7},{7,6},{8,9},{9,8},{10,11... | collective-permute-start | bytes 7077896 | tf_op jit(solution)/shard_map/ppermute | solution.py:604
  94.7 50.9 %collective-permute-start.3 = (bf16[2,272,768]{2,1,0:T(8,128)(2,1)}, bf16[2,272,768]{2,1,0:T(8,128)(2,1)}, u32[]{:S(2)}, u32[]{:S(2)}) collective-permute-start(bf16[2,272,768]{2,1,0:T(8,128)(2,1)} %get-tuple-element.118), channel_id=1, source_target_pairs={{0,1},{1,0},{2,3},{3,2},{4,5},{5,4},{6,7},{7,6},{8,9},{9,8},{10,11... | collective-permute-start | bytes 2506760 | tf_op jit(solution)/shard_map/ppermute | solution.py:604
  110.7 17.3 %copy-start.4 = (bf16[8,96,768]{2,1,0:T(8,128)(2,1)}, bf16[8,96,768]{2,1,0:T(8,128)(2,1)S(1)}, u32[]{:S(2)}) copy-start(bf16[8,96,768]{2,1,0:T(8,128)(2,1)S(1)} %get-tuple-element.131.refs_10_.refs_3_) | copy-start | bytes 3538948
  110.7 17.3 %collective-permute-start.6 = (bf16[4,96,768]{2,1,0:T(8,128)(2,1)S(1)}, bf16[4,96,768]{2,1,0:T(8,128)(2,1)S(1)}, u32[]{:S(2)}, u32[]{:S(2)}) collective-permute-start(bf16[4,96,768]{2,1,0:T(8,128)(2,1)S(1)} %get-tuple-element.125.refs_9_), channel_id=1, source_target_pairs={{0,4},{2,6},{4,0},{6,2},{8,12},{10,14},{12,8},{14,10},{16,20},{18,... | collective-permute-start | bytes 1769480 | tf_op jit(solution)/shard_map/ppermute | solution.py:604
  112.5 37.4 %collective-permute-start.8 = (bf16[8,96,768]{2,1,0:T(8,128)(2,1)}, bf16[8,96,768]{2,1,0:T(8,128)(2,1)}, u32[]{:S(2)}, u32[]{:S(2)}) collective-permute-start(bf16[8,96,768]{2,1,0:T(8,128)(2,1)} %get-tuple-element.132.refs_11_), channel_id=1, source_target_pairs={{0,2},{2,0},{4,6},{6,4},{8,10},{10,8},{12,14},{14,12},{16,18},{18,... | collective-permute-start | bytes 3538952 | tf_op jit(solution)/shard_map/ppermute | solution.py:604
  130.0 19.8 %collective-permute-start.9 = (bf16[16,48,768]{2,1,0:T(8,128)(2,1)}, bf16[16,48,768]{2,1,0:T(8,128)(2,1)}, u32[]{:S(2)}, u32[]{:S(2)}) collective-permute-start(bf16[16,48,768]{2,1,0:T(8,128)(2,1)} %get-tuple-element.137.refs_6_.refs_11_), channel_id=1, source_target_pairs={{0,1},{1,0},{2,3},{3,2},{4,5},{5,4},{6,7},{7,6},{8,9},{9,8},{10,11... | collective-permute-start | bytes 3538952 | tf_op jit(solution)/shard_map/ppermute | solution.py:604
  130.0 19.8 %collective-permute-start.7 = (bf16[2,96,768]{2,1,0:T(8,128)(2,1)}, bf16[2,96,768]{2,1,0:T(8,128)(2,1)}, u32[]{:S(2)}, u32[]{:S(2)}) collective-permute-start(bf16[2,96,768]{2,1,0:T(8,128)(2,1)} %get-tuple-element.135.refs_4_.refs_9_), channel_id=1, source_target_pairs={{0,8},{2,10},{4,12},{6,14},{8,0},{10,2},{12,4},{14,6},{16,24},{18,... | collective-permute-start | bytes 884744 | tf_op jit(solution)/shard_map/ppermute | solution.py:604
  149.8 6.3 %copy-start.2 = (bf16[4,272,768]{2,1,0:T(8,128)(2,1)S(1)}, bf16[4,272,768]{2,1,0:T(8,128)(2,1)}, u32[]{:S(2)}) copy-start(bf16[4,272,768]{2,1,0:T(8,128)(2,1)} %in_place.2.refs_14_) | copy-start | bytes 5013508
  152.4 17.7 %collective-permute-start.11 = (bf16[4,96,768]{2,1,0:T(8,128)(2,1)S(1)}, bf16[4,96,768]{2,1,0:T(8,128)(2,1)S(1)}, u32[]{:S(2)}, u32[]{:S(2)}) collective-permute-start(bf16[4,96,768]{2,1,0:T(8,128)(2,1)S(1)} %get-tuple-element.144.refs_11_), channel_id=1, source_target_pairs={{0,4},{2,6},{4,0},{6,2},{8,12},{10,14},{12,8},{14,10},{16,20},{18,... | collective-permute-start | bytes 1769480 | tf_op jit(solution)/shard_map/ppermute | solution.py:604
  153.0 17.1 %collective-permute-start.12 = (bf16[8,48,768]{2,1,0:T(8,128)(2,1)S(1)}, bf16[8,48,768]{2,1,0:T(8,128)(2,1)S(1)}, u32[]{:S(2)}, u32[]{:S(2)}) collective-permute-start(bf16[8,48,768]{2,1,0:T(8,128)(2,1)S(1)} %get-tuple-element.146.refs_13_), channel_id=1, source_target_pairs={{0,2},{2,0},{4,6},{6,4},{8,10},{10,8},{12,14},{14,12},{16,18},{18,... | collective-permute-start | bytes 1769480 | tf_op jit(solution)/shard_map/ppermute | solution.py:604
  153.5 16.6 %collective-permute-start.10 = (bf16[1,96,768]{2,1,0:T(8,128)(2,1)S(1)}, bf16[1,96,768]{2,1,0:T(8,128)(2,1)S(1)}, u32[]{:S(2)}, u32[]{:S(2)}) collective-permute-start(bf16[1,96,768]{2,1,0:T(8,128)(2,1)S(1)} %get-tuple-element.142.refs_9_), channel_id=1, source_target_pairs={{0,16},{2,18},{4,20},{6,22},{8,24},{10,26},{12,28},{14,30},{16,0},... | collective-permute-start | bytes 442376 | tf_op jit(solution)/shard_map/ppermute | solution.py:604
  171.9 4.3 %copy-start.6 = (bf16[4,48,768]{2,1,0:T(8,128)(2,1)}, bf16[4,48,768]{2,1,0:T(8,128)(2,1)S(1)}, u32[]{:S(2)}) copy-start(bf16[4,48,768]{2,1,0:T(8,128)(2,1)S(1)} %get-tuple-element.163.refs_6_.refs_1_) | copy-start | bytes 884740
  171.9 2.8 collective-permute-start.13
  171.9 16.3 %collective-permute-start.18 = (bf16[2,96,768]{2,1,0:T(8,128)(2,1)S(1)}, bf16[2,96,768]{2,1,0:T(8,128)(2,1)S(1)}, u32[]{:S(2)}, u32[]{:S(2)}) collective-permute-start(bf16[2,96,768]{2,1,0:T(8,128)(2,1)S(1)} %get-tuple-element.162.refs_5_), channel_id=1, source_target_pairs={{0,8},{2,10},{4,12},{6,14},{8,0},{10,2},{12,4},{14,6},{16,24},{18,... | collective-permute-start | bytes 884744 | tf_op jit(solution)/shard_map/ppermute | solution.py:604
  172.4 18.5 %collective-permute-start.17 = (bf16[1,96,768]{2,1,0:T(8,128)(2,1)}, bf16[1,96,768]{2,1,0:T(8,128)(2,1)}, u32[]{:S(2)}, u32[]{:S(2)}) collective-permute-start(bf16[1,96,768]{2,1,0:T(8,128)(2,1)} %get-tuple-element.160.refs_3_.refs_1_), channel_id=1, source_target_pairs={{0,16},{2,18},{4,20},{6,22},{8,24},{10,26},{12,28},{14,30},{16,0},... | collective-permute-start | bytes 442376 | tf_op jit(solution)/shard_map/ppermute | solution.py:604
  173.0 21.1 %collective-permute-start.16 = (bf16[4,48,768]{2,1,0:T(8,128)(2,1)}, bf16[4,48,768]{2,1,0:T(8,128)(2,1)}, u32[]{:S(2)}, u32[]{:S(2)}) collective-permute-start(bf16[4,48,768]{2,1,0:T(8,128)(2,1)} %get-tuple-element.164.refs_7_), channel_id=1, source_target_pairs={{0,4},{2,6},{4,0},{6,2},{8,12},{10,14},{12,8},{14,10},{16,20},{18,... | collective-permute-start | bytes 884744 | tf_op jit(solution)/shard_map/ppermute | solution.py:604
  176.3 19.9 %collective-permute-start.15 = (bf16[8,48,768]{2,1,0:T(8,128)(2,1)}, bf16[8,48,768]{2,1,0:T(8,128)(2,1)}, u32[]{:S(2)}, u32[]{:S(2)}) collective-permute-start(bf16[8,48,768]{2,1,0:T(8,128)(2,1)} %get-tuple-element.166.refs_18_), channel_id=1, source_target_pairs={{0,2},{2,0},{4,6},{6,4},{8,10},{10,8},{12,14},{14,12},{16,18},{18,... | collective-permute-start | bytes 1769480 | tf_op jit(solution)/shard_map/ppermute | solution.py:604
  188.1 10.3 %collective-permute-start.14 = (bf16[2,272,768]{2,1,0:T(8,128)(2,1)S(1)}, bf16[2,272,768]{2,1,0:T(8,128)(2,1)S(1)}, u32[]{:S(2)}, u32[]{:S(2)}) collective-permute-start(bf16[2,272,768]{2,1,0:T(8,128)(2,1)S(1)} %get-tuple-element.168), channel_id=1, source_target_pairs={{0,1},{1,0},{2,3},{3,2},{4,5},{5,4},{6,7},{7,6},{8,9},{9,8},{10,11... | collective-permute-start | bytes 2506760 | tf_op jit(solution)/shard_map/ppermute | solution.py:604
  188.8 22.3 %collective-permute-start.24 = (bf16[1,96,768]{2,1,0:T(8,128)(2,1)S(1)}, bf16[1,96,768]{2,1,0:T(8,128)(2,1)S(1)}, u32[]{:S(2)}, u32[]{:S(2)}) collective-permute-start(bf16[1,96,768]{2,1,0:T(8,128)(2,1)S(1)} %get-tuple-element.171.refs_4_), channel_id=1, source_target_pairs={{0,16},{2,18},{4,20},{6,22},{8,24},{10,26},{12,28},{14,30},{16,0},... | collective-permute-start | bytes 442376 | tf_op jit(solution)/shard_map/ppermute | solution.py:604
  192.5 21.9 %collective-permute-start.23 = (bf16[2,96,768]{2,1,0:T(8,128)(2,1)S(1)}, bf16[2,96,768]{2,1,0:T(8,128)(2,1)S(1)}, u32[]{:S(2)}, u32[]{:S(2)}) collective-permute-start(bf16[2,96,768]{2,1,0:T(8,128)(2,1)S(1)} %merge.38.refs_3_.refs_1_), channel_id=1, source_target_pairs={{0,8},{2,10},{4,12},{6,14},{8,0},{10,2},{12,4},{14,6},{16,24},{18,... | collective-permute-start | bytes 884744 | tf_op jit(solution)/shard_map/ppermute | solution.py:604
  195.7 14.5 %collective-permute-start.19 = (bf16[2,48,768]{2,1,0:T(8,128)(2,1)S(1)}, bf16[2,48,768]{2,1,0:T(8,128)(2,1)S(1)}, u32[]{:S(2)}, u32[]{:S(2)}) collective-permute-start(bf16[2,48,768]{2,1,0:T(8,128)(2,1)S(1)} %get-tuple-element.173.refs_4_), channel_id=1, source_target_pairs={{0,8},{2,10},{4,12},{6,14},{8,0},{10,2},{12,4},{14,6},{16,24},{18,... | collective-permute-start | bytes 442376 | tf_op jit(solution)/shard_map/ppermute | solution.py:604
  197.9 8.6 %collective-permute-start.20 = (bf16[4,48,768]{2,1,0:T(8,128)(2,1)S(1)}, bf16[4,48,768]{2,1,0:T(8,128)(2,1)S(1)}, u32[]{:S(2)}, u32[]{:S(2)}) collective-permute-start(bf16[4,48,768]{2,1,0:T(8,128)(2,1)S(1)} %get-tuple-element.175.refs_4_), channel_id=1, source_target_pairs={{0,4},{2,6},{4,0},{6,2},{8,12},{10,14},{12,8},{14,10},{16,20},{18,... | collective-permute-start | bytes 884744 | tf_op jit(solution)/shard_map/ppermute | solution.py:604
  208.5 7.0 %collective-permute-start.22 = (bf16[2,48,768]{2,1,0:T(8,128)(2,1)S(1)}, bf16[2,48,768]{2,1,0:T(8,128)(2,1)S(1)}, u32[]{:S(2)}, u32[]{:S(2)}) collective-permute-start(bf16[2,48,768]{2,1,0:T(8,128)(2,1)S(1)} %get-tuple-element.177.refs_4_), channel_id=1, source_target_pairs={{0,8},{2,10},{4,12},{6,14},{8,0},{10,2},{12,4},{14,6},{16,24},{18,... | collective-permute-start | bytes 442376 | tf_op jit(solution)/shard_map/ppermute | solution.py:604
  210.7 12.0 %collective-permute-start.21 = (bf16[1,48,768]{2,1,0:T(8,128)(2,1)S(1)}, bf16[1,48,768]{2,1,0:T(8,128)(2,1)S(1)}, u32[]{:S(2)}, u32[]{:S(2)}) collective-permute-start(bf16[1,48,768]{2,1,0:T(8,128)(2,1)S(1)} %get-tuple-element.179.refs_4_), channel_id=1, source_target_pairs={{0,16},{2,18},{4,20},{6,22},{8,24},{10,26},{12,28},{14,30},{16,0},... | collective-permute-start | bytes 221192 | tf_op jit(solution)/shard_map/ppermute | solution.py:604
  211.7 17.1 %collective-permute-start.26 = (bf16[1,96,768]{2,1,0:T(8,128)(2,1)S(1)}, bf16[1,96,768]{2,1,0:T(8,128)(2,1)S(1)}, u32[]{:S(2)}, u32[]{:S(2)}) collective-permute-start(bf16[1,96,768]{2,1,0:T(8,128)(2,1)S(1)} %merge.43.refs_3_.refs_1_), channel_id=1, source_target_pairs={{0,16},{2,18},{4,20},{6,22},{8,24},{10,26},{12,28},{14,30},{16,0},... | collective-permute-start | bytes 442376 | tf_op jit(solution)/shard_map/ppermute | solution.py:604
  214.9 13.2 %collective-permute-start.27 = (bf16[4,96,768]{2,1,0:T(8,128)(2,1)S(1)}, bf16[4,96,768]{2,1,0:T(8,128)(2,1)S(1)}, u32[]{:S(2)}, u32[]{:S(2)}) collective-permute-start(bf16[4,96,768]{2,1,0:T(8,128)(2,1)S(1)} %merge.44.refs_3_.refs_1_), channel_id=1, source_target_pairs={{0,2},{2,0},{4,6},{6,4},{8,10},{10,8},{12,14},{14,12},{16,18},{18,... | collective-permute-start | bytes 1769480 | tf_op jit(solution)/shard_map/ppermute | solution.py:604
  216.1 16.0 %collective-permute-start.29 = (bf16[1,48,768]{2,1,0:T(8,128)(2,1)S(1)}, bf16[1,48,768]{2,1,0:T(8,128)(2,1)S(1)}, u32[]{:S(2)}, u32[]{:S(2)}) collective-permute-start(bf16[1,48,768]{2,1,0:T(8,128)(2,1)S(1)} %get-tuple-element.181.refs_4_), channel_id=1, source_target_pairs={{0,16},{2,18},{4,20},{6,22},{8,24},{10,26},{12,28},{14,30},{16,0},... | collective-permute-start | bytes 221192 | tf_op jit(solution)/shard_map/ppermute | solution.py:604
  223.2 6.6 %collective-permute-start.25 = (bf16[1,48,768]{2,1,0:T(8,128)(2,1)S(1)}, bf16[1,48,768]{2,1,0:T(8,128)(2,1)S(1)}, u32[]{:S(2)}, u32[]{:S(2)}) collective-permute-start(bf16[1,48,768]{2,1,0:T(8,128)(2,1)S(1)} %merge.46.refs_3_.refs_1_), channel_id=1, source_target_pairs={{0,16},{2,18},{4,20},{6,22},{8,24},{10,26},{12,28},{14,30},{16,0},... | collective-permute-start | bytes 221192 | tf_op jit(solution)/shard_map/ppermute | solution.py:604
  229.3 12.1 %collective-permute-start.31 = (bf16[2,96,768]{2,1,0:T(8,128)(2,1)S(1)}, bf16[2,96,768]{2,1,0:T(8,128)(2,1)S(1)}, u32[]{:S(2)}, u32[]{:S(2)}) collective-permute-start(bf16[2,96,768]{2,1,0:T(8,128)(2,1)S(1)} %merge.48.refs_3_.refs_1_), channel_id=1, source_target_pairs={{0,8},{2,10},{4,12},{6,14},{8,0},{10,2},{12,4},{14,6},{16,24},{18,... | collective-permute-start | bytes 884744 | tf_op jit(solution)/shard_map/ppermute | solution.py:604
  230.4 10.4 %collective-permute-start.28 = (bf16[2,48,768]{2,1,0:T(8,128)(2,1)S(1)}, bf16[2,48,768]{2,1,0:T(8,128)(2,1)S(1)}, u32[]{:S(2)}, u32[]{:S(2)}) collective-permute-start(bf16[2,48,768]{2,1,0:T(8,128)(2,1)S(1)} %merge.49.refs_4_.refs_1_), channel_id=1, source_target_pairs={{0,8},{2,10},{4,12},{6,14},{8,0},{10,2},{12,4},{14,6},{16,24},{18,... | collective-permute-start | bytes 442376 | tf_op jit(solution)/shard_map/ppermute | solution.py:604
  232.6 9.4 %collective-permute-start.34 = (bf16[64,768]{1,0:T(8,128)(2,1)S(1)}, bf16[64,768]{1,0:T(8,128)(2,1)S(1)}, u32[]{:S(2)}, u32[]{:S(2)}) collective-permute-start(bf16[64,768]{1,0:T(8,128)(2,1)S(1)} %merge.50.refs_3_.refs_1_), channel_id=1, source_target_pairs={{0,16},{2,18},{4,20},{6,22},{8,24},{10,26},{12,28},{14,30},{16,0},... | collective-permute-start | bytes 294920 | tf_op jit(solution)/shard_map/ppermute | solution.py:604
  242.6 5.5 %collective-permute-start.35 = (bf16[112,768]{1,0:T(8,128)(2,1)S(1)}, bf16[112,768]{1,0:T(8,128)(2,1)S(1)}, u32[]{:S(2)}, u32[]{:S(2)}) collective-permute-start(bf16[112,768]{1,0:T(8,128)(2,1)S(1)} %merge.53.refs_1_.refs_3_), channel_id=1, source_target_pairs={{0,8},{2,10},{4,12},{6,14},{8,0},{10,2},{12,4},{14,6},{16,24},{18,... | collective-permute-start | bytes 516104 | tf_op jit(solution)/shard_map/ppermute | solution.py:604
  242.6 29.0 %collective-permute-start.33 = (bf16[8,96,768]{2,1,0:T(8,128)(2,1)S(1)}, bf16[8,96,768]{2,1,0:T(8,128)(2,1)S(1)}, u32[]{:S(2)}, u32[]{:S(2)}) collective-permute-start(bf16[8,96,768]{2,1,0:T(8,128)(2,1)S(1)} %merge.47.refs_3_.refs_1_), channel_id=1, source_target_pairs={{0,4},{2,6},{4,0},{6,2},{8,12},{10,14},{12,8},{14,10},{16,20},{18,... | collective-permute-start | bytes 3538952 | tf_op jit(solution)/shard_map/ppermute | solution.py:604
  243.2 32.1 %collective-permute-start.30 = (bf16[4,48,768]{2,1,0:T(8,128)(2,1)S(1)}, bf16[4,48,768]{2,1,0:T(8,128)(2,1)S(1)}, u32[]{:S(2)}, u32[]{:S(2)}) collective-permute-start(bf16[4,48,768]{2,1,0:T(8,128)(2,1)S(1)} %merge.51.refs_3_.refs_1_), channel_id=1, source_target_pairs={{0,4},{2,6},{4,0},{6,2},{8,12},{10,14},{12,8},{14,10},{16,20},{18,... | collective-permute-start | bytes 884744 | tf_op jit(solution)/shard_map/ppermute | solution.py:604
  244.7 27.7 %collective-permute-start.32 = (bf16[4,96,768]{2,1,0:T(8,128)(2,1)S(1)}, bf16[4,96,768]{2,1,0:T(8,128)(2,1)S(1)}, u32[]{:S(2)}, u32[]{:S(2)}) collective-permute-start(bf16[4,96,768]{2,1,0:T(8,128)(2,1)S(1)} %merge.52.refs_3_.refs_1_), channel_id=1, source_target_pairs={{0,2},{2,0},{4,6},{6,4},{8,10},{10,8},{12,14},{14,12},{16,18},{18,... | collective-permute-start | bytes 1769480 | tf_op jit(solution)/shard_map/ppermute | solution.py:604
  248.6 32.8 %collective-permute-start.37 = (bf16[208,768]{1,0:T(8,128)(2,1)S(1)}, bf16[208,768]{1,0:T(8,128)(2,1)S(1)}, u32[]{:S(2)}, u32[]{:S(2)}) collective-permute-start(bf16[208,768]{1,0:T(8,128)(2,1)S(1)} %merge.54.refs_3_.refs_1_), channel_id=1, source_target_pairs={{0,4},{2,6},{4,0},{6,2},{8,12},{10,14},{12,8},{14,10},{16,20},{18,... | collective-permute-start | bytes 958472 | tf_op jit(solution)/shard_map/ppermute | solution.py:604
  272.3 4.6 %collective-permute-start.38 = (bf16[16,96,768]{2,1,0:T(8,128)(2,1)S(1)}, bf16[16,96,768]{2,1,0:T(8,128)(2,1)S(1)}, u32[]{:S(2)}, u32[]{:S(2)}) collective-permute-start(bf16[16,96,768]{2,1,0:T(8,128)(2,1)S(1)} %merge.55.refs_3_.refs_1_), channel_id=1, source_target_pairs={{0,1},{1,0},{2,3},{3,2},{4,5},{5,4},{6,7},{7,6},{8,9},{9,8},{10,11... | collective-permute-start | bytes 7077896 | tf_op jit(solution)/shard_map/ppermute | solution.py:604
  273.0 31.0 %collective-permute-start.42 = (bf16[8,96,768]{2,1,0:T(8,128)(2,1)S(1)}, bf16[8,96,768]{2,1,0:T(8,128)(2,1)S(1)}, u32[]{:S(2)}, u32[]{:S(2)}) collective-permute-start(bf16[8,96,768]{2,1,0:T(8,128)(2,1)S(1)} %merge.56.refs_3_.refs_1_), channel_id=1, source_target_pairs={{0,4},{2,6},{4,0},{6,2},{8,12},{10,14},{12,8},{14,10},{16,20},{18,... | collective-permute-start | bytes 3538952 | tf_op jit(solution)/shard_map/ppermute | solution.py:604
  275.9 15.0 %collective-permute-start.36 = (bf16[8,48,768]{2,1,0:T(8,128)(2,1)S(1)}, bf16[8,48,768]{2,1,0:T(8,128)(2,1)S(1)}, u32[]{:S(2)}, u32[]{:S(2)}) collective-permute-start(bf16[8,48,768]{2,1,0:T(8,128)(2,1)S(1)} %merge.57.refs_3_.refs_1_), channel_id=1, source_target_pairs={{0,2},{2,0},{4,6},{6,4},{8,10},{10,8},{12,14},{14,12},{16,18},{18,... | collective-permute-start | bytes 1769480 | tf_op jit(solution)/shard_map/ppermute | solution.py:604
  285.6 17.2 %collective-permute-start.40 = (bf16[400,768]{1,0:T(8,128)(2,1)S(1)}, bf16[400,768]{1,0:T(8,128)(2,1)S(1)}, u32[]{:S(2)}, u32[]{:S(2)}) collective-permute-start(bf16[400,768]{1,0:T(8,128)(2,1)S(1)} %merge.58.refs_3_.refs_1_), channel_id=1, source_target_pairs={{0,2},{2,0},{4,6},{6,4},{8,10},{10,8},{12,14},{14,12},{16,18},{18,... | collective-permute-start | bytes 1843208 | tf_op jit(solution)/shard_map/ppermute | solution.py:604
  291.5 13.3 %collective-permute-start.39 = (bf16[16,48,768]{2,1,0:T(8,128)(2,1)S(1)}, bf16[16,48,768]{2,1,0:T(8,128)(2,1)S(1)}, u32[]{:S(2)}, u32[]{:S(2)}) collective-permute-start(bf16[16,48,768]{2,1,0:T(8,128)(2,1)S(1)} %merge.59.refs_3_.refs_1_), channel_id=1, source_target_pairs={{0,1},{1,0},{2,3},{3,2},{4,5},{5,4},{6,7},{7,6},{8,9},{9,8},{10,11... | collective-permute-start | bytes 3538952 | tf_op jit(solution)/shard_map/ppermute | solution.py:604
  303.5 2.9 collective-permute-start.41
  304.7 7.3 %collective-permute-start.43 = (bf16[16,96,768]{2,1,0:T(8,128)(2,1)S(1)}, bf16[16,96,768]{2,1,0:T(8,128)(2,1)}, u32[]{:S(2)}, u32[]{:S(2)}) collective-permute-start(bf16[16,96,768]{2,1,0:T(8,128)(2,1)S(1)} %merge.61.refs_1_), channel_id=1, source_target_pairs={{0,1},{1,0},{2,3},{3,2},{4,5},{5,4},{6,7},{7,6},{8,9},{9,8},{10,11... | collective-permute-start | bytes 7077896 | tf_op jit(solution)/shard_map/ppermute | solution.py:604
  (14 other events, 35.3 us)

commit v3 on v2

--- a/solution.py
+++ b/solution.py
@@ -170,7 +170,7 @@
         ctx_ref[0, :, cols] = (ctx * scale).astype(BF16)
         return 0
 
-    lax.fori_loop(0, PAIRS, pair, 0)
+    lax.fori_loop(0, PAIRS, pair, 0, unroll=2)
     hidden = x + dot(ctx_ref[0], wo_ref[...]) + row_of(vec_ref, B_OUT)
     hid_ref[0] = hidden
     scaled, _ = norm_parts(hidden)
@@ -207,7 +207,7 @@
         + [pltpu.HBM((STRIPS, SLOTS, D), F32), pltpu.VMEM((STRIPS, SLOTS, D), BF16)]
         + [pltpu.HBM((STRIPS, SLOTS, D), BF16), pltpu.VMEM((STRIPS, SLOTS, D), BF16)],
         micros=28,
-        mib=30,
+        mib=44,
         name="attend",
     )
 
@@ -547,7 +547,7 @@
     block = pl.BlockSpec(
         (WIDE, FCALL // 16, D), lambda i, at_ref: (crossed(i, p.cross) ^ (at_ref[which] // WIDE), 0, 0)
     )
-    given = list(given)
+    given = [far(v) for v in given]
     return call(
         functools.partial(widen_mlp_kernel, which), [at, p.total, p.got] + given,
         [block, block] + [pl.BlockSpec(memory_space=pl.ANY)] * len(given), after,
@@ -557,7 +557,7 @@
             pl.BlockSpec((WIDE * FCALL // 16, D), lambda i, *_: (16 // WIDE * part + i, 0)),
             pl.BlockSpec((WIDE * D // 16, FCALL), lambda i, *_: (i, part)),
         ],
-        out_shape=[jax.ShapeDtypeStruct((FF, D), F32), jax.ShapeDtypeStruct((D, FF), F32)],
+        out_shape=[pltpu.HBM((FF, D), F32), pltpu.HBM((D, FF), F32)],
         input_output_aliases={3: 0, 4: 1} if given else {},
         micros=4,
         mib=12,
@@ -605,8 +605,8 @@
 
 
 TAIL = (
-    "b", "end", "1", "0", "a", "b", "place", "b", "a", "1", "0", "b", "a", "0", "1", "a",
-    "b", "a", "1", "b", "b", "0", "1", "a", "wide", "b", "a", "b", "1",
+    "b", "a", "b", "0", "1", "a", "b", "0", "a", "1", "end", "b", "1", "a",
+    "b", "place", "0", "b", "a", "1", "wide", "b", "out", "a", "b", "1",
 )
 
 
@@ -614,7 +614,7 @@
     def __init__(self, order, back, dp, keep=None, send=None, pick=None):
         self.keep, self.send, self.pick, self.small = keep, send, pick, None
         rest = [1 << i for i in range(4, dp.bit_length() - 1)]
-        hops = [("seq", 1, 2, "half")] + [("dp", b, dp, "half") for b in order]
+        hops = [("seq", 1, 2, "half"), ("dp", order[:2], dp, "quad")] + [("dp", b, dp, "half") for b in order[2:]]
         hops += [("dp", b, dp, "whole") for b in rest]
         hops += [("dp", b, dp, "join") for b in back] + [("seq", 1, 2, "pair")]
         self.hops, self.total, self.got = hops, None, None
@@ -623,14 +623,22 @@
 
     def start(self):
         axis, bit, size, kind = self.hops[0]
+        if kind == "quad":
+            masks = (bit[1], bit[0], bit[0] | bit[1])
+            self.got = [swap(part, axis, mask, size) for part, mask in zip(self.send, masks)]
+            return
         self.got = swap(self.send if kind == "half" else self.total, axis, bit, size)
+
+
+TAKES = {"load": 3, "quad": 4}
+GIVES = {"pick": 2, "split": 2, "quad": 2, "split4": 4}
 
 
 def merge_kernel(kinds, *refs):
     at_ref, refs = refs[0], refs[1:]
-    outs = refs[sum(3 if kind == "load" else 2 for kind in kinds) :]
+    outs = refs[sum(TAKES.get(kind, 2) for kind in kinds) :]
     for kind in kinds:
-        (a, b), refs = refs[:2], refs[2:]
+        (a, b, *more), refs = refs[: TAKES.get(kind, 2)], refs[TAKES.get(kind, 2) :]
         if kind == "pick":
             keep, send = outs[:2]
 
@@ -651,8 +659,17 @@
         elif kind == "load":
             rows = a.shape[1]
             outs[0][:rows] = a[0] + b[0]
-            outs[0][rows:] = refs[0][...]
-            refs = refs[1:]
+            outs[0][rows:] = more[0][...]
+        elif kind == "split4":
+            part = a.shape[0] // 4
+            for i in range(4):
+                outs[i][...] = a[i * part : (i + 1) * part] + b[i * part : (i + 1) * part]
+        elif kind == "quad":
+            half = a.shape[0] // 2
+            for i in range(2):
+                rows = slice(i * half, (i + 1) * half)
+                total = a[rows].astype(F32) + b[rows].astype(F32)
+                outs[i][...] = (total + (more[0][rows].astype(F32) + more[1][rows].astype(F32))).astype(BF16)
         elif kind == "join":
             half = a.shape[0]
             outs[0][:half] = a[...]
@@ -661,7 +678,7 @@
             rows = a.shape[0] - SMALL
             outs[0][:rows], outs[0][rows : 2 * rows] = a[:rows], b[:rows]
             outs[0][2 * rows :] = a[rows:] + b[rows:]
-        outs = outs[2 if kind in ("pick", "split") else 1 :]
+        outs = outs[GIVES.get(kind, 1) :]
 
 
 def merge(at, pieces, after):
@@ -671,9 +688,9 @@
             kind, args = "pick", list(p.pick)
         else:
             kind = p.hops.pop(0)[3]
-            args = [p.keep if kind == "half" else p.total, p.got]
+            args = [p.keep, *p.got] if kind == "quad" else [p.keep if kind == "half" else p.total, p.got]
             if kind == "half":
-                kind = "split" if p.hops[0][3] == "half" else "add"
+                kind = {"half": "split", "quad": "split4"}.get(p.hops[0][3], "add")
             elif kind == "whole":
                 kind = "add"
             if p.small is not None and kind == "add" and p.hops[0][3] == "join":
@@ -682,28 +699,30 @@
                 kind = "carry"
         n, tail = args[0].shape[0], args[0].shape[1:]
         n = {"pick": [n, n], "split": [n // 2, n // 2], "add": [n], "join": [2 * n], "carry": [2 * n - SMALL],
-             "load": [1]}[kind]
+             "load": [1], "split4": [n // 4] * 4, "quad": [n // 2] * 2}[kind]
         kinds.append(kind)
         operands += args
         shapes.append([(tail[0] + SMALL, D)] if kind == "load" else [(m,) + tail for m in n])
     flat = [shape for group in shapes for shape in group]
-    size = sum(2 * v.size for v in operands) + sum(2 * D * (s[0] * s[1] // D if len(s) == 2 else s[0] * s[1]) for s in flat)
     outs = list(call(
-        functools.partial(merge_kernel, kinds), [at] + operands, [whole(v.shape) for v in operands], after,
+        functools.partial(merge_kernel, kinds),
+        [at] + [pltpu.with_memory_space_constraint(v, pltpu.VMEM) for v in operands],
+        [pl.BlockSpec(memory_space=pltpu.VMEM)] * len(operands), after,
         prefetch=1,
         grid=(1,),
-        out_specs=[whole(shape) for shape in flat],
-        out_shape=[jax.ShapeDtypeStruct(shape, BF16) for shape in flat],
+        out_specs=[pl.BlockSpec(memory_space=pltpu.VMEM)] * len(flat),
+        out_shape=[pltpu.VMEM(shape, BF16) for shape in flat],
         micros=2,
-        mib=4 + (size >> 20),
+        mib=6,
         name="merge",
     ))
     made = list(outs)
     for p, kind in zip(pieces, kinds):
         p.pick = None
-        if kind in ("pick", "split"):
-            p.keep, p.send = outs[:2]
-            outs = outs[2:]
+        if kind == "split4":
+            p.keep, p.send, outs = outs[0], outs[1:4], outs[4:]
+        elif kind in ("pick", "split", "quad"):
+            p.keep, p.send, outs = outs[0], outs[1], outs[2:]
         else:
             p.total, outs = outs[0], outs[1:]
         p.start()
@@ -745,10 +764,9 @@
     grads_0, d_0, sums_0 = attend_back(0, 1, *back, made)
     a0 = Sum(x_first, X_LAST, dp, pick=(g_out, grads_0))
     made = merge(at, [m0, a0], [grads_0])
-    output = back_in_place(at, out_own, out_other, made)
     grads_1, d_1, sums_1 = attend_back(1, 1, *back, made)
     made = merge(at, [m0, m1, a0], [grads_1])
-    grads_2, d_2, sums_2 = attend_back(2, 1, *back, made + [output])
+    grads_2, d_2, sums_2 = attend_back(2, 1, *back, made)
     a1 = Sum(x_first, X_LAST, dp, pick=(grads_1, grads_2))
     made = merge(at, [m0, m1, a0, a1], [grads_2])
     pieces = {"0": m0, "1": m1, "a": a0, "b": a1}
@@ -763,10 +781,13 @@
             made = [a1.small]
         elif turn == "place":
             grad_patches = back_in_place(at, gp_own, gp_other, made)
-            made = [grad_patches]
+            made = [far(grad_patches)]
+        elif turn == "out":
+            output = back_in_place(at, out_own, out_other, made)
+            made = [far(output)]
         elif turn == "wide":
             given = widen_mlp(0, at, m0, (), made)
-            made = [given[0]]
+            made = [far(given[0])]
         else:
             made = merge(at, [pieces[c] for c in turn], made)
     for p in pieces.values():

time: 323 us -> 295 us (0.913)
  the two profiles are of different devices: /device:TPU:0 before, /device:TPU:23 now
where the time goes in v3:
time: 295 us; the launch traced here: 289 us
  Pallas kernels  195 us (66%)
  starting transfers between devices  49.6 us (17%)
  waiting for transfers between devices  39.7 us (13%)
    pallas_call x41, Pallas kernels, call(): pl.pallas_call(body, grid_spec=spec, compiler_params=params(mib), cost_es...  195 us
    ppermute x48, starting transfers between devices, swap(): return lax.ppermute(value, axis, [(i, i ^ bit) for i in range(size)])  49.6 us
    ppermute x48, waiting for transfers between devices, swap(): return lax.ppermute(value, axis, [(i, i ^ bit) for i in range(size)])  39.7 us
  transfers between devices with their start and end apart: 48, of which 14 were waited for; matrix products, arithmetic and copies ran while one was open for 1% of the time, Pallas kernels for 43%

profile of v3, /device:TPU:23, one launch (start us, length us, event | category | flops | bytes accessed | tf_op | source)
XLA Modules:
  0.0 289.4 jit_solution(9475440840890850578)
XLA Ops:
  0.8 1.3 constant_dynamic-slice_fusion.1
  3.5 1.3 collective-permute-done.refs_3_
  6.0 30.8 %attend.1 = (bf16[2,544,768]{2,1,0:T(8,128)(2,1)}, bf16[2,544,1536]{2,1,0:T(8,128)(2,1)}, bf16[2,544,768]{2,1,0:T(8,128)(2,1)}, bf16[2,544,768]{2,1,0:T(8,128)(2...) custom-call(s32[3]{0:T(128)S(1)} %pad_add_fusion.refs_0_, ...), custom_call_target="tpu_custom_call" | custom-call | flops 321999994880 | tf_op jit(solution)/shard_map/attend/pallas_call | solution.py:58
  36.9 24.8 %mlp.3 = (bf16[16,96,768]{2,1,0:T(8,128)(2,1)S(1)}, bf16[16,96,768]{2,1,0:T(8,128)(2,1)S(1)}, f32[1088,768]{1,0:T(8,128)S(1)}, f32[2,1,768]{2,1,0:T(1,128)S(1)}, f32[1088,768]{1,0:T(8,128)S(1)}) custom-call(s32[3]{0:T(128)S(1)} %pad_add_fusion.refs_0_, bf16[1088,768]{1,0:T(8,128)(2,1)S(1)} %bitcast.11, bf16[1088,768]{1,0:T(8,128)(2,1)S(1)} %bitcast.8, ...), custom_call_target="tpu_custom_call" | custom-call | flops 276000014336 | tf_op jit(solution)/shard_map/mlp/pallas_call | solution.py:58
  62.1 12.9 %mlp.4 = (bf16[16,96,768]{2,1,0:T(8,128)(2,1)S(1)}, bf16[16,96,768]{2,1,0:T(8,128)(2,1)S(1)}, f32[1088,768]{1,0:T(8,128)S(1)}, f32[1,1,768]{2,1,0:T(1,128)S(1)}, f32[1088,768]{1,0:T(8,128)S(1)}) custom-call(s32[3]{0:T(128)S(1)} %pad_add_fusion.refs_0_, bf16[1088,768]{1,0:T(8,128)(2,1)S(1)} %bitcast.12, ...), custom_call_target="tpu_custom_call", output_to_operand_aliasing={{4}: (6, {}), {2}: (7, {})} | custom-call | flops 138000007168 | tf_op jit(solution)/shard_map/mlp/pallas_call | solution.py:58
  75.0 2.0 merge.27
  77.5 2.2 collective-permute-start.6
  79.7 13.7 %mlp.5 = (bf16[16,96,768]{2,1,0:T(8,128)(2,1)S(1)}, bf16[16,96,768]{2,1,0:T(8,128)(2,1)S(1)}, f32[1088,768]{1,0:T(8,128)S(1)}, f32[1,1,768]{2,1,0:T(1,128)S(1)},...) custom-call(s32[3]{0:T(128)S(1)} %pad_add_fusion.refs_0_, ...), custom_call_target="tpu_custom_call", output_to_operand_aliasing={{4}: (6, {}), {2}: (7, {}), {0}: (8, {}), {1}: (9, {})} | custom-call | flops 138000007168 | tf_op jit(solution)/shard_map/mlp/pallas_call | solution.py:58
  94.4 10.3 %middle.1 = (bf16[2,544,768]{2,1,0:T(8,128)(2,1)}, bf16[2,544,768]{2,1,0:T(8,128)(2,1)}, bf16[16,48,768]{2,1,0:T(8,128)(2,1)S(1)}, f32[8,768]{1,0:T(8,128)S(1)}) custom-call(s32[3]{0:T(128)S(1)} %pad_add_fusion.refs_0_, f32[2,544,768]{2,1,0:T(8,128)S(1)} %bitcast.7, f32[2,544,768]{2,1,0:T(8,128)} %get-tuple-element.107.refs_2_, ...), custom_call_target="tpu_custom_call" | custom-call | flops 115000000512 | tf_op jit(solution)/shard_map/middle/pallas_call | solution.py:58
  105.6 3.4 %merge.28 = (bf16[2,96,768]{2,1,0:T(8,128)(2,1)S(1)}, bf16[2,96,768]{2,1,0:T(8,128)(2,1)S(1)}, bf16[4,96,768]{2,1,0:T(8,128)(2,1)S(1)}, bf16[4,96,768]{2,1,0:T(8...) custom-call(s32[3]{0:T(128)S(1)} %pad_add_fusion.refs_0_, ...), custom_call_target="tpu_custom_call" | custom-call | flops 23000000512 | tf_op jit(solution)/shard_map/merge/pallas_call | solution.py:58
  109.0 1.3 collective-permute-start.8
  110.8 2.2 collective-permute-start.12
  113.0 14.0 %attend_back.3 = (bf16[16,48,768]{2,1,0:T(8,128)(2,1)S(1)}, bf16[2,544,768]{2,1,0:T(8,128)(2,1)}, f32[1,768]{1,0:T(1,128)S(1)}) custom-call(s32[3]{0:T(128)S(1)} %pad_add_fusion.refs_0_, s32[4]{0:T(128)S(1)} %copy-done, bf16[2,544,1536]{2,1,0:T(8,128)(2,1)} %get-tuple-element.129.refs_2_, bf16[2,544,768]{2,1,0:T(8,128)(2,1)} %get-tuple-element.130.refs_3_, ...), custom_call_target="tpu_custom_call" | custom-call | flops 138000007168 | tf_op jit(solution)/shard_map/attend_back/pallas_call | solution.py:58
  127.9 2.5 collective-permute-start.13
  130.4 14.0 %attend_back.4 = (bf16[16,48,768]{2,1,0:T(8,128)(2,1)S(1)}, bf16[2,544,768]{2,1,0:T(8,128)(2,1)}, f32[1,768]{1,0:T(1,128)S(1)}) custom-call(s32[3]{0:T(128)S(1)} %pad_add_fusion.refs_0_, s32[4]{0:T(128)S(1)} %copy-done, bf16[2,544,1536]{2,1,0:T(8,128)(2,1)} %get-tuple-element.129.refs_2_, bf16[2,544,768]{2,1,0:T(8,128)(2,1)} %get-tuple-element.130.refs_3_, ...), custom_call_target="tpu_custom_call" | custom-call | flops 138000007168 | tf_op jit(solution)/shard_map/attend_back/pallas_call | solution.py:58
  144.5 2.5 merge.30
  147.6 2.2 collective-permute-start.18
  149.9 2.3 collective-permute-start.14
  152.2 14.0 %attend_back.5 = (bf16[16,48,768]{2,1,0:T(8,128)(2,1)S(1)}, bf16[2,544,768]{2,1,0:T(8,128)(2,1)}, f32[1,768]{1,0:T(1,128)S(1)}) custom-call(s32[3]{0:T(128)S(1)} %pad_add_fusion.refs_0_, s32[4]{0:T(128)S(1)} %copy-done, bf16[2,544,1536]{2,1,0:T(8,128)(2,1)} %get-tuple-element.129.refs_2_, bf16[2,544,768]{2,1,0:T(8,128)(2,1)} %get-tuple-element.130.refs_3_, ...), custom_call_target="tpu_custom_call" | custom-call | flops 138000007168 | tf_op jit(solution)/shard_map/attend_back/pallas_call | solution.py:58
  167.4 1.8 collective-permute-start.19
  169.3 1.3 collective-permute-start.23
  170.8 1.8 collective-permute-done.19.refs_2_
  174.3 1.7 collective-permute-start.22
  176.6 5.0 %collective-permute-done.20.refs_2_ = bf16[4,48,768]{2,1,0:T(8,128)(2,1)S(1)} collective-permute-done((bf16[4,48,768]{2,1,0:T(8,128)(2,1)S(1)}, bf16[4,48,768]{2,1,0:T(8,128)(2,1)S(1)}, u32[]{:S(2)}, u32[]{:S(2)}) %collective-permute-start.20) | collective-permute-done | bytes 294944 | tf_op jit(solution)/shard_map/ppermute | solution.py:604
  181.6 2.3 collective-permute-start.25
  183.9 4.8 %collective-permute-done.22.refs_4_ = bf16[4,48,768]{2,1,0:T(8,128)(2,1)S(1)} collective-permute-done((bf16[4,48,768]{2,1,0:T(8,128)(2,1)S(1)}, bf16[4,48,768]{2,1,0:T(8,128)(2,1)S(1)}, u32[]{:S(2)}, u32[]{:S(2)}) %collective-permute-start.22) | collective-permute-done | bytes 294944 | tf_op jit(solution)/shard_map/ppermute | solution.py:604
  189.4 1.4 collective-permute-start.24
  193.1 2.2 collective-permute-start.30
  197.8 2.8 collective-permute-start.28
  200.6 3.9 %collective-permute-done.31.refs_2_ = bf16[4,96,768]{2,1,0:T(8,128)(2,1)S(1)} collective-permute-done((bf16[4,96,768]{2,1,0:T(8,128)(2,1)S(1)}, bf16[4,96,768]{2,1,0:T(8,128)(2,1)S(1)}, u32[]{:S(2)}, u32[]{:S(2)}) %collective-permute-start.31) | collective-permute-done | bytes 589856 | tf_op jit(solution)/shard_map/ppermute | solution.py:604
  204.5 1.6 merge.39.refs_3_.refs_1_
  207.5 1.8 collective-permute-start.33
  210.0 10.4 %end.1 = (bf16[2,272,768]{2,1,0:T(8,128)(2,1)S(1)}, bf16[2,272,768]{2,1,0:T(8,128)(2,1)S(1)}, bf16[16,768]{1,0:T(8,128)(2,1)S(1)}) custom-call(s32[3]{0:T(128)S(1)} %pad_add_fusion.refs_0_, bf16[2,544,768]{2,1,0:T(8,128)(2,1)} %get-tuple-element.169.refs_1_, bf16[2,544,768]{2,1,0:T(8,128)(2,1)} %get-tuple-element.170.refs_2_, ...), custom_call_target="tpu_custom_call" | custom-call | flops 103499997184 | tf_op jit(solution)/shard_map/end/pallas_call | solution.py:58
  220.4 1.4 merge.42.refs_3_.refs_1_
  221.9 3.5 %collective-permute-start.37 = (bf16[2,272,768]{2,1,0:T(8,128)(2,1)S(1)}, bf16[2,272,768]{2,1,0:T(8,128)(2,1)S(1)}, u32[]{:S(2)}, u32[]{:S(2)}) collective-permute-start(bf16[2,272,768]{2,1,0:T(8,128)(2,1)S(1)} %get-tuple-element.183), channel_id=1, source_target_pairs={{0,1},{1,0},{2,3},{3,2},{4,5},{5,4},{6,7},{7,6},{8,9},{9,8},{10,11... | collective-permute-start | bytes 2506760 | tf_op jit(solution)/shard_map/ppermute | solution.py:604
  226.3 1.5 merge.44.refs_3_.refs_1_
  227.9 1.3 collective-permute-start.41
  230.0 2.3 in_place.2.refs_3_
  232.3 2.3 merge.46.refs_3_.refs_1_
  234.6 5.7 %collective-permute-start.39 = (bf16[16,96,768]{2,1,0:T(8,128)(2,1)S(1)}, bf16[16,96,768]{2,1,0:T(8,128)(2,1)S(1)}, u32[]{:S(2)}, u32[]{:S(2)}) collective-permute-start(bf16[16,96,768]{2,1,0:T(8,128)(2,1)S(1)} %merge.46.refs_3_.refs_1_), channel_id=1, source_target_pairs={{0,1},{1,0},{2,3},{3,2},{4,5},{5,4},{6,7},{7,6},{8,9},{9,8},{10,11... | collective-permute-start | bytes 7077896 | tf_op jit(solution)/shard_map/ppermute | solution.py:604
  242.3 1.5 collective-permute-start.46
  244.5 4.5 %widen_mlp.2 = (f32[3072,768]{1,0:T(8,128)}, f32[768,3072]{1,0:T(8,128)}) custom-call(s32[3]{0:T(128)S(1)} %pad_add_fusion.refs_0_, bf16[16,96,768]{2,1,0:T(8,128)(2,1)S(1)} %merge.46.refs_3_.refs_1_, bf16[16,96,768]{2,1,0:T(8,128)(2,1)S(1)} %collective-permute-done.39.refs_2_, bf16[8,96,768]{2,1,0:T(8,128)(2,1)S(1)} %merge.49.refs_3_.refs_1_), custom_call_target="tpu_custom_call" | custom-call | flops 46000001024 | tf_op jit(solution)/shard_map/widen_mlp/pallas_call | solution.py:58
  250.8 4.2 %in_place.3.refs_3_ = bf16[4,272,768]{2,1,0:T(8,128)(2,1)} custom-call(s32[3]{0:T(128)S(1)} %pad_add_fusion.refs_0_, bf16[2,272,768]{2,1,0:T(8,128)(2,1)S(1)} %get-tuple-element.120.refs_1_, bf16[2,272,768]{2,1,0:T(8,128)(2,1)} %collective-permute-done.3.refs_2_, bf16[400,768]{1,0:T(8,128)(2,1)S(1)} %merge.50.refs_3_.refs_1_), custom_call_target="tpu_custom_call" | custom-call | flops 23000000512 | tf_op jit(solution)/shard_map/in_place/pallas_call | solution.py:58
  255.0 1.6 collective-permute-done.42.refs_2_
  258.5 11.3 %collective-permute-done.44.refs_2_ = bf16[400,768]{1,0:T(8,128)(2,1)S(1)} collective-permute-done((bf16[400,768]{1,0:T(8,128)(2,1)S(1)}, bf16[400,768]{1,0:T(8,128)(2,1)S(1)}, u32[]{:S(2)}, u32[]{:S(2)}) %collective-permute-start.44) | collective-permute-done | bytes 614432 | tf_op jit(solution)/shard_map/ppermute | solution.py:604
  271.3 4.1 %collective-permute-done.46.refs_2_ = bf16[8,96,768]{2,1,0:T(8,128)(2,1)S(1)} collective-permute-done((bf16[8,96,768]{2,1,0:T(8,128)(2,1)S(1)}, bf16[8,96,768]{2,1,0:T(8,128)(2,1)S(1)}, u32[]{:S(2)}, u32[]{:S(2)}) %collective-permute-start.46) | collective-permute-done | bytes 1179680 | tf_op jit(solution)/shard_map/ppermute | solution.py:604
  277.0 4.3 %widen_attn.1 = (f32[768,768]{1,0:T(8,128)}, f32[768,768]{1,0:T(8,128)}, f32[768,768]{1,0:T(8,128)}, f32[768,768]{1,0:T(8,128)}, f32[16,768]{1,0:T(8,128)S(1)}) custom-call(s32[3]{0:T(128)S(1)} %pad_add_fusion.refs_0_, bf16[16,48,768]{2,1,0:T(8,128)(2,1)S(1)} %merge.51.refs_3_.refs_1_, bf16[16,48,768]{2,1,0:T(8,128)(2,1)S(1)} %collective-permute-done.43.refs_2_, ...), custom_call_target="tpu_custom_call" | custom-call | flops 46000001024 | tf_op jit(solution)/shard_map/widen_attn/pallas_call | solution.py:58
  282.6 6.3 %widen_mlp.3 = (f32[3072,768]{1,0:T(8,128)}, f32[768,3072]{1,0:T(8,128)}) custom-call(s32[3]{0:T(128)S(1)} %pad_add_fusion.refs_0_, bf16[16,96,768]{2,1,0:T(8,128)(2,1)S(1)} %merge.53.refs_1_, bf16[16,96,768]{2,1,0:T(8,128)(2,1)} %collective-permute-done.47.refs_2_, ...), custom_call_target="tpu_custom_call", output_to_operand_aliasing={{0}: (3, {}), {1}: (4, {})} | custom-call | flops 46000001024 | tf_op jit(solution)/shard_map/widen_mlp/pallas_call | solution.py:58
  (132 shorter events, 30.9 us)
Async XLA Ops:
  2.1 2.7 collective-permute-start
  2.9 3.1 %collective-permute-start.1 = (bf16[2,272,768]{2,1,0:T(8,128)(2,1)S(1)}, bf16[2,272,768]{2,1,0:T(8,128)(2,1)S(1)}, u32[]{:S(2)}, u32[]{:S(2)}) collective-permute-start(bf16[2,272,768]{2,1,0:T(8,128)(2,1)S(1)} %constant_dynamic-slice_fusion), channel_id=1, source_target_pairs={{0,1},{1,0},{2,3},{3,2},{4,5},{5,4},{6,7},{7,6},{8,9},{9,8},{10,11... | collective-permute-start | bytes 2506760 | tf_op jit(solution)/shard_map/ppermute | solution.py:604
  61.7 13.4 %collective-permute-start.2 = (bf16[16,96,768]{2,1,0:T(8,128)(2,1)S(1)}, bf16[16,96,768]{2,1,0:T(8,128)(2,1)S(1)}, u32[]{:S(2)}, u32[]{:S(2)}) collective-permute-start(bf16[16,96,768]{2,1,0:T(8,128)(2,1)S(1)} %get-tuple-element.115), channel_id=1, source_target_pairs={{0,1},{1,0},{2,3},{3,2},{4,5},{5,4},{6,7},{7,6},{8,9},{9,8},{10,11... | collective-permute-start | bytes 7077896 | tf_op jit(solution)/shard_map/ppermute | solution.py:604
  77.0 27.7 %collective-permute-start.4 = (bf16[4,96,768]{2,1,0:T(8,128)(2,1)}, bf16[4,96,768]{2,1,0:T(8,128)(2,1)}, u32[]{:S(2)}, u32[]{:S(2)}) collective-permute-start(bf16[4,96,768]{2,1,0:T(8,128)(2,1)} %get-tuple-element.117.refs_11_), channel_id=1, source_target_pairs={{0,4},{2,6},{4,0},{6,2},{8,12},{10,14},{12,8},{14,10},{16,20},{18,... | collective-permute-start | bytes 1769480 | tf_op jit(solution)/shard_map/ppermute | solution.py:604
  77.3 27.5 %collective-permute-start.5 = (bf16[4,96,768]{2,1,0:T(8,128)(2,1)}, bf16[4,96,768]{2,1,0:T(8,128)(2,1)}, u32[]{:S(2)}, u32[]{:S(2)}) collective-permute-start(bf16[4,96,768]{2,1,0:T(8,128)(2,1)} %get-tuple-element.118.refs_12_), channel_id=1, source_target_pairs={{0,2},{2,0},{4,6},{6,4},{8,10},{10,8},{12,14},{14,12},{16,18},{18,... | collective-permute-start | bytes 1769480 | tf_op jit(solution)/shard_map/ppermute | solution.py:604
  77.5 28.1 %collective-permute-start.6 = (bf16[4,96,768]{2,1,0:T(8,128)(2,1)}, bf16[4,96,768]{2,1,0:T(8,128)(2,1)}, u32[]{:S(2)}, u32[]{:S(2)}) collective-permute-start(bf16[4,96,768]{2,1,0:T(8,128)(2,1)} %get-tuple-element.119.refs_13_), channel_id=1, source_target_pairs={{0,6},{2,4},{4,2},{6,0},{8,14},{10,12},{12,10},{14,8},{16,22},{18,... | collective-permute-start | bytes 1769480 | tf_op jit(solution)/shard_map/ppermute | solution.py:604
  93.4 12.2 %collective-permute-start.7 = (bf16[16,96,768]{2,1,0:T(8,128)(2,1)S(1)}, bf16[16,96,768]{2,1,0:T(8,128)(2,1)S(1)}, u32[]{:S(2)}, u32[]{:S(2)}) collective-permute-start(bf16[16,96,768]{2,1,0:T(8,128)(2,1)S(1)} %get-tuple-element.123.refs_7_), channel_id=1, source_target_pairs={{0,1},{1,0},{2,3},{3,2},{4,5},{5,4},{6,7},{7,6},{8,9},{9,8},{10,11... | collective-permute-start | bytes 7077896 | tf_op jit(solution)/shard_map/ppermute | solution.py:604
  109.0 18.0 %collective-permute-start.8 = (bf16[2,96,768]{2,1,0:T(8,128)(2,1)S(1)}, bf16[2,96,768]{2,1,0:T(8,128)(2,1)S(1)}, u32[]{:S(2)}, u32[]{:S(2)}) collective-permute-start(bf16[2,96,768]{2,1,0:T(8,128)(2,1)S(1)} %get-tuple-element.128.refs_9_), channel_id=1, source_target_pairs={{0,8},{2,10},{4,12},{6,14},{8,0},{10,2},{12,4},{14,6},{16,24},{18,... | collective-permute-start | bytes 884744 | tf_op jit(solution)/shard_map/ppermute | solution.py:604
  110.3 34.1 %collective-permute-start.10 = (bf16[4,96,768]{2,1,0:T(8,128)(2,1)}, bf16[4,96,768]{2,1,0:T(8,128)(2,1)}, u32[]{:S(2)}, u32[]{:S(2)}) collective-permute-start(bf16[4,96,768]{2,1,0:T(8,128)(2,1)} %get-tuple-element.135.refs_11_), channel_id=1, source_target_pairs={{0,4},{2,6},{4,0},{6,2},{8,12},{10,14},{12,8},{14,10},{16,20},{18,... | collective-permute-start | bytes 1769480 | tf_op jit(solution)/shard_map/ppermute | solution.py:604
  110.5 33.9 %collective-permute-start.11 = (bf16[4,96,768]{2,1,0:T(8,128)(2,1)}, bf16[4,96,768]{2,1,0:T(8,128)(2,1)}, u32[]{:S(2)}, u32[]{:S(2)}) collective-permute-start(bf16[4,96,768]{2,1,0:T(8,128)(2,1)} %get-tuple-element.136.refs_12_), channel_id=1, source_target_pairs={{0,2},{2,0},{4,6},{6,4},{8,10},{10,8},{12,14},{14,12},{16,18},{18,... | collective-permute-start | bytes 1769480 | tf_op jit(solution)/shard_map/ppermute | solution.py:604
  110.8 33.7 %collective-permute-start.12 = (bf16[4,96,768]{2,1,0:T(8,128)(2,1)}, bf16[4,96,768]{2,1,0:T(8,128)(2,1)}, u32[]{:S(2)}, u32[]{:S(2)}) collective-permute-start(bf16[4,96,768]{2,1,0:T(8,128)(2,1)} %get-tuple-element.137.refs_13_), channel_id=1, source_target_pairs={{0,6},{2,4},{4,2},{6,0},{8,14},{10,12},{12,10},{14,8},{16,22},{18,... | collective-permute-start | bytes 1769480 | tf_op jit(solution)/shard_map/ppermute | solution.py:604
  127.9 16.6 %collective-permute-start.13 = (bf16[16,48,768]{2,1,0:T(8,128)(2,1)S(1)}, bf16[16,48,768]{2,1,0:T(8,128)(2,1)S(1)}, u32[]{:S(2)}, u32[]{:S(2)}) collective-permute-start(bf16[16,48,768]{2,1,0:T(8,128)(2,1)S(1)} %get-tuple-element.142.refs_11_), channel_id=1, source_target_pairs={{0,1},{1,0},{2,3},{3,2},{4,5},{5,4},{6,7},{7,6},{8,9},{9,8},{10,11... | collective-permute-start | bytes 3538952 | tf_op jit(solution)/shard_map/ppermute | solution.py:604
  130.4 14.1 %collective-permute-start.9 = (bf16[1,96,768]{2,1,0:T(8,128)(2,1)S(1)}, bf16[1,96,768]{2,1,0:T(8,128)(2,1)S(1)}, u32[]{:S(2)}, u32[]{:S(2)}) collective-permute-start(bf16[1,96,768]{2,1,0:T(8,128)(2,1)S(1)} %get-tuple-element.140.refs_9_), channel_id=1, source_target_pairs={{0,16},{2,18},{4,20},{6,22},{8,24},{10,26},{12,28},{14,30},{16,0},... | collective-permute-start | bytes 442376 | tf_op jit(solution)/shard_map/ppermute | solution.py:604
  147.0 19.2 %collective-permute-start.15 = (bf16[2,96,768]{2,1,0:T(8,128)(2,1)S(1)}, bf16[2,96,768]{2,1,0:T(8,128)(2,1)S(1)}, u32[]{:S(2)}, u32[]{:S(2)}) collective-permute-start(bf16[2,96,768]{2,1,0:T(8,128)(2,1)S(1)} %get-tuple-element.146.refs_10_), channel_id=1, source_target_pairs={{0,8},{2,10},{4,12},{6,14},{8,0},{10,2},{12,4},{14,6},{16,24},{18,... | collective-permute-start | bytes 884744 | tf_op jit(solution)/shard_map/ppermute | solution.py:604
  147.2 19.0 %collective-permute-start.16 = (bf16[4,48,768]{2,1,0:T(8,128)(2,1)S(1)}, bf16[4,48,768]{2,1,0:T(8,128)(2,1)S(1)}, u32[]{:S(2)}, u32[]{:S(2)}) collective-permute-start(bf16[4,48,768]{2,1,0:T(8,128)(2,1)S(1)} %get-tuple-element.148.refs_12_), channel_id=1, source_target_pairs={{0,4},{2,6},{4,0},{6,2},{8,12},{10,14},{12,8},{14,10},{16,20},{18,... | collective-permute-start | bytes 884744 | tf_op jit(solution)/shard_map/ppermute | solution.py:604
  147.4 18.8 %collective-permute-start.17 = (bf16[4,48,768]{2,1,0:T(8,128)(2,1)S(1)}, bf16[4,48,768]{2,1,0:T(8,128)(2,1)S(1)}, u32[]{:S(2)}, u32[]{:S(2)}) collective-permute-start(bf16[4,48,768]{2,1,0:T(8,128)(2,1)S(1)} %get-tuple-element.149.refs_13_), channel_id=1, source_target_pairs={{0,2},{2,0},{4,6},{6,4},{8,10},{10,8},{12,14},{14,12},{16,18},{18,... | collective-permute-start | bytes 884744 | tf_op jit(solution)/shard_map/ppermute | solution.py:604
  147.6 18.6 %collective-permute-start.18 = (bf16[4,48,768]{2,1,0:T(8,128)(2,1)S(1)}, bf16[4,48,768]{2,1,0:T(8,128)(2,1)S(1)}, u32[]{:S(2)}, u32[]{:S(2)}) collective-permute-start(bf16[4,48,768]{2,1,0:T(8,128)(2,1)S(1)} %get-tuple-element.150.refs_14_), channel_id=1, source_target_pairs={{0,6},{2,4},{4,2},{6,0},{8,14},{10,12},{12,10},{14,8},{16,22},{18,... | collective-permute-start | bytes 884744 | tf_op jit(solution)/shard_map/ppermute | solution.py:604
  149.9 16.3 %collective-permute-start.14 = (bf16[1,96,768]{2,1,0:T(8,128)(2,1)S(1)}, bf16[1,96,768]{2,1,0:T(8,128)(2,1)S(1)}, u32[]{:S(2)}, u32[]{:S(2)}) collective-permute-start(bf16[1,96,768]{2,1,0:T(8,128)(2,1)S(1)} %get-tuple-element.144.refs_8_.refs_1_), channel_id=1, source_target_pairs={{0,16},{2,18},{4,20},{6,22},{8,24},{10,26},{12,28},{14,30},{16,0},... | collective-permute-start | bytes 442376 | tf_op jit(solution)/shard_map/ppermute | solution.py:604
  167.4 5.2 %collective-permute-start.19 = (bf16[16,48,768]{2,1,0:T(8,128)(2,1)S(1)}, bf16[16,48,768]{2,1,0:T(8,128)(2,1)S(1)}, u32[]{:S(2)}, u32[]{:S(2)}) collective-permute-start(bf16[16,48,768]{2,1,0:T(8,128)(2,1)S(1)} %get-tuple-element.153.refs_9_), channel_id=1, source_target_pairs={{0,1},{1,0},{2,3},{3,2},{4,5},{5,4},{6,7},{7,6},{8,9},{9,8},{10,11... | collective-permute-start | bytes 3538952 | tf_op jit(solution)/shard_map/ppermute | solution.py:604
  169.2 81.6 %collective-permute-start.3 = (bf16[2,272,768]{2,1,0:T(8,128)(2,1)}, bf16[2,272,768]{2,1,0:T(8,128)(2,1)}, u32[]{:S(2)}, u32[]{:S(2)}) collective-permute-start(bf16[2,272,768]{2,1,0:T(8,128)(2,1)} %get-tuple-element.121), channel_id=1, source_target_pairs={{0,1},{1,0},{2,3},{3,2},{4,5},{5,4},{6,7},{7,6},{8,9},{9,8},{10,11... | collective-permute-start | bytes 2506760 | tf_op jit(solution)/shard_map/ppermute | solution.py:604
  169.3 5.0 %collective-permute-start.23 = (bf16[2,48,768]{2,1,0:T(8,128)(2,1)S(1)}, bf16[2,48,768]{2,1,0:T(8,128)(2,1)S(1)}, u32[]{:S(2)}, u32[]{:S(2)}) collective-permute-start(bf16[2,48,768]{2,1,0:T(8,128)(2,1)S(1)} %get-tuple-element.158.refs_7_), channel_id=1, source_target_pairs={{0,8},{2,10},{4,12},{6,14},{8,0},{10,2},{12,4},{14,6},{16,24},{18,... | collective-permute-start | bytes 442376 | tf_op jit(solution)/shard_map/ppermute | solution.py:604
  170.6 20.2 %collective-permute-start.27 = (bf16[2,96,768]{2,1,0:T(8,128)(2,1)S(1)}, bf16[2,96,768]{2,1,0:T(8,128)(2,1)S(1)}, u32[]{:S(2)}, u32[]{:S(2)}) collective-permute-start(bf16[2,96,768]{2,1,0:T(8,128)(2,1)S(1)} %get-tuple-element.154.refs_3_.refs_1_), channel_id=1, source_target_pairs={{0,8},{2,10},{4,12},{6,14},{8,0},{10,2},{12,4},{14,6},{16,24},{18,... | collective-permute-start | bytes 884744 | tf_op jit(solution)/shard_map/ppermute | solution.py:604
  173.3 8.3 %collective-permute-start.20 = (bf16[4,48,768]{2,1,0:T(8,128)(2,1)S(1)}, bf16[4,48,768]{2,1,0:T(8,128)(2,1)S(1)}, u32[]{:S(2)}, u32[]{:S(2)}) collective-permute-start(bf16[4,48,768]{2,1,0:T(8,128)(2,1)S(1)} %get-tuple-element.160.refs_4_), channel_id=1, source_target_pairs={{0,4},{2,6},{4,0},{6,2},{8,12},{10,14},{12,8},{14,10},{16,20},{18,... | collective-permute-start | bytes 884744 | tf_op jit(solution)/shard_map/ppermute | solution.py:604
  173.6 8.0 %collective-permute-start.21 = (bf16[4,48,768]{2,1,0:T(8,128)(2,1)S(1)}, bf16[4,48,768]{2,1,0:T(8,128)(2,1)S(1)}, u32[]{:S(2)}, u32[]{:S(2)}) collective-permute-start(bf16[4,48,768]{2,1,0:T(8,128)(2,1)S(1)} %get-tuple-element.161.refs_5_), channel_id=1, source_target_pairs={{0,2},{2,0},{4,6},{6,4},{8,10},{10,8},{12,14},{14,12},{16,18},{18,... | collective-permute-start | bytes 884744 | tf_op jit(solution)/shard_map/ppermute | solution.py:604
  174.3 14.4 %collective-permute-start.22 = (bf16[4,48,768]{2,1,0:T(8,128)(2,1)S(1)}, bf16[4,48,768]{2,1,0:T(8,128)(2,1)S(1)}, u32[]{:S(2)}, u32[]{:S(2)}) collective-permute-start(bf16[4,48,768]{2,1,0:T(8,128)(2,1)S(1)} %get-tuple-element.162.refs_6_), channel_id=1, source_target_pairs={{0,6},{2,4},{4,2},{6,0},{8,14},{10,12},{12,10},{14,8},{16,22},{18,... | collective-permute-start | bytes 884744 | tf_op jit(solution)/shard_map/ppermute | solution.py:604
  181.6 10.1 %collective-permute-start.26 = (bf16[1,96,768]{2,1,0:T(8,128)(2,1)S(1)}, bf16[1,96,768]{2,1,0:T(8,128)(2,1)S(1)}, u32[]{:S(2)}, u32[]{:S(2)}) collective-permute-start(bf16[1,96,768]{2,1,0:T(8,128)(2,1)S(1)} %get-tuple-element.156.refs_5_), channel_id=1, source_target_pairs={{0,16},{2,18},{4,20},{6,22},{8,24},{10,26},{12,28},{14,30},{16,0},... | collective-permute-start | bytes 442376 | tf_op jit(solution)/shard_map/ppermute | solution.py:604
  181.6 10.9 %collective-permute-start.25 = (bf16[1,48,768]{2,1,0:T(8,128)(2,1)S(1)}, bf16[1,48,768]{2,1,0:T(8,128)(2,1)S(1)}, u32[]{:S(2)}, u32[]{:S(2)}) collective-permute-start(bf16[1,48,768]{2,1,0:T(8,128)(2,1)S(1)} %get-tuple-element.164.refs_6_), channel_id=1, source_target_pairs={{0,16},{2,18},{4,20},{6,22},{8,24},{10,26},{12,28},{14,30},{16,0},... | collective-permute-start | bytes 221192 | tf_op jit(solution)/shard_map/ppermute | solution.py:604
  189.4 7.1 %collective-permute-start.24 = (bf16[2,48,768]{2,1,0:T(8,128)(2,1)S(1)}, bf16[2,48,768]{2,1,0:T(8,128)(2,1)S(1)}, u32[]{:S(2)}, u32[]{:S(2)}) collective-permute-start(bf16[2,48,768]{2,1,0:T(8,128)(2,1)S(1)} %get-tuple-element.166.refs_4_), channel_id=1, source_target_pairs={{0,8},{2,10},{4,12},{6,14},{8,0},{10,2},{12,4},{14,6},{16,24},{18,... | collective-permute-start | bytes 442376 | tf_op jit(solution)/shard_map/ppermute | solution.py:604
  191.4 13.1 %collective-permute-start.31 = (bf16[4,96,768]{2,1,0:T(8,128)(2,1)S(1)}, bf16[4,96,768]{2,1,0:T(8,128)(2,1)S(1)}, u32[]{:S(2)}, u32[]{:S(2)}) collective-permute-start(bf16[4,96,768]{2,1,0:T(8,128)(2,1)S(1)} %merge.35.refs_3_.refs_1_), channel_id=1, source_target_pairs={{0,2},{2,0},{4,6},{6,4},{8,10},{10,8},{12,14},{14,12},{16,18},{18,... | collective-permute-start | bytes 1769480 | tf_op jit(solution)/shard_map/ppermute | solution.py:604
  192.3 17.0 %collective-permute-start.29 = (bf16[1,96,768]{2,1,0:T(8,128)(2,1)S(1)}, bf16[1,96,768]{2,1,0:T(8,128)(2,1)S(1)}, u32[]{:S(2)}, u32[]{:S(2)}) collective-permute-start(bf16[1,96,768]{2,1,0:T(8,128)(2,1)S(1)} %merge.36.refs_3_.refs_1_), channel_id=1, source_target_pairs={{0,16},{2,18},{4,20},{6,22},{8,24},{10,26},{12,28},{14,30},{16,0},... | collective-permute-start | bytes 442376 | tf_op jit(solution)/shard_map/ppermute | solution.py:604
  193.1 13.2 %collective-permute-start.30 = (bf16[1,48,768]{2,1,0:T(8,128)(2,1)S(1)}, bf16[1,48,768]{2,1,0:T(8,128)(2,1)S(1)}, u32[]{:S(2)}, u32[]{:S(2)}) collective-permute-start(bf16[1,48,768]{2,1,0:T(8,128)(2,1)S(1)} %merge.37.refs_3_.refs_1_), channel_id=1, source_target_pairs={{0,16},{2,18},{4,20},{6,22},{8,24},{10,26},{12,28},{14,30},{16,0},... | collective-permute-start | bytes 221192 | tf_op jit(solution)/shard_map/ppermute | solution.py:604
  197.8 22.6 %collective-permute-start.28 = (bf16[1,48,768]{2,1,0:T(8,128)(2,1)}, bf16[1,48,768]{2,1,0:T(8,128)(2,1)}, u32[]{:S(2)}, u32[]{:S(2)}) collective-permute-start(bf16[1,48,768]{2,1,0:T(8,128)(2,1)} %get-tuple-element.168.refs_4_), channel_id=1, source_target_pairs={{0,16},{2,18},{4,20},{6,22},{8,24},{10,26},{12,28},{14,30},{16,0},... | collective-permute-start | bytes 221192 | tf_op jit(solution)/shard_map/ppermute | solution.py:604
  206.1 26.2 %collective-permute-start.36 = (bf16[8,96,768]{2,1,0:T(8,128)(2,1)}, bf16[8,96,768]{2,1,0:T(8,128)(2,1)}, u32[]{:S(2)}, u32[]{:S(2)}) collective-permute-start(bf16[8,96,768]{2,1,0:T(8,128)(2,1)} %merge.39.refs_3_.refs_1_), channel_id=1, source_target_pairs={{0,4},{2,6},{4,0},{6,2},{8,12},{10,14},{12,8},{14,10},{16,20},{18,... | collective-permute-start | bytes 3538952 | tf_op jit(solution)/shard_map/ppermute | solution.py:604
  207.5 18.5 %collective-permute-start.33 = (bf16[2,48,768]{2,1,0:T(8,128)(2,1)}, bf16[2,48,768]{2,1,0:T(8,128)(2,1)}, u32[]{:S(2)}, u32[]{:S(2)}) collective-permute-start(bf16[2,48,768]{2,1,0:T(8,128)(2,1)} %merge.40.refs_3_.refs_1_), channel_id=1, source_target_pairs={{0,8},{2,10},{4,12},{6,14},{8,0},{10,2},{12,4},{14,6},{16,24},{18,... | collective-permute-start | bytes 442376 | tf_op jit(solution)/shard_map/ppermute | solution.py:604
  209.9 12.0 %collective-permute-start.34 = (bf16[2,96,768]{2,1,0:T(8,128)(2,1)S(1)}, bf16[2,96,768]{2,1,0:T(8,128)(2,1)S(1)}, u32[]{:S(2)}, u32[]{:S(2)}) collective-permute-start(bf16[2,96,768]{2,1,0:T(8,128)(2,1)S(1)} %merge.41.refs_17_.refs_1_), channel_id=1, source_target_pairs={{0,8},{2,10},{4,12},{6,14},{8,0},{10,2},{12,4},{14,6},{16,24},{18,... | collective-permute-start | bytes 884744 | tf_op jit(solution)/shard_map/ppermute | solution.py:604
  221.8 6.1 %collective-permute-start.32 = (bf16[64,768]{1,0:T(8,128)(2,1)S(1)}, bf16[64,768]{1,0:T(8,128)(2,1)S(1)}, u32[]{:S(2)}, u32[]{:S(2)}) collective-permute-start(bf16[64,768]{1,0:T(8,128)(2,1)S(1)} %merge.42.refs_3_.refs_1_), channel_id=1, source_target_pairs={{0,16},{2,18},{4,20},{6,22},{8,24},{10,26},{12,28},{14,30},{16,0},... | collective-permute-start | bytes 294920 | tf_op jit(solution)/shard_map/ppermute | solution.py:604
  221.9 7.9 %collective-permute-start.37 = (bf16[2,272,768]{2,1,0:T(8,128)(2,1)S(1)}, bf16[2,272,768]{2,1,0:T(8,128)(2,1)S(1)}, u32[]{:S(2)}, u32[]{:S(2)}) collective-permute-start(bf16[2,272,768]{2,1,0:T(8,128)(2,1)S(1)} %get-tuple-element.183), channel_id=1, source_target_pairs={{0,1},{1,0},{2,3},{3,2},{4,5},{5,4},{6,7},{7,6},{8,9},{9,8},{10,11... | collective-permute-start | bytes 2506760 | tf_op jit(solution)/shard_map/ppermute | solution.py:604
  226.1 15.6 %collective-permute-start.40 = (bf16[4,96,768]{2,1,0:T(8,128)(2,1)S(1)}, bf16[4,96,768]{2,1,0:T(8,128)(2,1)S(1)}, u32[]{:S(2)}, u32[]{:S(2)}) collective-permute-start(bf16[4,96,768]{2,1,0:T(8,128)(2,1)S(1)} %merge.43.refs_3_.refs_1_), channel_id=1, source_target_pairs={{0,2},{2,0},{4,6},{6,4},{8,10},{10,8},{12,14},{14,12},{16,18},{18,... | collective-permute-start | bytes 1769480 | tf_op jit(solution)/shard_map/ppermute | solution.py:604
  227.9 13.1 %collective-permute-start.41 = (bf16[4,48,768]{2,1,0:T(8,128)(2,1)S(1)}, bf16[4,48,768]{2,1,0:T(8,128)(2,1)S(1)}, u32[]{:S(2)}, u32[]{:S(2)}) collective-permute-start(bf16[4,48,768]{2,1,0:T(8,128)(2,1)S(1)} %merge.44.refs_3_.refs_1_), channel_id=1, source_target_pairs={{0,4},{2,6},{4,0},{6,2},{8,12},{10,14},{12,8},{14,10},{16,20},{18,... | collective-permute-start | bytes 884744 | tf_op jit(solution)/shard_map/ppermute | solution.py:604
  229.8 10.6 %collective-permute-start.35 = (bf16[112,768]{1,0:T(8,128)(2,1)S(1)}, bf16[112,768]{1,0:T(8,128)(2,1)S(1)}, u32[]{:S(2)}, u32[]{:S(2)}) collective-permute-start(bf16[112,768]{1,0:T(8,128)(2,1)S(1)} %merge.45.refs_3_.refs_1_), channel_id=1, source_target_pairs={{0,8},{2,10},{4,12},{6,14},{8,0},{10,2},{12,4},{14,6},{16,24},{18,... | collective-permute-start | bytes 516104 | tf_op jit(solution)/shard_map/ppermute | solution.py:604
  234.6 9.9 %collective-permute-start.39 = (bf16[16,96,768]{2,1,0:T(8,128)(2,1)S(1)}, bf16[16,96,768]{2,1,0:T(8,128)(2,1)S(1)}, u32[]{:S(2)}, u32[]{:S(2)}) collective-permute-start(bf16[16,96,768]{2,1,0:T(8,128)(2,1)S(1)} %merge.46.refs_3_.refs_1_), channel_id=1, source_target_pairs={{0,1},{1,0},{2,3},{3,2},{4,5},{5,4},{6,7},{7,6},{8,9},{9,8},{10,11... | collective-permute-start | bytes 7077896 | tf_op jit(solution)/shard_map/ppermute | solution.py:604
  240.9 9.2 %collective-permute-start.38 = (bf16[208,768]{1,0:T(8,128)(2,1)S(1)}, bf16[208,768]{1,0:T(8,128)(2,1)S(1)}, u32[]{:S(2)}, u32[]{:S(2)}) collective-permute-start(bf16[208,768]{1,0:T(8,128)(2,1)S(1)} %merge.47.refs_3_.refs_1_), channel_id=1, source_target_pairs={{0,4},{2,6},{4,0},{6,2},{8,12},{10,14},{12,8},{14,10},{16,20},{18,... | collective-permute-start | bytes 958472 | tf_op jit(solution)/shard_map/ppermute | solution.py:604
  241.6 15.0 %collective-permute-start.42 = (bf16[8,48,768]{2,1,0:T(8,128)(2,1)S(1)}, bf16[8,48,768]{2,1,0:T(8,128)(2,1)S(1)}, u32[]{:S(2)}, u32[]{:S(2)}) collective-permute-start(bf16[8,48,768]{2,1,0:T(8,128)(2,1)S(1)} %merge.48.refs_3_.refs_1_), channel_id=1, source_target_pairs={{0,2},{2,0},{4,6},{6,4},{8,10},{10,8},{12,14},{14,12},{16,18},{18,... | collective-permute-start | bytes 1769480 | tf_op jit(solution)/shard_map/ppermute | solution.py:604
  242.3 33.1 %collective-permute-start.46 = (bf16[8,96,768]{2,1,0:T(8,128)(2,1)S(1)}, bf16[8,96,768]{2,1,0:T(8,128)(2,1)S(1)}, u32[]{:S(2)}, u32[]{:S(2)}) collective-permute-start(bf16[8,96,768]{2,1,0:T(8,128)(2,1)S(1)} %merge.49.refs_3_.refs_1_), channel_id=1, source_target_pairs={{0,4},{2,6},{4,0},{6,2},{8,12},{10,14},{12,8},{14,10},{16,20},{18,... | collective-permute-start | bytes 3538952 | tf_op jit(solution)/shard_map/ppermute | solution.py:604
  250.7 19.0 %collective-permute-start.44 = (bf16[400,768]{1,0:T(8,128)(2,1)S(1)}, bf16[400,768]{1,0:T(8,128)(2,1)S(1)}, u32[]{:S(2)}, u32[]{:S(2)}) collective-permute-start(bf16[400,768]{1,0:T(8,128)(2,1)S(1)} %merge.50.refs_3_.refs_1_), channel_id=1, source_target_pairs={{0,2},{2,0},{4,6},{6,4},{8,10},{10,8},{12,14},{14,12},{16,18},{18,... | collective-permute-start | bytes 1843208 | tf_op jit(solution)/shard_map/ppermute | solution.py:604
  257.2 19.8 %collective-permute-start.43 = (bf16[16,48,768]{2,1,0:T(8,128)(2,1)S(1)}, bf16[16,48,768]{2,1,0:T(8,128)(2,1)S(1)}, u32[]{:S(2)}, u32[]{:S(2)}) collective-permute-start(bf16[16,48,768]{2,1,0:T(8,128)(2,1)S(1)} %merge.51.refs_3_.refs_1_), channel_id=1, source_target_pairs={{0,1},{1,0},{2,3},{3,2},{4,5},{5,4},{6,7},{7,6},{8,9},{9,8},{10,11... | collective-permute-start | bytes 3538952 | tf_op jit(solution)/shard_map/ppermute | solution.py:604
  270.4 6.6 %collective-permute-start.45 = (bf16[784,768]{1,0:T(8,128)(2,1)S(1)}, bf16[784,768]{1,0:T(8,128)(2,1)S(1)}, u32[]{:S(2)}, u32[]{:S(2)}) collective-permute-start(bf16[784,768]{1,0:T(8,128)(2,1)S(1)} %merge.52.refs_3_), channel_id=1, source_target_pairs={{0,1},{1,0},{2,3},{3,2},{4,5},{5,4},{6,7},{7,6},{8,9},{9,8},{10,11... | collective-permute-start | bytes 3612680 | tf_op jit(solution)/shard_map/ppermute | solution.py:604
  276.1 6.5 %collective-permute-start.47 = (bf16[16,96,768]{2,1,0:T(8,128)(2,1)S(1)}, bf16[16,96,768]{2,1,0:T(8,128)(2,1)}, u32[]{:S(2)}, u32[]{:S(2)}) collective-permute-start(bf16[16,96,768]{2,1,0:T(8,128)(2,1)S(1)} %merge.53.refs_1_), channel_id=1, source_target_pairs={{0,1},{1,0},{2,3},{3,2},{4,5},{5,4},{6,7},{7,6},{8,9},{9,8},{10,11... | collective-permute-start | bytes 7077896 | tf_op jit(solution)/shard_map/ppermute | solution.py:604
  (13 other events, 49.1 us)
